TPU v7x, 32 devices: a whole 2x2x4 slice. The times are simulated.
32 devices in a mesh: seq: 8 (over z, y), chan: 4 (over x, core).
Axes of the slice: x: 2, y: 2, z: 4, core: 2. Of those that a mesh axis runs over, the one named last changes fastest.
Arguments:
- signal: bfloat16 [2048, 2048], P('seq', 'chan'), may hold values from -6 to 6
- gate_rows: bfloat16 [2048, 2048], P('seq', 'chan'), may hold values from -60 to 60
- skip_gain: float32 [2048], P('chan'), may hold values from 0.5 to 1.5
- filter_taps: bfloat16 [2048, 16], P(None, 'chan'), may hold values from -2 to 2
- queries: bfloat16 [2048, 2048], P('seq', 'chan'), may hold values from -6 to 6
- key_rows: bfloat16 [2048, 2048], P('seq', 'chan'), may hold values from -6 to 6
Outputs:
- conv_mixed: bfloat16 [2048, 2048], P('seq', 'chan')
- attended: bfloat16 [32, 1024, 128], P(('chan', 'seq'))
All inputs are finite; a program needn't handle non-finite values.
Results may differ from a plain program's by a relative error of at most 0.0061.
Values may be sent and summed in bfloat16 or wider, within the bound.
No kernel may reach another device: no remote copies, remote signals or barrier semaphores. Data moves between devices by JAX's collectives and lax.ppermute only.
A program may use at most 128 MiB of HBM per device.

v0:
```python
import math

import jax
import jax.numpy as jnp
from jax import lax
from jax.sharding import PartitionSpec as P


def toeplitz_block(padded_taps, out_start, in_start, block_rows, group_rows, seq_len):
    heads_loc = padded_taps.shape[0]
    window_len = group_rows + block_rows - 1
    offset = out_start - in_start - block_rows + 1 + seq_len
    window = lax.dynamic_slice_in_dim(padded_taps, offset, window_len, 1)
    flipped = jnp.concatenate(
        [window[:, ::-1], jnp.zeros((heads_loc, 1), padded_taps.dtype)], axis=1
    )
    repeated = jnp.tile(flipped, (1, group_rows))[:, : group_rows * window_len]
    return repeated.reshape(heads_loc, group_rows, window_len)[:, :, group_rows - 1 :]


def add_range(total_acc, inputs, first_row, target, lower, upper, padded_taps, seq_len, head_dim):
    block_rows = inputs.shape[0]
    group_rows = total_acc.shape[0]
    positions = first_row + jnp.arange(block_rows, dtype=jnp.int32)
    keep_rows = (positions >= lower) & (positions < upper)
    is_live = (first_row < upper) & (first_row + block_rows > lower)

    def compute(running):
        masked = jnp.where(keep_rows[:, None], inputs, jnp.zeros_like(inputs))
        matrix = toeplitz_block(padded_taps, target, first_row, block_rows, group_rows, seq_len)
        heads_loc = matrix.shape[0]
        split_in = masked.reshape(block_rows, heads_loc, head_dim)
        product = jnp.einsum("htn,nhd->thd", matrix, split_in, preferred_element_type=jnp.float32)
        return running + product.reshape(group_rows, heads_loc * head_dim)

    def unchanged(running):
        return running

    return lax.cond(is_live, compute, unchanged, total_acc)


def attend_block(q_rows, q_pos, key_end, keys_all, values_all, score_scale):
    key_part = keys_all[:key_end]
    value_part = values_all[:key_end]
    raw_scores = (
        jnp.einsum("qd,kd->qk", q_rows, key_part, preferred_element_type=jnp.float32) * score_scale
    )
    k_pos = jnp.arange(key_end, dtype=jnp.int32)
    masked = jnp.where(k_pos[None, :] <= q_pos[:, None], raw_scores, -jnp.inf)
    peak = jnp.max(masked, axis=1)
    exp_scores = jnp.exp(masked - peak[:, None])
    row_total = jnp.sum(exp_scores, axis=1)
    weighted = jnp.dot(
        exp_scores.astype(jnp.bfloat16), value_part, preferred_element_type=jnp.float32
    )
    return (weighted / row_total[:, None]).astype(jnp.bfloat16)


def shards(signal, gate_rows, skip_gain, filter_taps, queries, key_rows):
    group_rows, local_width = signal.shape
    heads_loc = filter_taps.shape[1]
    head_dim = local_width // heads_loc
    seq_count = lax.axis_size("seq")
    chan_count = lax.axis_size("chan")
    my_group = lax.axis_index("seq")
    seq_len = group_rows * seq_count
    padded_taps = jnp.concatenate(
        [jnp.zeros((seq_len, heads_loc), filter_taps.dtype), filter_taps], axis=0
    ).T
    own_start = my_group * group_rows
    own_upper = own_start + group_rows
    halfway = seq_count // 2
    own_lower = jnp.zeros((), jnp.int32)
    help_upper = jnp.zeros((), jnp.int32)
    help_start = (my_group + halfway) % seq_count * group_rows

    def add_both(totals, inputs, first_row):
        own_acc = add_range(
            totals[0],
            inputs,
            first_row,
            own_start,
            own_lower,
            own_upper,
            padded_taps,
            seq_len,
            head_dim,
        )
        help_acc = add_range(
            totals[1], inputs, first_row, help_start, 0, help_upper, padded_taps, seq_len, head_dim
        )
        return (own_acc, help_acc)

    zero_acc = jnp.zeros((group_rows, local_width), jnp.float32)
    totals = (zero_acc, zero_acc)
    incoming = lax.all_gather(signal, "seq", axis=0, tiled=True)
    incoming_rows = incoming.shape[0]
    pieces_count = incoming_rows // group_rows
    blocks = incoming.reshape(pieces_count, group_rows, local_width)
    starts = group_rows * jnp.arange(pieces_count, dtype=jnp.int32)

    def step_block(running, entry_pair):
        return (add_both(running, entry_pair[0], entry_pair[1]), None)

    totals, unused = lax.scan(step_block, totals, (blocks, starts))
    own_acc, help_acc = totals
    conv_mixed = (
        gate_rows.astype(jnp.float32) * (own_acc + skip_gain[None, :] * signal.astype(jnp.float32))
    ).astype(jnp.bfloat16)
    widened = conv_mixed.astype(jnp.float32)
    squares = jnp.sum(jnp.square(widened), axis=1)
    whole_sum = lax.psum(squares, "chan")
    inv_scale = lax.rsqrt(whole_sum / (local_width * chan_count) + 1e-06)
    values = (widened * inv_scale[:, None]).astype(jnp.bfloat16)
    query_sets = seq_count // heads_loc
    query_rows = group_rows // query_sets
    query_send = (
        queries.reshape(query_sets, query_rows, heads_loc, head_dim)
        .transpose(2, 0, 1, 3)
        .reshape(seq_count, query_rows, head_dim)
    )
    pair_stack = jnp.concatenate(
        [
            key_rows.reshape(group_rows, heads_loc, head_dim),
            values.reshape(group_rows, heads_loc, head_dim),
        ],
        axis=2,
    ).transpose(1, 0, 2)
    pair_send = jnp.broadcast_to(
        pair_stack[:, None], (heads_loc, query_sets, group_rows, 2 * head_dim)
    ).reshape(seq_count, group_rows, 2 * head_dim)
    query_got, pair_got = (
        lax.all_to_all(query_send, "seq", split_axis=0, concat_axis=1, tiled=True),
        lax.all_to_all(pair_send, "seq", split_axis=0, concat_axis=1, tiled=True),
    )
    query_all = query_got[0]
    keys_all = pair_got[0, :, :head_dim]
    values_all = pair_got[0, :, head_dim:]
    my_set = my_group % query_sets
    query_len = query_all.shape[0]
    query_block = min(512, query_len)
    score_scale = 1.0 / math.sqrt(head_dim)
    outputs = []
    for query_step in range(query_len // query_block):
        local_index = query_step * query_block + jnp.arange(query_block, dtype=jnp.int32)
        q_pos = (
            local_index // query_rows * group_rows + my_set * query_rows + local_index % query_rows
        )
        last_source = ((query_step + 1) * query_block - 1) // query_rows
        key_end = (last_source + 1) * group_rows
        q_rows = query_all[query_step * query_block : (query_step + 1) * query_block]
        outputs.append(attend_block(q_rows, q_pos, key_end, keys_all, values_all, score_scale))
    attended = jnp.concatenate(outputs, axis=0)[None]
    return (conv_mixed, attended)


def solution(mesh):
    in_specs = (
        P("seq", "chan"),
        P("seq", "chan"),
        P("chan"),
        P(None, "chan"),
        P("seq", "chan"),
        P("seq", "chan"),
    )
    out_specs = (P("seq", "chan"), P(("chan", "seq"), None, None))
    return jax.shard_map(shards, mesh=mesh, in_specs=in_specs, out_specs=out_specs, check_vma=False)
```

profile of v0, /device:TPU:0, one launch (start us, length us, event | category | flops | bytes accessed | tf_op | source)
XLA Modules:
  0.0 182.6 jit_solution(9240131706119696246)
XLA Ops:
  7.2 0.0 all-gather.2.cloned.1.call-start
  7.2 0.7 all-gather.2.cloned.1.call-update
  7.9 1.0 reshape.122
  8.9 0.7 copy.16
  9.7 7.3 %all-to-all-start.1 = ((bf16[8,128,128]{2,1,0:T(8,128)(2,1)}), bf16[8,128,128]{2,1,0:T(8,128)(2,1)S(1)}, u32[]{:S(2)}, u32[]{:S(2)}) async-start(bf16[8,128,128]{2,1,0:T(8,128)(2,1)} %bitcast.11), calls=%async_computation.1 | async-start | bytes 524288 | tf_op jit(solution)/shard_map/all_to_all | solution.py:133
  17.0 1.7 reshape.119
  18.7 45.1 %all-gather.2.cloned.1.call-done = bf16[2048,512]{1,0:T(8,128)(2,1)} async-done(((bf16[256,512]{1,0:T(8,128)(2,1)}), bf16[2048,512]{1,0:T(8,128)(2,1)}) %all-gather.2.cloned.1.call-update) | async-done | bytes 2097168 | tf_op jit(solution)/shard_map/all_gather | solution.py:96
  63.8 3.9 %copy.13 = bf16[8,256,512]{1,2,0:T(8,128)(2,1)} copy(bf16[8,256,512]{2,1,0:T(8,128)(2,1)} %bitcast.53) | data formatting | bytes 4194304 | tf_op jit(solution)/shard_map/while | solution.py:105
  67.8 0.0 copy-start
  67.8 0.0 copy-start.4
  67.8 21.8 %while.13 = (s32[]{:T(128)}, f32[256,512]{0,1:T(8,128)S(1)}, s32[8]{0:T(128)S(1)}, s32[]{:T(128)}, bf16[8,256,512]{1,2,0:T(8,128)(2,1)}, /*index=5*/s32[]{:T(128...) while((s32[]{:T(128)}, f32[256,512]{0,1:T(8,128)S(1)}, s32[8]{0:T(128)S(1)}, s32[]{:T(128)}, ...), condition=%wide.region_3.4_spmd, body=%wide.region_0.3_spmd.sunk | while | flops 67372048 | bytes 10779659 | solution.py:105
  67.8 0.6 dynamic_slice.18
  69.7 6.3 %conditional.2 = (f32[256,512]{0,1:T(8,128)S(1)}) conditional(s32[]{:T(128)} %convert_element_type.63, f32[256,512]{0,1:T(8,128)S(1)} %get-tuple-element.193, (s32[]{:T(128)}, s32[256]{0:T(256)S(1)}, s32[]{:T(128)}, bf16[8,256,512]{1,2,0:T(8,128)(2,1)}, s32[]{:T(128)}, /*index=5*/s32[]{:T(128)}, bf16[4,4096]{1,0:T(4,128)(2,1)S(1)}, ...), branch_computations={%region_1.1_spmd, %region_2.2_spmd} | conditional | flops 67372040 | bytes 10778412 | solution.py:39
  70.3 0.6 compare_and_fusion
  71.0 0.1 constant_dynamic-slice_fusion
  71.1 0.4 reverse
  71.4 0.1 slice.69
  71.5 1.0 constant_dynamic-slice_fusion.1
  72.5 0.1 broadcast_bitcast_fusion
  72.6 0.8 copy.17
  73.4 0.4 slice.51
  73.8 1.8 reshape.110
  75.5 0.4 fusion
  75.9 0.1 bitcast_add_fusion
  76.0 0.6 dynamic_slice.18
  78.0 0.6 dynamic_slice.18
  79.9 0.6 dynamic_slice.18
  81.9 0.6 dynamic_slice.18
  83.8 0.6 dynamic_slice.18
  85.7 0.6 dynamic_slice.18
  87.7 0.6 dynamic_slice.18
  89.6 0.2 copy.14
  89.8 1.2 fusion.22
  91.0 5.7 %psum.7 = f32[256]{0:T(256)S(1)} all-reduce(f32[256]{0:T(256)S(1)} %get-tuple-element.129), channel_id=1, replica_groups=mesh['seq'=8,'chan'=4] {'chan'}, use_global_device_ids=true, to_apply=%region_5.6 | all-reduce | flops 256 | bytes 2048 | tf_op jit(solution)/shard_map/psum | solution.py:112
  96.7 0.1 fusion.23
  96.8 0.1 reshape.120
  96.9 0.3 maximum_bitcast_fusion
  97.2 0.1 copy.15
  97.3 1.0 broadcast_in_dim.23
  98.3 48.1 %all-to-all-start = ((bf16[8,256,256]{2,1,0:T(8,128)(2,1)}), bf16[8,256,256]{2,1,0:T(8,128)(2,1)S(1)}, u32[]{:S(2)}, u32[]{:S(2)}) async-start(bf16[8,256,256]{2,1,0:T(8,128)(2,1)} %bitcast.7), calls=%async_computation | async-start | bytes 2097152 | tf_op jit(solution)/shard_map/all_to_all | solution.py:134
  146.4 25.1 %all-to-all-done = bf16[8,256,256]{2,1,0:T(8,128)(2,1)S(1)} async-done(((bf16[8,256,256]{2,1,0:T(8,128)(2,1)}), bf16[8,256,256]{2,1,0:T(8,128)(2,1)S(1)}, u32[]{:S(2)}, u32[]{:S(2)}) %all-to-all-start) | async-done | bytes 1048608 | tf_op jit(solution)/shard_map/all_to_all | solution.py:134
  171.6 0.5 fusion.41
  172.0 0.4 fusion.11
  172.4 0.5 fusion.16
  172.9 0.7 fusion.40
  173.6 0.6 fusion.6
  174.3 0.8 fusion.17
  175.1 0.7 maximum_bitcast_fusion.1
  (31 shorter events, 0.2 us)
Async XLA Ops:
  7.2 11.5 %copy-start.3 = (bf16[2048,4]{0,1:T(4,128)(2,1)S(1)}, bf16[2048,4]{0,1:T(4,128)(2,1)}, u32[]{:S(2)}) copy-start(bf16[2048,4]{0,1:T(4,128)(2,1)} %param.13) | copy-start | bytes 49156
  7.2 56.6 %all-gather.2.cloned.1.call-start = ((), (), s32[]{:S(2)}) async-start(), calls=%async_computation.2 | async-start | bytes 2359296 | tf_op jit(solution)/shard_map/all_gather | solution.py:96
  9.7 87.6 %all-to-all-start.1 = ((bf16[8,128,128]{2,1,0:T(8,128)(2,1)}), bf16[8,128,128]{2,1,0:T(8,128)(2,1)S(1)}, u32[]{:S(2)}, u32[]{:S(2)}) async-start(bf16[8,128,128]{2,1,0:T(8,128)(2,1)} %bitcast.11), calls=%async_computation.1 | async-start | bytes 524288 | tf_op jit(solution)/shard_map/all_to_all | solution.py:133
  67.8 22.1 %copy-start = (bf16[256,512]{1,0:T(8,128)(2,1)S(1)}, bf16[256,512]{1,0:T(8,128)(2,1)}, u32[]{:S(2)}) copy-start(bf16[256,512]{1,0:T(8,128)(2,1)} %param.10) | copy-start | bytes 786436
  67.8 22.1 %copy-start.4 = (f32[512]{0:T(512)S(1)}, f32[512]{0:T(512)}, u32[]{:S(2)}) copy-start(f32[512]{0:T(512)} %param.12) | copy-start | bytes 6148
  89.6 7.3 %copy-start.1 = (bf16[256,4,128]{2,1,0:T(4,128)(2,1)S(1)}, bf16[256,4,128]{2,1,0:T(4,128)(2,1)}, u32[]{:S(2)}) copy-start(bf16[256,4,128]{2,1,0:T(4,128)(2,1)} %reshape.119) | copy-start | bytes 786436
  91.0 7.3 %copy-start.2 = (bf16[256,512]{1,0:T(8,128)(2,1)}, bf16[256,512]{1,0:T(8,128)(2,1)S(1)}, u32[]{:S(2)}) copy-start(bf16[256,512]{1,0:T(8,128)(2,1)S(1)} %get-tuple-element.130) | copy-start | bytes 786436
  98.3 73.2 %all-to-all-start = ((bf16[8,256,256]{2,1,0:T(8,128)(2,1)}), bf16[8,256,256]{2,1,0:T(8,128)(2,1)S(1)}, u32[]{:S(2)}, u32[]{:S(2)}) async-start(bf16[8,256,256]{2,1,0:T(8,128)(2,1)} %bitcast.7), calls=%async_computation | async-start | bytes 2097152 | tf_op jit(solution)/shard_map/all_to_all | solution.py:134
Sparse Core Ops, SparseCore 0:
  10.1 53.6 all-gather.1
where the time goes:
time: 184 us; the launch traced here: 183 us
  waiting for transfers between devices  71 us (39%)
  starting transfers between devices  55.4 us (30%)
  local copies, waits for them, and re-layouts  18.5 us (10%)
  between operations  14.2 us (8%)
  loops' own time  11 us (6%)
  blocking collectives  5.67 us (3%)
  other arithmetic  4.01 us (2%)
  matrix products  2.89 us (2%)
    all_to_all x1, starting transfers between devices, shards(): lax.all_to_all(pair_send, 'seq', split_axis=0, concat_axis=1, tiled=True)  48.1 us
    all_gather x1, waiting for transfers between devices, shards(): incoming = lax.all_gather(signal, 'seq', axis=0, tiled=True)  45.1 us
    all_to_all x1, waiting for transfers between devices, shards(): lax.all_to_all(pair_send, 'seq', split_axis=0, concat_axis=1, tiled=True)  25.1 us
    another operation x1, loops' own time, shards(): totals, unused = lax.scan(step_block, totals, (blocks, starts))  10.2 us
    all_to_all x1, starting transfers between devices, shards(): lax.all_to_all(query_send, 'seq', split_axis=0, concat_axis=1, tiled=True)  7.28 us
    dynamic_slice x9, local copies, waits for them, and re-layouts, shards(): totals, unused = lax.scan(step_block, totals, (blocks, starts))  6.09 us
    psum x1, blocking collectives, shards(): whole_sum = lax.psum(squares, 'chan')  5.67 us
    while x2, local copies, waits for them, and re-layouts, shards(): totals, unused = lax.scan(step_block, totals, (blocks, starts))  4.11 us
  transfers between devices with their start and end apart: 3, of which 2 were waited for; matrix products, arithmetic and copies ran while one was open for 11% of the time, Pallas kernels for 0%

commit v1 on v0

v1 whole, which is shorter than its diff:
```python
import functools
import math

import jax
import jax.numpy as jnp
from jax import lax
from jax.experimental import pallas as pl
from jax.experimental.pallas import tpu as pltpu
from jax.sharding import PartitionSpec as P

BF16, F32 = jnp.bfloat16, jnp.float32
QUERY_BLOCK = 256
KEY_CHUNK = 512
VMEM_LIMIT = 56 * 1024 * 1024
NT = (((1,), (1,)), ((), ()))


def call(kernel, out_shape, flops=0, exps=0, moved=0, **options):
    return pl.pallas_call(
        kernel,
        out_shape=out_shape,
        compiler_params=pltpu.CompilerParams(vmem_limit_bytes=VMEM_LIMIT),
        cost_estimate=pl.CostEstimate(flops=flops, bytes_accessed=moved, transcendentals=exps),
        **options,
    )


def merge_rows(blocks):
    count, rows, columns = blocks.shape
    if blocks.dtype == BF16 and rows % 16:
        return blocks.astype(F32).reshape(count * rows, columns).astype(BF16)
    return blocks.reshape(count * rows, columns)


def loop(count, body, carry):
    if count <= 8:
        for index in range(count):
            carry = body(index, carry)
        return carry
    return lax.fori_loop(0, count, body, carry)


def split_kernel(signal_ref, gate_ref, sent_ref):
    count, _, rows, positions = sent_ref.shape
    for slot, ref in enumerate((signal_ref, gate_ref)):
        turned = ref[...].astype(F32).T
        sent_ref[:, slot] = turned.reshape(count, rows, positions).astype(BF16)


def pack_kernel(sets, query_ref, key_ref, sent_ref):
    count, _, rows, head_dim = sent_ref.shape
    for device in range(count):
        head, part = divmod(device, sets)
        for slot, ref in enumerate((query_ref, key_ref)):
            sent_ref[device, slot] = ref[
                part * rows : (part + 1) * rows, head * head_dim : (head + 1) * head_dim
            ]


def unsplit_kernel(got_ref, out_ref):
    out_ref[...] = merge_rows(got_ref[...].astype(F32)).T.astype(BF16)


def toeplitz_kernel(head_count_per, taps_ref, matrix_ref):
    block, length = matrix_ref.shape
    head = lax.axis_index("seq") // head_count_per
    taps = taps_ref[...].astype(F32)
    mine = lax.broadcasted_iota(jnp.int32, taps.shape, 0) == head
    row = jnp.sum(jnp.where(mine, taps, 0.0), axis=0, keepdims=True)
    rolled = pltpu.roll(jnp.broadcast_to(row, (block, length)), 0, 1, stride=1, stride_axis=0)
    source = lax.broadcasted_iota(jnp.int32, (block, block), 0)
    target = lax.broadcasted_iota(jnp.int32, (block, block), 1)
    matrix_ref[:, :block] = jnp.where(target >= source, rolled[:, :block], 0.0).astype(BF16)
    matrix_ref[:, block:] = rolled[:, block:].astype(BF16)


def conv_kernel(got_ref, matrix_ref, skip_ref, mixed_ref, squares_ref, total_ref):
    count, _, rows, block = got_ref.shape
    inputs = merge_rows(got_ref[:, 0])
    for lag in range(count):
        product = jnp.dot(
            inputs[: (count - lag) * rows],
            matrix_ref[:, lag * block : (lag + 1) * block],
            preferred_element_type=F32,
        )
        if lag == 0:
            total_ref[...] = product
        else:
            total_ref[lag * rows :] += product
    skip = skip_ref[...]
    sums = []
    for index in range(count):
        conv = total_ref[index * rows : (index + 1) * rows]
        direct = skip * got_ref[index, 0].astype(F32)
        mixed = (got_ref[index, 1].astype(F32) * (conv + direct)).astype(BF16)
        mixed_ref[index] = mixed
        widened = mixed.astype(F32)
        sums.append(jnp.sum(widened * widened, axis=0, keepdims=True))
    squares = jnp.concatenate(sums, axis=0).astype(BF16)
    for device in range(squares_ref.shape[0]):
        squares_ref[device] = squares


def weights_block(step, last, key_ref, query, sets, rows, scores_ref, weights_ref, total_ref):
    wide = query.shape[0]
    seq_block = sets * rows
    reach = wide // rows * seq_block
    chunk = min(KEY_CHUNK, reach)
    chunks = (step + 1) * reach // chunk
    head_dim = query.shape[1]
    factor = math.log2(math.e) / math.sqrt(head_dim)
    mine = lax.rem(lax.axis_index("seq"), sets)
    lane = step * wide + lax.broadcasted_iota(jnp.int32, (1, wide), 1)
    query_pos = lane // rows * seq_block + mine * rows + lax.rem(lane, rows)

    def score(index, peak):
        first = index * chunk
        part = key_ref[pl.ds(first, chunk), :]
        raw = lax.dot_general(part, query, NT, preferred_element_type=F32)
        if not isinstance(index, int) or first + chunk - 1 > step * reach:
            key_pos = first + lax.broadcasted_iota(jnp.int32, (chunk, 1), 0)
            raw = jnp.where(key_pos <= query_pos, raw, -jnp.inf)
        scores_ref[pl.ds(first, chunk), :] = raw
        return jnp.maximum(peak, jnp.max(raw, axis=0, keepdims=True))

    peak = loop(chunks, score, jnp.full((1, wide), -jnp.inf, F32))

    def weigh(index, total):
        first = index * chunk
        weights = jnp.exp2((scores_ref[pl.ds(first, chunk), :] - peak) * factor)
        weights_ref[pl.ds(first, chunk), :] = weights.astype(BF16)
        return total + jnp.sum(weights, axis=0, keepdims=True)

    total = loop(chunks, weigh, jnp.zeros((1, wide), F32))
    total_ref[...] = jnp.broadcast_to(total, total_ref.shape)


def weights_kernel(sets, gridded, got_ref, *refs):
    others, (weights_ref, total_ref, key_ref, query_ref, scores_ref) = refs[:-5], refs[-5:]
    count, _, rows, head_dim = got_ref.shape
    mine = lax.rem(lax.axis_index("seq"), sets)

    def assemble():
        query_ref[...] = merge_rows(got_ref[:, 0])
        for offset in range(sets):
            keys = got_ref[:, 1] if offset == 0 else others[offset - 1][...]
            place = lax.rem(mine + offset, sets)
            key_ref[:, pl.ds(place, 1)] = keys[:, None]

    steps = query_ref.shape[0] // QUERY_BLOCK
    keys = key_ref.reshape(count * sets * rows, head_dim)

    def block(step, weights, total):
        query = query_ref[step * QUERY_BLOCK : (step + 1) * QUERY_BLOCK]
        weights_block(step, steps - 1, keys, query, sets, rows, scores_ref, weights, total)

    if not gridded:
        assemble()
        for step in range(steps):
            block(step, weights_ref.at[step], total_ref.at[step])
        return
    pl.when(pl.program_id(0) == 0)(assemble)
    for step in range(steps):
        pl.when(pl.program_id(0) == step)(
            functools.partial(block, step, weights_ref.at[0], total_ref.at[0])
        )


def output_kernel(sets, width, gridded, squares_ref, weights_ref, total_ref, mixed_ref, *refs):
    others, (out_ref, wide_ref, values_ref) = refs[:-3], refs[-3:]
    count, rows, block = mixed_ref.shape
    mine = lax.rem(lax.axis_index("seq"), sets)
    steps = count * block // sets // QUERY_BLOCK
    reach = count * block // steps

    def norm():
        squares = jnp.sum(squares_ref[...].astype(F32), axis=0)
        inv_scale = lax.rsqrt(squares / width + 1e-06)
        for offset in range(sets):
            ref = mixed_ref if offset == 0 else others[offset - 1]
            place = lax.rem(mine + offset, sets)
            for index in range(count):
                part = ref[index].astype(F32) * inv_scale[index : index + 1]
                wide_ref[place, :, index * block : (index + 1) * block] = part
        for index in range(count):
            span = slice(index * block, (index + 1) * block)
            values_ref[:, span] = merge_rows(wide_ref[:, :, span]).astype(BF16)

    def attend(step, weights, total, out):
        keys = (step + 1) * reach
        summed = jnp.dot(values_ref[:, :keys], weights[:keys], preferred_element_type=F32)
        out[...] = (summed / total[:1]).T.astype(BF16)

    if not gridded:
        norm()
        for step in range(steps):
            rows_out = out_ref.at[pl.ds(step * QUERY_BLOCK, QUERY_BLOCK)]
            attend(step, weights_ref.at[step], total_ref.at[step], rows_out)
        return
    pl.when(pl.program_id(0) == 0)(norm)
    for step in range(steps):
        pl.when(pl.program_id(0) == step)(
            functools.partial(attend, step, weights_ref.at[0], total_ref.at[0], out_ref)
        )


def shards(signal, gate_rows, skip_gain, filter_taps, queries, key_rows):
    block, local_width = signal.shape
    heads_loc = filter_taps.shape[1]
    head_dim = local_width // heads_loc
    seq_count = lax.axis_size("seq")
    chan_count = lax.axis_size("chan")
    everyone = seq_count * chan_count
    length = block * seq_count
    sets = seq_count // heads_loc
    rows = block // sets
    channels = local_width // seq_count
    query_len = length // sets
    steps = query_len // QUERY_BLOCK
    gridded = length > 4096
    shape = jax.ShapeDtypeStruct

    def set_neighbour(array, offset):
        pairs = []
        for head in range(heads_loc):
            for part in range(sets):
                pairs.append((head * sets + (part + offset) % sets, head * sets + part))
        return lax.ppermute(array, "seq", pairs)

    split = call(
        split_kernel, shape((seq_count, 2, channels, block), BF16), moved=4 * signal.size * 2
    )(signal, gate_rows)
    split_got = lax.all_to_all(split, "seq", 0, 0, tiled=True)

    pack = call(
        functools.partial(pack_kernel, sets),
        shape((seq_count, 2, rows, head_dim), BF16),
        moved=4 * signal.size * 2,
    )(queries, key_rows)
    pack_got = lax.all_to_all(pack, "seq", 0, 0, tiled=True)

    matrix = call(
        functools.partial(toeplitz_kernel, sets),
        shape((block, length), BF16),
        moved=block * length * 2,
        flops=block * length * 8,
    )(filter_taps.T)
    skip = lax.dynamic_slice_in_dim(skip_gain, lax.axis_index("seq") * channels, channels)
    mixed, squares = call(
        conv_kernel,
        (
            shape((seq_count, channels, block), BF16),
            shape((everyone, seq_count, block), BF16),
        ),
        moved=split.size * 6,
        flops=length * length * channels,
        scratch_shapes=[pltpu.VMEM((seq_count * channels, block), F32)],
    )(split_got, matrix, skip[:, None])

    squares_got = lax.all_to_all(squares, ("seq", "chan"), 0, 0, tiled=True)
    mixed_others = [set_neighbour(mixed, offset) for offset in range(1, sets)]
    mixed_home = lax.all_to_all(mixed, "seq", 0, 0, tiled=True)

    key_others = [set_neighbour(pack_got[:, 1], offset) for offset in range(1, sets)]
    weights_shape = (steps, length, QUERY_BLOCK)
    total_shape = (steps, 8, QUERY_BLOCK)
    one = lambda dims: pl.BlockSpec((1,) + dims[1:], lambda step: (step, 0, 0))
    whole = pl.BlockSpec(memory_space=pltpu.VMEM)
    grid = dict(grid=(steps,), out_specs=(one(weights_shape), one(total_shape)))
    grid["in_specs"] = [whole] * sets
    weights, totals = call(
        functools.partial(weights_kernel, sets, gridded),
        (shape(weights_shape, BF16), shape(total_shape, F32)),
        moved=steps * length * QUERY_BLOCK * 2,
        flops=query_len * length * head_dim,
        exps=query_len * length // 2,
        scratch_shapes=[
            pltpu.VMEM((seq_count, sets, rows, head_dim), BF16),
            pltpu.VMEM((query_len, head_dim), BF16),
            pltpu.VMEM((length, QUERY_BLOCK), F32),
        ],
        **(grid if gridded else {}),
    )(pack_got, *key_others)

    grid = dict(grid=(steps,), out_specs=pl.BlockSpec((QUERY_BLOCK, head_dim), lambda step: (step, 0)))
    grid["in_specs"] = [whole, one(weights_shape), one(total_shape)] + [whole] * sets
    attended = call(
        functools.partial(output_kernel, sets, local_width * chan_count, gridded),
        shape((query_len, head_dim), BF16),
        moved=steps * length * QUERY_BLOCK * 2,
        flops=query_len * length * head_dim,
        scratch_shapes=[
            pltpu.VMEM((sets, channels, length), F32),
            pltpu.VMEM((head_dim, length), BF16),
        ],
        **(grid if gridded else {}),
    )(squares_got, weights, totals, mixed, *mixed_others)

    conv_mixed = call(unsplit_kernel, shape((block, local_width), BF16), moved=signal.size * 4)(
        mixed_home
    )
    return (conv_mixed, attended[None])


def solution(mesh):
    in_specs = (
        P("seq", "chan"),
        P("seq", "chan"),
        P("chan"),
        P(None, "chan"),
        P("seq", "chan"),
        P("seq", "chan"),
    )
    out_specs = (P("seq", "chan"), P(("chan", "seq"), None, None))
    return jax.shard_map(shards, mesh=mesh, in_specs=in_specs, out_specs=out_specs, check_vma=False)
```

time: 184 us -> 83.5 us (0.45)
  waiting for transfers between devices: 71 us -> 31.8 us
  starting transfers between devices: 55.4 us -> 16.4 us
  Pallas kernels: 0 us -> 19 us
  local copies, waits for them, and re-layouts: 18.5 us -> 2.91 us
  between operations: 14.2 us -> 0.67 us
  loops' own time: 11 us -> 0 us
  blocking collectives: 5.67 us -> 12 us
  other arithmetic: 4.01 us -> 0 us
  matrix products: 2.89 us -> 0 us
    all_gather x1 -> x0, waiting for transfers between devices: 45.1 us -> none  [shards(): incoming = lax.all_gather(signal, 'seq', axis=0, tiled=True)]
    all_to_all x2 -> x3, starting transfers between devices: 55.3 us -> 14.3 us  [the longest x1 7.28 us: shards(): split_got = lax.all_to_all(split, 'seq', 0, 0, tiled=True)]
    pallas_call x0 -> x7, Pallas kernels: none -> 19 us  [the longest x1 5 us: shards(): call(functools.partial(weights_kernel, sets, gridded), (shape(weights_sha...]
    all_to_all x0 -> x1, blocking collectives: none -> 12 us  [shards(): squares_got = lax.all_to_all(squares, ('seq', 'chan'), 0, 0, tiled=True)]
    another operation x9 -> x0, loops' own time: 11 us -> none  [the longest x1 10.2 us: shards(): totals, unused = lax.scan(step_block, totals, (blocks, starts))]
    ppermute x0 -> x2, waiting for transfers between devices: none -> 9.93 us  [set_neighbour(): return lax.ppermute(array, 'seq', pairs)]
    dynamic_slice x10 -> x0, local copies, waits for them, and re-layouts: 6.18 us -> none  [the longest x9 6.09 us: shards(): totals, unused = lax.scan(step_block, totals, (blocks, starts))]
    psum x1 -> x0, blocking collectives: 5.67 us -> none  [shards(): whole_sum = lax.psum(squares, 'chan')]
  transfers between devices with their start and end apart: 3 -> 5, of which waited for: 2 -> 3; matrix products, arithmetic and copies ran while one was open for 11% -> 1% of each run, Pallas kernels for 0% -> 18%
where the time goes in v1:
time: 83.5 us; the launch traced here: 82.9 us
  waiting for transfers between devices  31.8 us (38%)
  Pallas kernels  19 us (23%)
  starting transfers between devices  16.4 us (20%)
  blocking collectives  12 us (14%)
  local copies, waits for them, and re-layouts  2.91 us (3%)
    all_to_all x1, waiting for transfers between devices, shards(): split_got = lax.all_to_all(split, 'seq', 0, 0, tiled=True)  12.5 us
    all_to_all x1, blocking collectives, shards(): squares_got = lax.all_to_all(squares, ('seq', 'chan'), 0, 0, tiled=True)  12 us
    ppermute x2, waiting for transfers between devices, set_neighbour(): return lax.ppermute(array, 'seq', pairs)  9.93 us
    all_to_all x1, waiting for transfers between devices, shards(): pack_got = lax.all_to_all(pack, 'seq', 0, 0, tiled=True)  9.37 us
    all_to_all x1, starting transfers between devices, shards(): split_got = lax.all_to_all(split, 'seq', 0, 0, tiled=True)  7.28 us
    pallas_call x1, Pallas kernels, shards(): call(functools.partial(weights_kernel, sets, gridded), (shape(weights_sha...  5 us
    pallas_call x1, Pallas kernels, shards(): call(functools.partial(output_kernel, sets, local_width * chan_count, gri...  3.77 us
    all_to_all x1, starting transfers between devices, shards(): pack_got = lax.all_to_all(pack, 'seq', 0, 0, tiled=True)  3.64 us
  transfers between devices with their start and end apart: 5, of which 3 were waited for; matrix products, arithmetic and copies ran while one was open for 1% of the time, Pallas kernels for 18%

profile of v1, /device:TPU:0, one launch (start us, length us, event | category | flops | bytes accessed | tf_op | source)
XLA Modules:
  0.0 82.9 jit_solution(12906561120686115984)
XLA Ops:
  0.6 0.0 copy-start
  0.6 2.0 %shard_map.77 = bf16[8,2,64,256]{3,2,1,0:T(8,128)(2,1)} custom-call(bf16[256,512]{1,0:T(8,128)(2,1)} %signal_ref.1, bf16[256,512]{1,0:T(8,128)(2,1)} %gate_ref.1), custom_call_target="tpu_custom_call" | custom-call | bytes 1048576 | tf_op jit(solution)/shard_map/pallas_call | solution.py:230
  2.7 7.3 %all-to-all-start = ((bf16[8,2,64,256]{3,2,1,0:T(8,128)(2,1)}), bf16[8,2,64,256]{3,2,1,0:T(8,128)(2,1)S(1)}, u32[]{:S(2)}, u32[]{:S(2)}) async-start(bf16[8,2,64,256]{3,2,1,0:T(8,128)(2,1)} %shard_map.77), calls=%async_computation | async-start | bytes 1048576 | tf_op jit(solution)/shard_map/all_to_all | solution.py:233
  10.0 1.9 %shard_map.81 = bf16[8,2,128,128]{3,2,1,0:T(8,128)(2,1)} custom-call(bf16[256,512]{1,0:T(8,128)(2,1)} %query_ref.1, bf16[256,512]{1,0:T(8,128)(2,1)} %key_ref.1), custom_call_target="tpu_custom_call" | custom-call | bytes 1048576 | tf_op jit(solution)/shard_map/pallas_call | solution.py:235
  11.9 12.5 %all-to-all-done.got_ref = bf16[8,2,64,256]{3,2,1,0:T(8,128)(2,1)S(1)} async-done(((bf16[8,2,64,256]{3,2,1,0:T(8,128)(2,1)}), bf16[8,2,64,256]{3,2,1,0:T(8,128)(2,1)S(1)}, u32[]{:S(2)}, u32[]{:S(2)}) %all-to-all-start) | async-done | bytes 524320 | tf_op jit(solution)/shard_map/all_to_all | solution.py:233
  24.4 0.0 copy-start.1
  24.4 3.6 %all-to-all-start.3 = ((bf16[8,2,128,128]{3,2,1,0:T(8,128)(2,1)}), bf16[8,2,128,128]{3,2,1,0:T(8,128)(2,1)S(1)}, u32[]{:S(2)}, u32[]{:S(2)}) async-start(bf16[8,2,128,128]{3,2,1,0:T(8,128)(2,1)} %shard_map.81), calls=%async_computation.3 | async-start | bytes 1048576 | tf_op jit(solution)/shard_map/all_to_all | solution.py:240
  28.1 0.0 copy-done
  28.1 0.1 dynamic-slice_bitcast_fusion
  28.2 0.7 copy.11.skip_ref
  28.9 1.9 %shard_map.78.matrix_ref = bf16[256,2048]{1,0:T(8,128)(2,1)} custom-call(bf16[4,2048]{1,0:T(4,128)(2,1)} %bitcast.9), custom_call_target="tpu_custom_call" | custom-call | flops 4194304 | bytes 1048576 | tf_op jit(solution)/shard_map/pallas_call | solution.py:242
  30.8 0.0 copy-done.1
  30.8 2.6 %shard_map.79 = (bf16[8,64,256]{2,1,0:T(8,128)(2,1)}, bf16[32,8,256]{2,1,0:T(8,128)(2,1)}) custom-call(bf16[8,2,64,256]{3,2,1,0:T(8,128)(2,1)} %copy-done.1, bf16[256,2048]{1,0:T(8,128)(2,1)} %shard_map.78.matrix_ref, f32[64,1]{1,0:T(8,128)} %copy.11.skip_ref), custom_call_target="tpu_custom_call" | custom-call | flops 268435456 | bytes 1572864 | tf_op jit(solution)/shard_map/pallas_call | solution.py:249
  33.4 9.4 %all-to-all-done.3.got_ref = bf16[8,2,128,128]{3,2,1,0:T(8,128)(2,1)S(1)} async-done(((bf16[8,2,128,128]{3,2,1,0:T(8,128)(2,1)}), bf16[8,2,128,128]{3,2,1,0:T(8,128)(2,1)S(1)}, u32[]{:S(2)}, u32[]{:S(2)}) %all-to-all-start.3) | async-done | bytes 524320 | tf_op jit(solution)/shard_map/all_to_all | solution.py:240
  42.8 0.0 copy-start.2
  42.8 12.0 %all_to_all.20.squares_ref = bf16[32,8,256]{2,1,0:T(8,128)(2,1)} all-to-all(bf16[32,8,256]{2,1,0:T(8,128)(2,1)} %get-tuple-element.7), channel_id=1, replica_groups=mesh['seq'=8,'chan'=4] {'seq','chan'}, dimensions={0} | all-to-all | bytes 262144 | tf_op jit(solution)/shard_map/all_to_all | solution.py:260
  54.7 3.4 %all-to-all-start.1 = ((bf16[8,64,256]{2,1,0:T(8,128)(2,1)}), bf16[8,64,256]{2,1,0:T(8,128)(2,1)S(1)}, u32[]{:S(2)}, u32[]{:S(2)}) async-start(bf16[8,64,256]{2,1,0:T(8,128)(2,1)} %get-tuple-element.6.mixed_ref), calls=%async_computation.1 | async-start | bytes 524288 | tf_op jit(solution)/shard_map/all_to_all | solution.py:262
  58.2 2.0 %collective-permute-start = (bf16[8,128,128]{2,1,0:T(8,128)(2,1)S(1)}, bf16[8,128,128]{2,1,0:T(8,128)(2,1)S(1)}, u32[]{:S(2)}, u32[]{:S(2)}) collective-permute-start(bf16[8,128,128]{2,1,0:T(8,128)(2,1)S(1)} %slice_bitcast_fusion), channel_id=1, source_target_pairs={{4,0},{0,4},{12,8},{8,12},{20,16},{16,20},{28,24},{24,28},{5,1},{1... | collective-permute-start | bytes 786440 | tf_op jit(solution)/shard_map/ppermute | solution.py:228
  60.2 0.1 collective-permute-start.1
  60.3 9.9 %collective-permute-done.refs_0_ = bf16[8,128,128]{2,1,0:T(8,128)(2,1)S(1)} collective-permute-done((bf16[8,128,128]{2,1,0:T(8,128)(2,1)S(1)}, bf16[8,128,128]{2,1,0:T(8,128)(2,1)S(1)}, u32[]{:S(2)}, u32[]{:S(2)}) %collective-permute-start) | collective-permute-done | bytes 262176 | tf_op jit(solution)/shard_map/ppermute | solution.py:228
  70.2 0.0 copy-done.2
  70.2 0.0 copy-start.5
  70.2 0.7 copy-done.5
  70.9 5.0 %shard_map.82 = (bf16[4,2048,256]{2,1,0:T(8,128)(2,1)}, f32[4,8,256]{2,1,0:T(8,128)}) custom-call(bf16[8,2,128,128]{3,2,1,0:T(8,128)(2,1)} %copy-done.2, bf16[8,128,128]{2,1,0:T(8,128)(2,1)} %copy-done.5), custom_call_target="tpu_custom_call" | custom-call | flops 268435456 | bytes 4194304 | tf_op jit(solution)/shard_map/pallas_call | solution.py:271
  75.9 0.0 collective-permute-done.1.refs_0_
  75.9 0.0 copy-start.4
  75.9 0.7 copy-done.4
  76.6 3.8 %shard_map.83 = bf16[1024,128]{1,0:T(8,128)(2,1)} custom-call(bf16[32,8,256]{2,1,0:T(8,128)(2,1)} %all_to_all.20.squares_ref, bf16[4,2048,256]{2,1,0:T(8,128)(2,1)} %get-tuple-element.8.weights_ref, f32[4,8,256]{2,1,0:T(8,128)} %get-tuple-element.9.total_ref, bf16[8,64,256]{2,1,0:T(8,128)(2,1)} %get-tuple-element.6.mixed_ref, bf16[8,64,256]{2,1,0:T(8,128)(2,1)} %copy-done.4), custom_call_target="tpu_custom_call" | custom-call | flops 268435456 | bytes 4194304 | tf_op jit(solution)/shard_map/pallas_call | solution.py:287
  80.4 0.0 all-to-all-done.1.got_ref
  80.4 0.0 copy-start.3
  80.4 0.7 copy-done.3
  81.1 1.8 %shard_map.80 = bf16[256,512]{1,0:T(8,128)(2,1)} custom-call(bf16[8,64,256]{2,1,0:T(8,128)(2,1)} %copy-done.3), custom_call_target="tpu_custom_call" | custom-call | bytes 524288 | tf_op jit(solution)/shard_map/pallas_call | solution.py:299
  (1 shorter events, 0.0 us)
Async XLA Ops:
  0.6 27.5 %copy-start = (f32[512]{0:T(512)S(1)}, f32[512]{0:T(512)}, u32[]{:S(2)}) copy-start(f32[512]{0:T(512)} %param.8) | copy-start | bytes 6148
  2.7 21.8 %all-to-all-start = ((bf16[8,2,64,256]{3,2,1,0:T(8,128)(2,1)}), bf16[8,2,64,256]{3,2,1,0:T(8,128)(2,1)S(1)}, u32[]{:S(2)}, u32[]{:S(2)}) async-start(bf16[8,2,64,256]{3,2,1,0:T(8,128)(2,1)} %shard_map.77), calls=%async_computation | async-start | bytes 1048576 | tf_op jit(solution)/shard_map/all_to_all | solution.py:233
  24.4 6.3 %copy-start.1 = (bf16[8,2,64,256]{3,2,1,0:T(8,128)(2,1)}, bf16[8,2,64,256]{3,2,1,0:T(8,128)(2,1)S(1)}, u32[]{:S(2)}) copy-start(bf16[8,2,64,256]{3,2,1,0:T(8,128)(2,1)S(1)} %all-to-all-done.got_ref) | copy-start | bytes 1572868
  24.4 18.3 %all-to-all-start.3 = ((bf16[8,2,128,128]{3,2,1,0:T(8,128)(2,1)}), bf16[8,2,128,128]{3,2,1,0:T(8,128)(2,1)S(1)}, u32[]{:S(2)}, u32[]{:S(2)}) async-start(bf16[8,2,128,128]{3,2,1,0:T(8,128)(2,1)} %shard_map.81), calls=%async_computation.3 | async-start | bytes 1048576 | tf_op jit(solution)/shard_map/all_to_all | solution.py:240
  42.8 27.5 %copy-start.2 = (bf16[8,2,128,128]{3,2,1,0:T(8,128)(2,1)}, bf16[8,2,128,128]{3,2,1,0:T(8,128)(2,1)S(1)}, u32[]{:S(2)}) copy-start(bf16[8,2,128,128]{3,2,1,0:T(8,128)(2,1)S(1)} %all-to-all-done.3.got_ref) | copy-start | bytes 1572868
  54.7 25.7 %all-to-all-start.1 = ((bf16[8,64,256]{2,1,0:T(8,128)(2,1)}), bf16[8,64,256]{2,1,0:T(8,128)(2,1)S(1)}, u32[]{:S(2)}, u32[]{:S(2)}) async-start(bf16[8,64,256]{2,1,0:T(8,128)(2,1)} %get-tuple-element.6.mixed_ref), calls=%async_computation.1 | async-start | bytes 524288 | tf_op jit(solution)/shard_map/all_to_all | solution.py:262
  58.2 12.0 %collective-permute-start = (bf16[8,128,128]{2,1,0:T(8,128)(2,1)S(1)}, bf16[8,128,128]{2,1,0:T(8,128)(2,1)S(1)}, u32[]{:S(2)}, u32[]{:S(2)}) collective-permute-start(bf16[8,128,128]{2,1,0:T(8,128)(2,1)S(1)} %slice_bitcast_fusion), channel_id=1, source_target_pairs={{4,0},{0,4},{12,8},{8,12},{20,16},{16,20},{28,24},{24,28},{5,1},{1... | collective-permute-start | bytes 786440 | tf_op jit(solution)/shard_map/ppermute | solution.py:228
  60.2 15.8 %collective-permute-start.1 = (bf16[8,64,256]{2,1,0:T(8,128)(2,1)}, bf16[8,64,256]{2,1,0:T(8,128)(2,1)S(1)}, u32[]{:S(2)}, u32[]{:S(2)}) collective-permute-start(bf16[8,64,256]{2,1,0:T(8,128)(2,1)} %get-tuple-element.6.mixed_ref), channel_id=1, source_target_pairs={{4,0},{0,4},{12,8},{8,12},{20,16},{16,20},{28,24},{24,28},{5,1},{1... | collective-permute-start | bytes 786440 | tf_op jit(solution)/shard_map/ppermute | solution.py:228
  70.2 0.7 copy-start.5
  75.9 0.7 copy-start.4
  80.4 0.7 copy-start.3

commit v2 on v1

--- a/solution.py
+++ b/solution.py
@@ -11,15 +11,14 @@
 BF16, F32 = jnp.bfloat16, jnp.float32
 QUERY_BLOCK = 256
 KEY_CHUNK = 512
-VMEM_LIMIT = 56 * 1024 * 1024
 NT = (((1,), (1,)), ((), ()))
 
 
-def call(kernel, out_shape, flops=0, exps=0, moved=0, **options):
+def call(kernel, out_shape, flops=0, exps=0, moved=0, vmem=8, **options):
     return pl.pallas_call(
         kernel,
         out_shape=out_shape,
-        compiler_params=pltpu.CompilerParams(vmem_limit_bytes=VMEM_LIMIT),
+        compiler_params=pltpu.CompilerParams(vmem_limit_bytes=vmem * 1024 * 1024),
         cost_estimate=pl.CostEstimate(flops=flops, bytes_accessed=moved, transcendentals=exps),
         **options,
     )
@@ -40,25 +39,55 @@
     return lax.fori_loop(0, count, body, carry)
 
 
-def split_kernel(signal_ref, gate_ref, sent_ref):
+def pack_kernel(sets, *refs):
+    sources, (sent_ref, held_ref, semaphores) = refs[:4], refs[4:]
     count, _, rows, positions = sent_ref.shape
-    for slot, ref in enumerate((signal_ref, gate_ref)):
-        turned = ref[...].astype(F32).T
+    head_dim = positions // 2
+    copies = [
+        pltpu.make_async_copy(source, held_ref.at[slot], semaphores.at[slot])
+        for slot, source in enumerate(sources)
+    ]
+    for copy in copies:
+        copy.start()
+    for slot in (0, 1):
+        copies[slot].wait()
+        turned = held_ref[slot].astype(F32).T
         sent_ref[:, slot] = turned.reshape(count, rows, positions).astype(BF16)
-
-
-def pack_kernel(sets, query_ref, key_ref, sent_ref):
-    count, _, rows, head_dim = sent_ref.shape
-    for device in range(count):
-        head, part = divmod(device, sets)
-        for slot, ref in enumerate((query_ref, key_ref)):
-            sent_ref[device, slot] = ref[
-                part * rows : (part + 1) * rows, head * head_dim : (head + 1) * head_dim
-            ]
-
-
-def unsplit_kernel(got_ref, out_ref):
-    out_ref[...] = merge_rows(got_ref[...].astype(F32)).T.astype(BF16)
+    for slot in (2, 3):
+        copies[slot].wait()
+        for device in range(count):
+            head, part = divmod(device, sets)
+            first = part * 2 * rows
+            lanes = slice(head * head_dim, (head + 1) * head_dim)
+            sent_ref[device, slot] = side_by_side(held_ref[slot, first : first + 2 * rows, lanes])
+
+
+def side_by_side(piece):
+    rows = piece.shape[0] // 2
+    if rows % 16:
+        return side_by_side32(piece.astype(F32)).astype(BF16)
+    return side_by_side32(piece)
+
+
+def side_by_side32(piece):
+    rows = piece.shape[0] // 2
+    return jnp.concatenate([piece[:rows], piece[rows:]], axis=1)
+
+
+def one_below_other(wide):
+    columns = wide.shape[2] // 2
+    if wide.shape[1] % 16:
+        return one_below_other(wide.astype(F32)).astype(BF16) if wide.dtype == BF16 else (
+            jnp.concatenate([wide[:, :, :columns], wide[:, :, columns:]], axis=1)
+        )
+    return jnp.concatenate([wide[:, :, :columns], wide[:, :, columns:]], axis=1)
+
+
+def unpack_kernel(got_ref, out_ref):
+    count = got_ref.shape[0]
+    rows = out_ref.shape[1] // count
+    whole = got_ref[:, :rows].astype(F32).reshape(count * rows, got_ref.shape[2])
+    out_ref[...] = whole.T.astype(BF16)
 
 
 def toeplitz_kernel(head_count_per, taps_ref, matrix_ref):
@@ -74,7 +103,7 @@
     matrix_ref[:, block:] = rolled[:, block:].astype(BF16)
 
 
-def conv_kernel(got_ref, matrix_ref, skip_ref, mixed_ref, squares_ref, total_ref):
+def conv_kernel(got_ref, matrix_ref, skip_ref, mixed_ref, back_ref, key_ref, total_ref):
     count, _, rows, block = got_ref.shape
     inputs = merge_rows(got_ref[:, 0])
     for lag in range(count):
@@ -94,11 +123,15 @@
         direct = skip * got_ref[index, 0].astype(F32)
         mixed = (got_ref[index, 1].astype(F32) * (conv + direct)).astype(BF16)
         mixed_ref[index] = mixed
+        back_ref[index, :rows] = mixed
         widened = mixed.astype(F32)
         sums.append(jnp.sum(widened * widened, axis=0, keepdims=True))
-    squares = jnp.concatenate(sums, axis=0).astype(BF16)
-    for device in range(squares_ref.shape[0]):
-        squares_ref[device] = squares
+    squares = jnp.concatenate(sums, axis=0)
+    high = squares.astype(BF16).astype(F32)
+    both = jnp.concatenate([high, squares - high], axis=0).astype(BF16)
+    for index in range(count):
+        back_ref[index, rows:] = both
+    key_ref[...] = one_below_other(got_ref[:, 3])
 
 
 def weights_block(step, last, key_ref, query, sets, rows, scores_ref, weights_ref, total_ref):
@@ -136,16 +169,16 @@
 
 
 def weights_kernel(sets, gridded, got_ref, *refs):
-    others, (weights_ref, total_ref, key_ref, query_ref, scores_ref) = refs[:-5], refs[-5:]
-    count, _, rows, head_dim = got_ref.shape
+    parts, (key_ref, query_ref, scores_ref) = refs[:sets], refs[-3:]
+    total_ref, weights_refs = refs[sets], refs[sets + 1 : -3]
+    count, _, rows, head_dim = key_ref.shape
     mine = lax.rem(lax.axis_index("seq"), sets)
 
     def assemble():
-        query_ref[...] = merge_rows(got_ref[:, 0])
+        query_ref[...] = merge_rows(one_below_other(got_ref[:, 2]))
         for offset in range(sets):
-            keys = got_ref[:, 1] if offset == 0 else others[offset - 1][...]
             place = lax.rem(mine + offset, sets)
-            key_ref[:, pl.ds(place, 1)] = keys[:, None]
+            key_ref[:, pl.ds(place, 1)] = parts[offset][...][:, None]
 
     steps = query_ref.shape[0] // QUERY_BLOCK
     keys = key_ref.reshape(count * sets * rows, head_dim)
@@ -157,30 +190,30 @@
     if not gridded:
         assemble()
         for step in range(steps):
-            block(step, weights_ref.at[step], total_ref.at[step])
+            block(step, weights_refs[step], total_ref.at[step])
         return
     pl.when(pl.program_id(0) == 0)(assemble)
     for step in range(steps):
         pl.when(pl.program_id(0) == step)(
-            functools.partial(block, step, weights_ref.at[0], total_ref.at[0])
-        )
-
-
-def output_kernel(sets, width, gridded, squares_ref, weights_ref, total_ref, mixed_ref, *refs):
-    others, (out_ref, wide_ref, values_ref) = refs[:-3], refs[-3:]
-    count, rows, block = mixed_ref.shape
+            functools.partial(block, step, weights_refs[0].at[0], total_ref.at[0])
+        )
+
+
+def output_kernel(sets, steps, width, gridded, *refs):
+    squares_refs, refs = refs[: -4 - sets - (1 if gridded else steps)], refs[-4 - sets - (1 if gridded else steps) :]
+    parts, total_ref, weights_refs = refs[:sets], refs[sets], refs[sets + 1 : -3]
+    out_ref, wide_ref, values_ref = refs[-3:]
+    count, rows, block = parts[0].shape
     mine = lax.rem(lax.axis_index("seq"), sets)
-    steps = count * block // sets // QUERY_BLOCK
     reach = count * block // steps
 
     def norm():
-        squares = jnp.sum(squares_ref[...].astype(F32), axis=0)
+        squares = sum(ref[...] for ref in squares_refs[1:]) + squares_refs[0][...]
         inv_scale = lax.rsqrt(squares / width + 1e-06)
         for offset in range(sets):
-            ref = mixed_ref if offset == 0 else others[offset - 1]
             place = lax.rem(mine + offset, sets)
             for index in range(count):
-                part = ref[index].astype(F32) * inv_scale[index : index + 1]
+                part = parts[offset][index].astype(F32) * inv_scale[index : index + 1]
                 wide_ref[place, :, index * block : (index + 1) * block] = part
         for index in range(count):
             span = slice(index * block, (index + 1) * block)
@@ -195,12 +228,12 @@
         norm()
         for step in range(steps):
             rows_out = out_ref.at[pl.ds(step * QUERY_BLOCK, QUERY_BLOCK)]
-            attend(step, weights_ref.at[step], total_ref.at[step], rows_out)
+            attend(step, weights_refs[step], total_ref.at[step], rows_out)
         return
     pl.when(pl.program_id(0) == 0)(norm)
     for step in range(steps):
         pl.when(pl.program_id(0) == step)(
-            functools.partial(attend, step, weights_ref.at[0], total_ref.at[0], out_ref)
+            functools.partial(attend, step, weights_refs[0].at[0], total_ref.at[0], out_ref)
         )
 
 
@@ -227,78 +260,97 @@
                 pairs.append((head * sets + (part + offset) % sets, head * sets + part))
         return lax.ppermute(array, "seq", pairs)
 
-    split = call(
-        split_kernel, shape((seq_count, 2, channels, block), BF16), moved=4 * signal.size * 2
-    )(signal, gate_rows)
-    split_got = lax.all_to_all(split, "seq", 0, 0, tiled=True)
-
-    pack = call(
+    packed = call(
         functools.partial(pack_kernel, sets),
-        shape((seq_count, 2, rows, head_dim), BF16),
-        moved=4 * signal.size * 2,
-    )(queries, key_rows)
-    pack_got = lax.all_to_all(pack, "seq", 0, 0, tiled=True)
+        shape((seq_count, 4, channels, block), BF16),
+        moved=16 * signal.size,
+        in_specs=[pl.BlockSpec(memory_space=pl.ANY)] * 4,
+        vmem=56,
+        scratch_shapes=[
+            pltpu.VMEM((4,) + signal.shape, BF16),
+            pltpu.SemaphoreType.DMA((4,)),
+        ],
+    )(signal, gate_rows, queries, key_rows)
+    got = lax.all_to_all(packed, "seq", 0, 0, tiled=True)
 
     matrix = call(
         functools.partial(toeplitz_kernel, sets),
         shape((block, length), BF16),
         moved=block * length * 2,
         flops=block * length * 8,
+        vmem=8 if not gridded else 56,
     )(filter_taps.T)
     skip = lax.dynamic_slice_in_dim(skip_gain, lax.axis_index("seq") * channels, channels)
-    mixed, squares = call(
+
+    mixed, back, own_keys = call(
         conv_kernel,
-        (
+        [
             shape((seq_count, channels, block), BF16),
-            shape((everyone, seq_count, block), BF16),
-        ),
-        moved=split.size * 6,
+            shape((seq_count, channels + 2 * seq_count, block), BF16),
+            shape((seq_count, rows, head_dim), BF16),
+        ],
+        moved=signal.size * 10,
         flops=length * length * channels,
+        vmem=8 if not gridded else 56,
         scratch_shapes=[pltpu.VMEM((seq_count * channels, block), F32)],
-    )(split_got, matrix, skip[:, None])
-
-    squares_got = lax.all_to_all(squares, ("seq", "chan"), 0, 0, tiled=True)
-    mixed_others = [set_neighbour(mixed, offset) for offset in range(1, sets)]
-    mixed_home = lax.all_to_all(mixed, "seq", 0, 0, tiled=True)
-
-    key_others = [set_neighbour(pack_got[:, 1], offset) for offset in range(1, sets)]
-    weights_shape = (steps, length, QUERY_BLOCK)
+    )(got, matrix, skip[:, None])
+
+    home = lax.all_to_all(back, "seq", 0, 0, tiled=True)
+    key_parts = [own_keys] + [set_neighbour(own_keys, offset) for offset in range(1, sets)]
+    mixed_parts = [mixed] + [set_neighbour(mixed, offset) for offset in range(1, sets)]
+    squares = home[:, channels:].astype(F32).reshape(2 * seq_count, seq_count, block)
+    squares = jnp.sum(squares, axis=0)
+    all_squares = [squares]
+    for offset in range(1, chan_count):
+        pairs = [(source, (source + offset) % chan_count) for source in range(chan_count)]
+        all_squares.append(lax.ppermute(squares, "chan", pairs))
+
     total_shape = (steps, 8, QUERY_BLOCK)
     one = lambda dims: pl.BlockSpec((1,) + dims[1:], lambda step: (step, 0, 0))
     whole = pl.BlockSpec(memory_space=pltpu.VMEM)
-    grid = dict(grid=(steps,), out_specs=(one(weights_shape), one(total_shape)))
-    grid["in_specs"] = [whole] * sets
-    weights, totals = call(
+    if gridded:
+        weights_shapes = [(steps, length, QUERY_BLOCK)]
+        vmem = 56
+        weights_specs = [one(total_shape), one(weights_shapes[0])]
+        weights_grid = dict(grid=(steps,), in_specs=[whole] * (sets + 1), out_specs=weights_specs)
+        output_grid = dict(
+            grid=(steps,),
+            in_specs=[whole] * (chan_count + sets) + weights_specs,
+            out_specs=pl.BlockSpec((QUERY_BLOCK, head_dim), lambda step: (step, 0)),
+        )
+    else:
+        weights_shapes = [(length * step // steps, QUERY_BLOCK) for step in range(1, steps + 1)]
+        vmem = 12
+        weights_grid = output_grid = {}
+    totals, *weights = call(
         functools.partial(weights_kernel, sets, gridded),
-        (shape(weights_shape, BF16), shape(total_shape, F32)),
-        moved=steps * length * QUERY_BLOCK * 2,
+        [shape(total_shape, F32)] + [shape(dims, BF16) for dims in weights_shapes],
+        moved=2 * sum(math.prod(dims) for dims in weights_shapes),
         flops=query_len * length * head_dim,
         exps=query_len * length // 2,
+        vmem=vmem,
         scratch_shapes=[
             pltpu.VMEM((seq_count, sets, rows, head_dim), BF16),
             pltpu.VMEM((query_len, head_dim), BF16),
             pltpu.VMEM((length, QUERY_BLOCK), F32),
         ],
-        **(grid if gridded else {}),
-    )(pack_got, *key_others)
-
-    grid = dict(grid=(steps,), out_specs=pl.BlockSpec((QUERY_BLOCK, head_dim), lambda step: (step, 0)))
-    grid["in_specs"] = [whole, one(weights_shape), one(total_shape)] + [whole] * sets
+        **weights_grid,
+    )(got, *key_parts)
+
     attended = call(
-        functools.partial(output_kernel, sets, local_width * chan_count, gridded),
+        functools.partial(output_kernel, sets, steps, local_width * chan_count, gridded),
         shape((query_len, head_dim), BF16),
-        moved=steps * length * QUERY_BLOCK * 2,
+        moved=2 * sum(math.prod(dims) for dims in weights_shapes),
         flops=query_len * length * head_dim,
+        vmem=vmem,
         scratch_shapes=[
             pltpu.VMEM((sets, channels, length), F32),
             pltpu.VMEM((head_dim, length), BF16),
         ],
-        **(grid if gridded else {}),
-    )(squares_got, weights, totals, mixed, *mixed_others)
-
-    conv_mixed = call(unsplit_kernel, shape((block, local_width), BF16), moved=signal.size * 4)(
-        mixed_home
-    )
+        **output_grid,
+    )(*all_squares, *mixed_parts, totals, *weights)
+
+    conv_mixed = call(unpack_kernel, shape((block, local_width), BF16), moved=signal.size * 4)(home)
     return (conv_mixed, attended[None])
 
 

time: 83.5 us -> 59.9 us (0.72)
  blocking collectives: 12 us -> 0 us
  Pallas kernels: 19 us -> 7.93 us
  waiting for transfers between devices: 31.8 us -> 34.2 us
  local copies, waits for them, and re-layouts: 2.91 us -> 0.81 us
    all_to_all x1 -> x0, blocking collectives: 12 us -> none  [shards(): squares_got = lax.all_to_all(squares, ('seq', 'chan'), 0, 0, tiled=True)]
    all_to_all x3 -> x2, waiting for transfers between devices: 21.9 us -> 33.1 us  [the longest x1 24.7 us: shards(): got = lax.all_to_all(packed, 'seq', 0, 0, tiled=True)]
    pallas_call x6 -> x5, Pallas kernels: 17.1 us -> 7.71 us  [the longest x1 2.31 us: shards(): call(functools.partial(pack_kernel, sets), shape((seq_count, 4, channels,...]
    ppermute x2, waiting for transfers between devices: 9.93 us -> 1.06 us  [set_neighbour(): return lax.ppermute(array, 'seq', pairs)]
    all_to_all x3 -> x2, starting transfers between devices: 14.3 us -> 10.9 us  [the longest x1 7.29 us: shards(): got = lax.all_to_all(packed, 'seq', 0, 0, tiled=True)]
    ppermute x0 -> x3, starting transfers between devices: none -> 3 us  [shards(): all_squares.append(lax.ppermute(squares, 'chan', pairs))]
    pallas_call x1, Pallas kernels: 1.92 us -> 0.22 us  [shards(): call(functools.partial(toeplitz_kernel, sets), shape((block, length), BF1...]
    unnamed x12 -> x4, local copies, waits for them, and re-layouts: 2.12 us -> 0.63 us
  transfers between devices with their start and end apart: 5 -> 7, of which waited for: 3 -> 3; matrix products, arithmetic and copies ran while one was open for 1% -> 0% of each run, Pallas kernels for 18% -> 5%
where the time goes in v2:
time: 59.9 us; the launch traced here: 59.6 us
  waiting for transfers between devices  34.2 us (57%)
  starting transfers between devices  15.9 us (27%)
  Pallas kernels  7.93 us (13%)
  local copies, waits for them, and re-layouts  0.81 us (1%)
  between operations  0.68 us (1%)
    all_to_all x1, waiting for transfers between devices, shards(): got = lax.all_to_all(packed, 'seq', 0, 0, tiled=True)  24.7 us
    all_to_all x1, waiting for transfers between devices, shards(): home = lax.all_to_all(back, 'seq', 0, 0, tiled=True)  8.39 us
    all_to_all x1, starting transfers between devices, shards(): got = lax.all_to_all(packed, 'seq', 0, 0, tiled=True)  7.29 us
    all_to_all x1, starting transfers between devices, shards(): home = lax.all_to_all(back, 'seq', 0, 0, tiled=True)  3.6 us
    ppermute x3, starting transfers between devices, shards(): all_squares.append(lax.ppermute(squares, 'chan', pairs))  3 us
    pallas_call x1, Pallas kernels, shards(): call(functools.partial(pack_kernel, sets), shape((seq_count, 4, channels,...  2.31 us
    ppermute x2, starting transfers between devices, set_neighbour(): return lax.ppermute(array, 'seq', pairs)  2.07 us
    pallas_call x1, Pallas kernels, shards(): call(functools.partial(weights_kernel, sets, gridded), [shape(total_shape...  1.88 us
  transfers between devices with their start and end apart: 7, of which 3 were waited for; matrix products, arithmetic and copies ran while one was open for 0% of the time, Pallas kernels for 5%

profile of v2, /device:TPU:0, one launch (start us, length us, event | category | flops | bytes accessed | tf_op | source)
XLA Modules:
  0.0 59.6 jit_solution(4016513179635113055)
XLA Ops:
  0.6 0.0 copy-start
  0.6 2.3 %shard_map.77 = bf16[8,4,64,256]{3,2,1,0:T(8,128)(2,1)} custom-call(bf16[256,512]{1,0:T(8,128)(2,1)} %refs_0_.1, bf16[256,512]{1,0:T(8,128)(2,1)} %refs_1_.1, bf16[256,512]{1,0:T(8,128)(2,1)} %refs_2_.1, bf16[256,512]{1,0:T(8,128)(2,1)} %refs_3_.1), custom_call_target="tpu_custom_call" | custom-call | bytes 2097152 | tf_op jit(solution)/shard_map/pallas_call | solution.py:263
  3.0 7.3 %all-to-all-start = ((bf16[8,4,64,256]{3,2,1,0:T(8,128)(2,1)}), bf16[8,4,64,256]{3,2,1,0:T(8,128)(2,1)S(1)}, u32[]{:S(2)}, u32[]{:S(2)}) async-start(bf16[8,4,64,256]{3,2,1,0:T(8,128)(2,1)} %shard_map.77), calls=%async_computation | async-start | bytes 2097152 | tf_op jit(solution)/shard_map/all_to_all | solution.py:274
  10.3 0.0 copy-done
  10.3 0.1 dynamic-slice_bitcast_fusion
  10.3 0.0 copy-start.1
  10.3 0.1 copy.8.skip_ref
  10.4 0.6 %copy-done.1 = bf16[2048,4]{0,1:T(4,128)(2,1)S(1)} copy-done((bf16[2048,4]{0,1:T(4,128)(2,1)S(1)}, bf16[2048,4]{0,1:T(4,128)(2,1)}, u32[]{:S(2)}) %copy-start.1) | copy-done | bytes 16408
  11.1 0.2 shard_map.78.matrix_ref
  11.3 24.7 %all-to-all-done.got_ref = bf16[8,4,64,256]{3,2,1,0:T(8,128)(2,1)S(1)} async-done(((bf16[8,4,64,256]{3,2,1,0:T(8,128)(2,1)}), bf16[8,4,64,256]{3,2,1,0:T(8,128)(2,1)S(1)}, u32[]{:S(2)}, u32[]{:S(2)}) %all-to-all-start) | async-done | bytes 1048608 | tf_op jit(solution)/shard_map/all_to_all | solution.py:274
  36.0 1.3 %shard_map.79 = (bf16[8,64,256]{2,1,0:T(8,128)(2,1)S(1)}, bf16[8,80,256]{2,1,0:T(8,128)(2,1)}, bf16[8,128,128]{2,1,0:T(8,128)(2,1)S(1)}) custom-call(bf16[8,4,64,256]{3,2,1,0:T(8,128)(2,1)S(1)} %all-to-all-done.got_ref, bf16[256,2048]{1,0:T(8,128)(2,1)S(1)} %shard_map.78.matrix_ref, f32[64,1]{1,0:T(8,128)S(1)} %copy.8.skip_ref), custom_call_target="tpu_custom_call" | custom-call | flops 268435456 | bytes 1310720 | tf_op jit(solution)/shard_map/pallas_call | solution.py:285
  37.3 3.6 %all-to-all-start.1 = ((bf16[8,80,256]{2,1,0:T(8,128)(2,1)}), bf16[8,80,256]{2,1,0:T(8,128)(2,1)S(1)}, u32[]{:S(2)}, u32[]{:S(2)}) async-start(bf16[8,80,256]{2,1,0:T(8,128)(2,1)} %get-tuple-element.10), calls=%async_computation.1 | async-start | bytes 655360 | tf_op jit(solution)/shard_map/all_to_all | solution.py:298
  40.9 2.0 %collective-permute-start.4 = (bf16[8,128,128]{2,1,0:T(8,128)(2,1)S(1)}, bf16[8,128,128]{2,1,0:T(8,128)(2,1)S(1)}, u32[]{:S(2)}, u32[]{:S(2)}) collective-permute-start(bf16[8,128,128]{2,1,0:T(8,128)(2,1)S(1)} %get-tuple-element.12.refs_0_), channel_id=1, source_target_pairs={{4,0},{0,4},{12,8},{8,12},{20,16},{16,20},{28,24},{24,28},{5,1},{1... | collective-permute-start | bytes 786440 | tf_op jit(solution)/shard_map/ppermute | solution.py:261
  42.9 0.0 collective-permute-start.3
  42.9 8.4 %all-to-all-done.1.got_ref = bf16[8,80,256]{2,1,0:T(8,128)(2,1)S(1)} async-done(((bf16[8,80,256]{2,1,0:T(8,128)(2,1)}), bf16[8,80,256]{2,1,0:T(8,128)(2,1)S(1)}, u32[]{:S(2)}, u32[]{:S(2)}) %all-to-all-start.1) | async-done | bytes 327712 | tf_op jit(solution)/shard_map/all_to_all | solution.py:298
  51.4 0.1 collective-permute-start
  51.4 1.6 %collective-permute-start.1 = (f32[8,256]{1,0:T(8,128)S(1)}, f32[8,256]{1,0:T(8,128)S(1)}, u32[]{:S(2)}, u32[]{:S(2)}) collective-permute-start(f32[8,256]{1,0:T(8,128)S(1)} %convert_reduce_fusion.refs_0_), channel_id=1, source_target_pairs={{0,2},{1,3},{2,0},{3,1},{4,6},{5,7},{6,4},{7,5},{8,10},{9,11},{10,... | collective-permute-start | bytes 24584 | tf_op jit(solution)/shard_map/ppermute | solution.py:306
  53.0 1.4 %collective-permute-start.2 = (f32[8,256]{1,0:T(8,128)S(1)}, f32[8,256]{1,0:T(8,128)S(1)}, u32[]{:S(2)}, u32[]{:S(2)}) collective-permute-start(f32[8,256]{1,0:T(8,128)S(1)} %convert_reduce_fusion.refs_0_), channel_id=1, source_target_pairs={{0,3},{1,0},{2,1},{3,2},{4,7},{5,4},{6,5},{7,6},{8,11},{9,8},{10,9... | collective-permute-start | bytes 24584 | tf_op jit(solution)/shard_map/ppermute | solution.py:306
  54.4 0.0 collective-permute-done.4.refs_1_
  54.4 1.9 %shard_map.81 = (f32[4,8,256]{2,1,0:T(8,128)S(1)}, bf16[512,256]{1,0:T(8,128)(2,1)S(1)}, bf16[1024,256]{1,0:T(8,128)(2,1)S(1)}, bf16[1536,256]{1,0:T(8,128)(2,1)S(1)}, bf16[2048,256]{1,0:T(8,128)(2,1)S(1)}) custom-call(bf16[8,4,64,256]{3,2,1,0:T(8,128)(2,1)S(1)} %all-to-all-done.got_ref, bf16[8,128,128]{2,1,0:T(8,128)(2,1)S(1)} %get-tuple-element.12.refs_0_, ...), custom_call_target="tpu_custom_call" | custom-call | flops 268435456 | bytes 2621440 | tf_op jit(solution)/shard_map/pallas_call | solution.py:325
  56.3 0.8 %shard_map.80 = bf16[256,512]{1,0:T(8,128)(2,1)} custom-call(bf16[8,80,256]{2,1,0:T(8,128)(2,1)S(1)} %all-to-all-done.1.got_ref), custom_call_target="tpu_custom_call" | custom-call | bytes 524288 | tf_op jit(solution)/shard_map/pallas_call | solution.py:353
  57.1 1.1 %collective-permute-done.3.refs_5_ = bf16[8,64,256]{2,1,0:T(8,128)(2,1)S(1)} collective-permute-done((bf16[8,64,256]{2,1,0:T(8,128)(2,1)S(1)}, bf16[8,64,256]{2,1,0:T(8,128)(2,1)S(1)}, u32[]{:S(2)}, u32[]{:S(2)}) %collective-permute-start.3) | collective-permute-done | bytes 262176 | tf_op jit(solution)/shard_map/ppermute | solution.py:261
  58.2 0.0 collective-permute-done.refs_1_
  58.2 0.0 collective-permute-done.1.refs_2_
  58.2 0.0 collective-permute-done.2.refs_3_
  58.2 1.4 %shard_map.82 = bf16[1024,128]{1,0:T(8,128)(2,1)} custom-call(f32[8,256]{1,0:T(8,128)S(1)} %convert_reduce_fusion.refs_0_, f32[8,256]{1,0:T(8,128)S(1)} %collective-permute-done.refs_1_, f32[8,256]{1,0:T(8,128)S(1)} %collective-permute-done.1.refs_2_, f32[8,256]{1,0:T(8,128)S(1)} %collective-permute-done.2.refs_3_, ...), custom_call_target="tpu_custom_call" | custom-call | flops 268435456 | bytes 2621440 | tf_op jit(solution)/shard_map/pallas_call | solution.py:340
  (2 shorter events, 0.0 us)
Async XLA Ops:
  0.6 9.6 %copy-start = (f32[512]{0:T(512)S(1)}, f32[512]{0:T(512)}, u32[]{:S(2)}) copy-start(f32[512]{0:T(512)} %param.8) | copy-start | bytes 6148
  3.0 33.1 %all-to-all-start = ((bf16[8,4,64,256]{3,2,1,0:T(8,128)(2,1)}), bf16[8,4,64,256]{3,2,1,0:T(8,128)(2,1)S(1)}, u32[]{:S(2)}, u32[]{:S(2)}) async-start(bf16[8,4,64,256]{3,2,1,0:T(8,128)(2,1)} %shard_map.77), calls=%async_computation | async-start | bytes 2097152 | tf_op jit(solution)/shard_map/all_to_all | solution.py:274
  10.3 0.7 %copy-start.1 = (bf16[2048,4]{0,1:T(4,128)(2,1)S(1)}, bf16[2048,4]{0,1:T(4,128)(2,1)}, u32[]{:S(2)}) copy-start(bf16[2048,4]{0,1:T(4,128)(2,1)} %param.9) | copy-start | bytes 49156
  37.3 14.1 %all-to-all-start.1 = ((bf16[8,80,256]{2,1,0:T(8,128)(2,1)}), bf16[8,80,256]{2,1,0:T(8,128)(2,1)S(1)}, u32[]{:S(2)}, u32[]{:S(2)}) async-start(bf16[8,80,256]{2,1,0:T(8,128)(2,1)} %get-tuple-element.10), calls=%async_computation.1 | async-start | bytes 655360 | tf_op jit(solution)/shard_map/all_to_all | solution.py:298
  40.9 13.5 %collective-permute-start.4 = (bf16[8,128,128]{2,1,0:T(8,128)(2,1)S(1)}, bf16[8,128,128]{2,1,0:T(8,128)(2,1)S(1)}, u32[]{:S(2)}, u32[]{:S(2)}) collective-permute-start(bf16[8,128,128]{2,1,0:T(8,128)(2,1)S(1)} %get-tuple-element.12.refs_0_), channel_id=1, source_target_pairs={{4,0},{0,4},{12,8},{8,12},{20,16},{16,20},{28,24},{24,28},{5,1},{1... | collective-permute-start | bytes 786440 | tf_op jit(solution)/shard_map/ppermute | solution.py:261
  42.9 15.3 %collective-permute-start.3 = (bf16[8,64,256]{2,1,0:T(8,128)(2,1)S(1)}, bf16[8,64,256]{2,1,0:T(8,128)(2,1)S(1)}, u32[]{:S(2)}, u32[]{:S(2)}) collective-permute-start(bf16[8,64,256]{2,1,0:T(8,128)(2,1)S(1)} %get-tuple-element.11.refs_4_), channel_id=1, source_target_pairs={{4,0},{0,4},{12,8},{8,12},{20,16},{16,20},{28,24},{24,28},{5,1},{1... | collective-permute-start | bytes 786440 | tf_op jit(solution)/shard_map/ppermute | solution.py:261
  51.4 6.8 %collective-permute-start = (f32[8,256]{1,0:T(8,128)S(1)}, f32[8,256]{1,0:T(8,128)S(1)}, u32[]{:S(2)}, u32[]{:S(2)}) collective-permute-start(f32[8,256]{1,0:T(8,128)S(1)} %convert_reduce_fusion.refs_0_), channel_id=1, source_target_pairs={{0,1},{1,2},{2,3},{3,0},{4,5},{5,6},{6,7},{7,4},{8,9},{9,10},{10,1... | collective-permute-start | bytes 24584 | tf_op jit(solution)/shard_map/ppermute | solution.py:306
  51.4 6.7 %collective-permute-start.1 = (f32[8,256]{1,0:T(8,128)S(1)}, f32[8,256]{1,0:T(8,128)S(1)}, u32[]{:S(2)}, u32[]{:S(2)}) collective-permute-start(f32[8,256]{1,0:T(8,128)S(1)} %convert_reduce_fusion.refs_0_), channel_id=1, source_target_pairs={{0,2},{1,3},{2,0},{3,1},{4,6},{5,7},{6,4},{7,5},{8,10},{9,11},{10,... | collective-permute-start | bytes 24584 | tf_op jit(solution)/shard_map/ppermute | solution.py:306
  53.0 5.2 %collective-permute-start.2 = (f32[8,256]{1,0:T(8,128)S(1)}, f32[8,256]{1,0:T(8,128)S(1)}, u32[]{:S(2)}, u32[]{:S(2)}) collective-permute-start(f32[8,256]{1,0:T(8,128)S(1)} %convert_reduce_fusion.refs_0_), channel_id=1, source_target_pairs={{0,3},{1,0},{2,1},{3,2},{4,7},{5,4},{6,5},{7,6},{8,11},{9,8},{10,9... | collective-permute-start | bytes 24584 | tf_op jit(solution)/shard_map/ppermute | solution.py:306

commit v3 on v2

--- a/solution.py
+++ b/solution.py
@@ -39,48 +39,82 @@
     return lax.fori_loop(0, count, body, carry)
 
 
-def pack_kernel(sets, *refs):
-    sources, (sent_ref, held_ref, semaphores) = refs[:4], refs[4:]
+def pack_kernel(signal_ref, gate_ref, sent_ref, held_ref, semaphores):
     count, _, rows, positions = sent_ref.shape
-    head_dim = positions // 2
     copies = [
         pltpu.make_async_copy(source, held_ref.at[slot], semaphores.at[slot])
-        for slot, source in enumerate(sources)
+        for slot, source in enumerate((signal_ref, gate_ref))
     ]
     for copy in copies:
         copy.start()
-    for slot in (0, 1):
-        copies[slot].wait()
+    for slot, copy in enumerate(copies):
+        copy.wait()
         turned = held_ref[slot].astype(F32).T
         sent_ref[:, slot] = turned.reshape(count, rows, positions).astype(BF16)
-    for slot in (2, 3):
-        copies[slot].wait()
-        for device in range(count):
-            head, part = divmod(device, sets)
-            first = part * 2 * rows
-            lanes = slice(head * head_dim, (head + 1) * head_dim)
-            sent_ref[device, slot] = side_by_side(held_ref[slot, first : first + 2 * rows, lanes])
-
-
-def side_by_side(piece):
-    rows = piece.shape[0] // 2
-    if rows % 16:
-        return side_by_side32(piece.astype(F32)).astype(BF16)
-    return side_by_side32(piece)
-
-
-def side_by_side32(piece):
-    rows = piece.shape[0] // 2
-    return jnp.concatenate([piece[:rows], piece[rows:]], axis=1)
-
-
-def one_below_other(wide):
-    columns = wide.shape[2] // 2
-    if wide.shape[1] % 16:
-        return one_below_other(wide.astype(F32)).astype(BF16) if wide.dtype == BF16 else (
-            jnp.concatenate([wide[:, :, :columns], wide[:, :, columns:]], axis=1)
+
+
+def heads_kernel(sets, query_ref, key_ref, *refs):
+    pieces, semaphores = refs[:-1], refs[-1]
+    head_dim = pieces[0].shape[2]
+    mine = lax.axis_index("seq") // sets
+    copies = []
+    for offset, piece in enumerate(pieces):
+        head = lax.rem(mine + offset, len(pieces))
+        lanes = pl.ds(pl.multiple_of(head * head_dim, head_dim), head_dim)
+        for slot, source in enumerate((query_ref, key_ref)):
+            copies.append(
+                pltpu.make_async_copy(
+                    source.at[:, lanes], piece.at[slot], semaphores.at[offset, slot]
+                )
+            )
+    for copy in copies:
+        copy.start()
+    for copy in copies:
+        copy.wait()
+
+
+def sets_kernel(sets, *refs):
+    blocks = len(refs) - 2 - sets
+    sources, keys_ref, queries_refs, semaphores = refs[:blocks], refs[blocks], refs[blocks + 1 : -1], refs[-1]
+    rows = queries_refs[0].shape[1]
+    mine = lax.rem(lax.axis_index("seq"), sets)
+    copies = []
+    for block, source in enumerate(sources):
+        copies.append(
+            pltpu.make_async_copy(source.at[1], keys_ref.at[block], semaphores.at[block, sets])
         )
-    return jnp.concatenate([wide[:, :, :columns], wide[:, :, columns:]], axis=1)
+        for offset, queries_ref in enumerate(queries_refs):
+            part = lax.rem(mine + offset, sets)
+            span = pl.ds(pl.multiple_of(part * rows, rows), rows)
+            copies.append(
+                pltpu.make_async_copy(
+                    source.at[0, span], queries_ref.at[block], semaphores.at[block, offset]
+                )
+            )
+    for copy in copies:
+        copy.start()
+    for copy in copies:
+        copy.wait()
+
+
+def arrange_kernel(sets, *refs):
+    parts, (keys_ref, queries_ref, semaphores) = refs[: 2 * sets], refs[2 * sets :]
+    heads = parts[0].shape[0]
+    me = lax.axis_index("seq")
+    copies = []
+    for number, part in enumerate(parts):
+        offset, arranged_ref = number % sets, (keys_ref, queries_ref)[number // sets]
+        for index in range(heads):
+            source = lax.rem(me // sets + heads - index, heads) * sets + lax.rem(me + offset, sets)
+            copies.append(
+                pltpu.make_async_copy(
+                    part.at[index], arranged_ref.at[source], semaphores.at[number, index]
+                )
+            )
+    for copy in copies:
+        copy.start()
+    for copy in copies:
+        copy.wait()
 
 
 def unpack_kernel(got_ref, out_ref):
@@ -103,7 +137,7 @@
     matrix_ref[:, block:] = rolled[:, block:].astype(BF16)
 
 
-def conv_kernel(got_ref, matrix_ref, skip_ref, mixed_ref, back_ref, key_ref, total_ref):
+def conv_kernel(got_ref, matrix_ref, skip_ref, mixed_ref, back_ref, total_ref):
     count, _, rows, block = got_ref.shape
     inputs = merge_rows(got_ref[:, 0])
     for lag in range(count):
@@ -131,7 +165,6 @@
     both = jnp.concatenate([high, squares - high], axis=0).astype(BF16)
     for index in range(count):
         back_ref[index, rows:] = both
-    key_ref[...] = one_below_other(got_ref[:, 3])
 
 
 def weights_block(step, last, key_ref, query, sets, rows, scores_ref, weights_ref, total_ref):
@@ -168,31 +201,23 @@
     total_ref[...] = jnp.broadcast_to(total, total_ref.shape)
 
 
-def weights_kernel(sets, gridded, got_ref, *refs):
-    parts, (key_ref, query_ref, scores_ref) = refs[:sets], refs[-3:]
-    total_ref, weights_refs = refs[sets], refs[sets + 1 : -3]
-    count, _, rows, head_dim = key_ref.shape
-    mine = lax.rem(lax.axis_index("seq"), sets)
-
-    def assemble():
-        query_ref[...] = merge_rows(one_below_other(got_ref[:, 2]))
-        for offset in range(sets):
-            place = lax.rem(mine + offset, sets)
-            key_ref[:, pl.ds(place, 1)] = parts[offset][...][:, None]
-
-    steps = query_ref.shape[0] // QUERY_BLOCK
-    keys = key_ref.reshape(count * sets * rows, head_dim)
+def weights_kernel(gridded, key_ref, query_ref, total_ref, *refs):
+    weights_refs, scores_ref = refs[:-1], refs[-1]
+    count, positions, head_dim = key_ref.shape
+    rows = query_ref.shape[1]
+    sets = positions // rows
+    steps = count * rows // QUERY_BLOCK
+    keys = key_ref.reshape(count * positions, head_dim)
 
     def block(step, weights, total):
-        query = query_ref[step * QUERY_BLOCK : (step + 1) * QUERY_BLOCK]
+        each = QUERY_BLOCK // rows
+        query = merge_rows(query_ref[step * each : (step + 1) * each])
         weights_block(step, steps - 1, keys, query, sets, rows, scores_ref, weights, total)
 
     if not gridded:
-        assemble()
         for step in range(steps):
             block(step, weights_refs[step], total_ref.at[step])
         return
-    pl.when(pl.program_id(0) == 0)(assemble)
     for step in range(steps):
         pl.when(pl.program_id(0) == step)(
             functools.partial(block, step, weights_refs[0].at[0], total_ref.at[0])
@@ -253,25 +278,48 @@
     gridded = length > 4096
     shape = jax.ShapeDtypeStruct
 
-    def set_neighbour(array, offset):
+    def from_set(array, offset):
         pairs = []
         for head in range(heads_loc):
             for part in range(sets):
                 pairs.append((head * sets + (part + offset) % sets, head * sets + part))
         return lax.ppermute(array, "seq", pairs)
 
+    def from_head(array, offset):
+        pairs = [(source, (source + offset * sets) % seq_count) for source in range(seq_count)]
+        return lax.ppermute(array, "seq", pairs)
+
+    anywhere = pl.BlockSpec(memory_space=pl.ANY)
     packed = call(
-        functools.partial(pack_kernel, sets),
-        shape((seq_count, 4, channels, block), BF16),
-        moved=16 * signal.size,
-        in_specs=[pl.BlockSpec(memory_space=pl.ANY)] * 4,
+        pack_kernel,
+        shape((seq_count, 2, channels, block), BF16),
+        moved=8 * signal.size,
+        in_specs=[anywhere] * 2,
         vmem=56,
-        scratch_shapes=[
-            pltpu.VMEM((4,) + signal.shape, BF16),
-            pltpu.SemaphoreType.DMA((4,)),
-        ],
-    )(signal, gate_rows, queries, key_rows)
+        scratch_shapes=[pltpu.VMEM((2,) + signal.shape, BF16), pltpu.SemaphoreType.DMA((2,))],
+    )(signal, gate_rows)
     got = lax.all_to_all(packed, "seq", 0, 0, tiled=True)
+
+    pieces = call(
+        functools.partial(heads_kernel, sets),
+        [shape((2, block, head_dim), BF16)] * heads_loc,
+        moved=8 * signal.size,
+        in_specs=[anywhere] * 2,
+        out_specs=[anywhere] * heads_loc,
+        scratch_shapes=[pltpu.SemaphoreType.DMA((heads_loc, 2))],
+    )(queries, key_rows)
+    pieces = [pieces[0]] + [from_head(pieces[k], k) for k in range(1, heads_loc)]
+    own_keys, *set_queries = call(
+        functools.partial(sets_kernel, sets),
+        [shape((heads_loc, block, head_dim), BF16)] + [shape((heads_loc, rows, head_dim), BF16)] * sets,
+        moved=8 * signal.size,
+        flops=4 * 10**10,
+        in_specs=[anywhere] * heads_loc,
+        out_specs=[anywhere] * (sets + 1),
+        scratch_shapes=[pltpu.SemaphoreType.DMA((heads_loc, sets + 1))],
+    )(*pieces)
+    key_parts = [own_keys] + [from_set(own_keys, k) for k in range(1, sets)]
+    query_parts = [set_queries[0]] + [from_set(set_queries[-k], k) for k in range(1, sets)]
 
     matrix = call(
         functools.partial(toeplitz_kernel, sets),
@@ -282,12 +330,12 @@
     )(filter_taps.T)
     skip = lax.dynamic_slice_in_dim(skip_gain, lax.axis_index("seq") * channels, channels)
 
-    mixed, back, own_keys = call(
+    whole = pl.BlockSpec(memory_space=pltpu.VMEM)
+    mixed, back = call(
         conv_kernel,
         [
             shape((seq_count, channels, block), BF16),
             shape((seq_count, channels + 2 * seq_count, block), BF16),
-            shape((seq_count, rows, head_dim), BF16),
         ],
         moved=signal.size * 10,
         flops=length * length * channels,
@@ -296,8 +344,7 @@
     )(got, matrix, skip[:, None])
 
     home = lax.all_to_all(back, "seq", 0, 0, tiled=True)
-    key_parts = [own_keys] + [set_neighbour(own_keys, offset) for offset in range(1, sets)]
-    mixed_parts = [mixed] + [set_neighbour(mixed, offset) for offset in range(1, sets)]
+    mixed_parts = [mixed] + [from_set(mixed, offset) for offset in range(1, sets)]
     squares = home[:, channels:].astype(F32).reshape(2 * seq_count, seq_count, block)
     squares = jnp.sum(squares, axis=0)
     all_squares = [squares]
@@ -312,7 +359,7 @@
         weights_shapes = [(steps, length, QUERY_BLOCK)]
         vmem = 56
         weights_specs = [one(total_shape), one(weights_shapes[0])]
-        weights_grid = dict(grid=(steps,), in_specs=[whole] * (sets + 1), out_specs=weights_specs)
+        weights_grid = dict(grid=(steps,), in_specs=[whole] * 2, out_specs=weights_specs)
         output_grid = dict(
             grid=(steps,),
             in_specs=[whole] * (chan_count + sets) + weights_specs,
@@ -322,20 +369,27 @@
         weights_shapes = [(length * step // steps, QUERY_BLOCK) for step in range(1, steps + 1)]
         vmem = 12
         weights_grid = output_grid = {}
+    keys, arranged = call(
+        functools.partial(arrange_kernel, sets),
+        [shape((seq_count, block, head_dim), BF16), shape((seq_count, rows, head_dim), BF16)],
+        moved=6 * length * head_dim,
+        flops=4 * 10**10,
+        in_specs=[anywhere] * (2 * sets),
+        out_specs=[anywhere] * 2,
+        scratch_shapes=[pltpu.SemaphoreType.DMA((2 * sets, heads_loc))],
+    )(*key_parts, *query_parts)
     totals, *weights = call(
-        functools.partial(weights_kernel, sets, gridded),
+        functools.partial(weights_kernel, gridded),
         [shape(total_shape, F32)] + [shape(dims, BF16) for dims in weights_shapes],
         moved=2 * sum(math.prod(dims) for dims in weights_shapes),
         flops=query_len * length * head_dim,
         exps=query_len * length // 2,
         vmem=vmem,
         scratch_shapes=[
-            pltpu.VMEM((seq_count, sets, rows, head_dim), BF16),
-            pltpu.VMEM((query_len, head_dim), BF16),
             pltpu.VMEM((length, QUERY_BLOCK), F32),
         ],
         **weights_grid,
-    )(got, *key_parts)
+    )(keys, arranged)
 
     attended = call(
         functools.partial(output_kernel, sets, steps, local_width * chan_count, gridded),

time: 59.9 us -> 52.9 us (0.88)
  waiting for transfers between devices: 34.2 us -> 19.1 us
  starting transfers between devices: 15.9 us -> 20.2 us
  local copies, waits for them, and re-layouts: 0.81 us -> 2.7 us
  Pallas kernels: 7.93 us -> 9.75 us
    all_to_all x1, waiting for transfers between devices: 24.7 us -> 10.1 us  [shards(): got = lax.all_to_all(packed, 'seq', 0, 0, tiled=True)]
    ppermute x2 -> x6, starting transfers between devices: 2.07 us -> 11.1 us  [the longest x3 7.01 us: from_head(): return lax.ppermute(array, 'seq', pairs)]
    all_to_all x1, starting transfers between devices: 7.29 us -> 3.5 us  [shards(): got = lax.all_to_all(packed, 'seq', 0, 0, tiled=True)]
    unnamed x4 -> x8, local copies, waits for them, and re-layouts: 0.63 us -> 2.53 us
    pallas_call x2 -> x5, Pallas kernels: 4.19 us -> 6.03 us  [the longest x1 2.04 us: shards(): call(pack_kernel, shape((seq_count, 2, channels, block), BF16), moved=8 *...]
    all_to_all x1, waiting for transfers between devices: 8.39 us -> 7.06 us  [shards(): home = lax.all_to_all(back, 'seq', 0, 0, tiled=True)]
    ppermute x3, starting transfers between devices: 3 us -> 1.78 us  [shards(): all_squares.append(lax.ppermute(squares, 'chan', pairs))]
    ppermute x2 -> x6, waiting for transfers between devices: 1.06 us -> 1.74 us  [the longest x3 1.73 us: from_head(): return lax.ppermute(array, 'seq', pairs)]
  transfers between devices with their start and end apart: 7 -> 11, of which waited for: 3 -> 4; matrix products, arithmetic and copies ran while one was open for 0% -> 0% of each run, Pallas kernels for 5% -> 16%
where the time goes in v3:
time: 52.9 us; the launch traced here: 52.5 us
  starting transfers between devices  20.2 us (38%)
  waiting for transfers between devices  19.1 us (36%)
  Pallas kernels  9.75 us (18%)
  local copies, waits for them, and re-layouts  2.7 us (5%)
  between operations  0.73 us (1%)
    all_to_all x1, waiting for transfers between devices, shards(): got = lax.all_to_all(packed, 'seq', 0, 0, tiled=True)  10.1 us
    all_to_all x1, waiting for transfers between devices, shards(): home = lax.all_to_all(back, 'seq', 0, 0, tiled=True)  7.06 us
    ppermute x3, starting transfers between devices, from_head(): return lax.ppermute(array, 'seq', pairs)  7.01 us
    ppermute x3, starting transfers between devices, from_set(): return lax.ppermute(array, 'seq', pairs)  4.11 us
    all_to_all x1, starting transfers between devices, shards(): home = lax.all_to_all(back, 'seq', 0, 0, tiled=True)  3.81 us
    all_to_all x1, starting transfers between devices, shards(): got = lax.all_to_all(packed, 'seq', 0, 0, tiled=True)  3.5 us
    unnamed x8, local copies, waits for them, and re-layouts  2.53 us
    pallas_call x1, Pallas kernels, shards(): call(pack_kernel, shape((seq_count, 2, channels, block), BF16), moved=8 *...  2.04 us
  transfers between devices with their start and end apart: 11, of which 4 were waited for; matrix products, arithmetic and copies ran while one was open for 0% of the time, Pallas kernels for 16%

profile of v3, /device:TPU:0, one launch (start us, length us, event | category | flops | bytes accessed | tf_op | source)
XLA Modules:
  0.0 52.5 jit_solution(13810019427789119914)
XLA Ops:
  0.6 0.0 copy-start
  0.6 0.0 copy-start.1
  0.7 0.9 %copy-done.1 = bf16[256,512]{1,0:T(8,128)(2,1)S(1)} copy-done((bf16[256,512]{1,0:T(8,128)(2,1)S(1)}, bf16[256,512]{1,0:T(8,128)(2,1)}, u32[]{:S(2)}) %copy-start.1) | copy-done | bytes 262168
  1.6 0.0 copy-start.2
  1.6 0.9 %copy-done.2 = bf16[256,512]{1,0:T(8,128)(2,1)S(1)} copy-done((bf16[256,512]{1,0:T(8,128)(2,1)S(1)}, bf16[256,512]{1,0:T(8,128)(2,1)}, u32[]{:S(2)}) %copy-start.2) | copy-done | bytes 262168
  2.6 0.2 shard_map.81
  2.7 3.1 %collective-permute-start.4 = (bf16[2,256,128]{2,1,0:T(8,128)(2,1)S(1)}, bf16[2,256,128]{2,1,0:T(8,128)(2,1)S(1)}, u32[]{:S(2)}, u32[]{:S(2)}) collective-permute-start(bf16[2,256,128]{2,1,0:T(8,128)(2,1)S(1)} %get-tuple-element.21), channel_id=1, source_target_pairs={{0,8},{4,12},{8,16},{12,20},{16,24},{20,28},{24,0},{28,4},{1,9},{5... | collective-permute-start | bytes 393224 | tf_op jit(solution)/shard_map/ppermute | solution.py:290
  5.8 2.6 %collective-permute-start.5 = (bf16[2,256,128]{2,1,0:T(8,128)(2,1)S(1)}, bf16[2,256,128]{2,1,0:T(8,128)(2,1)S(1)}, u32[]{:S(2)}, u32[]{:S(2)}) collective-permute-start(bf16[2,256,128]{2,1,0:T(8,128)(2,1)S(1)} %get-tuple-element.22), channel_id=1, source_target_pairs={{0,16},{4,20},{8,24},{12,28},{16,0},{20,4},{24,8},{28,12},{1,17},{... | collective-permute-start | bytes 393224 | tf_op jit(solution)/shard_map/ppermute | solution.py:290
  8.4 1.3 %collective-permute-start.6 = (bf16[2,256,128]{2,1,0:T(8,128)(2,1)S(1)}, bf16[2,256,128]{2,1,0:T(8,128)(2,1)S(1)}, u32[]{:S(2)}, u32[]{:S(2)}) collective-permute-start(bf16[2,256,128]{2,1,0:T(8,128)(2,1)S(1)} %get-tuple-element.23), channel_id=1, source_target_pairs={{0,24},{4,28},{8,0},{12,4},{16,8},{20,12},{24,16},{28,20},{1,25},{... | collective-permute-start | bytes 393224 | tf_op jit(solution)/shard_map/ppermute | solution.py:290
  9.8 2.0 %shard_map.77 = bf16[8,2,64,256]{3,2,1,0:T(8,128)(2,1)} custom-call(bf16[256,512]{1,0:T(8,128)(2,1)} %signal_ref.1, bf16[256,512]{1,0:T(8,128)(2,1)} %gate_ref.1), custom_call_target="tpu_custom_call" | custom-call | bytes 1048576 | tf_op jit(solution)/shard_map/pallas_call | solution.py:293
  11.8 3.5 %all-to-all-start = ((bf16[8,2,64,256]{3,2,1,0:T(8,128)(2,1)}), bf16[8,2,64,256]{3,2,1,0:T(8,128)(2,1)S(1)}, u32[]{:S(2)}, u32[]{:S(2)}) async-start(bf16[8,2,64,256]{3,2,1,0:T(8,128)(2,1)} %shard_map.77), calls=%async_computation | async-start | bytes 1048576 | tf_op jit(solution)/shard_map/all_to_all | solution.py:301
  15.3 0.0 collective-permute-done.4.refs_1_
  15.3 1.7 %collective-permute-done.5.refs_2_ = bf16[2,256,128]{2,1,0:T(8,128)(2,1)S(1)} collective-permute-done((bf16[2,256,128]{2,1,0:T(8,128)(2,1)S(1)}, bf16[2,256,128]{2,1,0:T(8,128)(2,1)S(1)}, u32[]{:S(2)}, u32[]{:S(2)}) %collective-permute-start.5) | collective-permute-done | bytes 131104 | tf_op jit(solution)/shard_map/ppermute | solution.py:290
  17.1 0.0 collective-permute-done.6.refs_3_
  17.1 0.8 %shard_map.82 = (bf16[4,256,128]{2,1,0:T(8,128)(2,1)S(1)}, bf16[4,128,128]{2,1,0:T(8,128)(2,1)S(1)}, bf16[4,128,128]{2,1,0:T(8,128)(2,1)S(1)}) custom-call(bf16[2,256,128]{2,1,0:T(8,128)(2,1)S(1)} %get-tuple-element.20.refs_0_, bf16[2,256,128]{2,1,0:T(8,128)(2,1)S(1)} %collective-permute-done.4.refs_1_, ...), custom_call_target="tpu_custom_call" | custom-call | flops 40000000000 | bytes 1048576 | tf_op jit(solution)/shard_map/pallas_call | solution.py:312
  17.9 1.6 %collective-permute-start.7 = (bf16[4,256,128]{2,1,0:T(8,128)(2,1)S(1)}, bf16[4,256,128]{2,1,0:T(8,128)(2,1)S(1)}, u32[]{:S(2)}, u32[]{:S(2)}) collective-permute-start(bf16[4,256,128]{2,1,0:T(8,128)(2,1)S(1)} %get-tuple-element.24.refs_0_), channel_id=1, source_target_pairs={{4,0},{0,4},{12,8},{8,12},{20,16},{16,20},{28,24},{24,28},{5,1},{1... | collective-permute-start | bytes 786440 | tf_op jit(solution)/shard_map/ppermute | solution.py:286
  19.4 0.5 collective-permute-start.8
  19.9 0.0 copy-done
  19.9 0.1 dynamic-slice_bitcast_fusion
  20.0 0.0 copy-start.3
  20.0 0.1 copy.8.skip_ref
  20.1 0.6 %copy-done.3 = bf16[2048,4]{0,1:T(4,128)(2,1)S(1)} copy-done((bf16[2048,4]{0,1:T(4,128)(2,1)S(1)}, bf16[2048,4]{0,1:T(4,128)(2,1)}, u32[]{:S(2)}) %copy-start.3) | copy-done | bytes 16408
  20.7 0.2 shard_map.78.matrix_ref
  21.0 10.1 %all-to-all-done.got_ref = bf16[8,2,64,256]{3,2,1,0:T(8,128)(2,1)S(1)} async-done(((bf16[8,2,64,256]{3,2,1,0:T(8,128)(2,1)}), bf16[8,2,64,256]{3,2,1,0:T(8,128)(2,1)S(1)}, u32[]{:S(2)}, u32[]{:S(2)}) %all-to-all-start) | async-done | bytes 524320 | tf_op jit(solution)/shard_map/all_to_all | solution.py:301
  31.1 1.2 %shard_map.79 = (bf16[8,64,256]{2,1,0:T(8,128)(2,1)S(1)}, bf16[8,80,256]{2,1,0:T(8,128)(2,1)}) custom-call(bf16[8,2,64,256]{3,2,1,0:T(8,128)(2,1)S(1)} %all-to-all-done.got_ref, bf16[256,2048]{1,0:T(8,128)(2,1)S(1)} %shard_map.78.matrix_ref, f32[64,1]{1,0:T(8,128)S(1)} %copy.8.skip_ref), custom_call_target="tpu_custom_call" | custom-call | flops 268435456 | bytes 1310720 | tf_op jit(solution)/shard_map/pallas_call | solution.py:334
  32.3 3.8 %all-to-all-start.1 = ((bf16[8,80,256]{2,1,0:T(8,128)(2,1)}), bf16[8,80,256]{2,1,0:T(8,128)(2,1)S(1)}, u32[]{:S(2)}, u32[]{:S(2)}) async-start(bf16[8,80,256]{2,1,0:T(8,128)(2,1)} %get-tuple-element.18), calls=%async_computation.1 | async-start | bytes 655360 | tf_op jit(solution)/shard_map/all_to_all | solution.py:346
  36.1 2.0 %collective-permute-start.3 = (bf16[8,64,256]{2,1,0:T(8,128)(2,1)S(1)}, bf16[8,64,256]{2,1,0:T(8,128)(2,1)S(1)}, u32[]{:S(2)}, u32[]{:S(2)}) collective-permute-start(bf16[8,64,256]{2,1,0:T(8,128)(2,1)S(1)} %get-tuple-element.19.refs_4_), channel_id=1, source_target_pairs={{4,0},{0,4},{12,8},{8,12},{20,16},{16,20},{28,24},{24,28},{5,1},{1... | collective-permute-start | bytes 786440 | tf_op jit(solution)/shard_map/ppermute | solution.py:286
  38.1 0.0 collective-permute-done.8.refs_3_
  38.1 0.0 collective-permute-done.7.refs_1_
  38.1 1.2 %shard_map.83 = (bf16[8,256,128]{2,1,0:T(8,128)(2,1)S(1)}, bf16[8,128,128]{2,1,0:T(8,128)(2,1)S(1)}) custom-call(bf16[4,256,128]{2,1,0:T(8,128)(2,1)S(1)} %get-tuple-element.24.refs_0_, bf16[4,256,128]{2,1,0:T(8,128)(2,1)S(1)} %collective-permute-done.7.refs_1_, bf16[4,128,128]{2,1,0:T(8,128)(2,1)S(1)} %get-tuple-element.25.refs_2_, ...), custom_call_target="tpu_custom_call" | custom-call | flops 40000000000 | bytes 1572864 | tf_op jit(solution)/shard_map/pallas_call | solution.py:372
  39.3 7.1 %all-to-all-done.1.got_ref = bf16[8,80,256]{2,1,0:T(8,128)(2,1)S(1)} async-done(((bf16[8,80,256]{2,1,0:T(8,128)(2,1)}), bf16[8,80,256]{2,1,0:T(8,128)(2,1)S(1)}, u32[]{:S(2)}, u32[]{:S(2)}) %all-to-all-start.1) | async-done | bytes 327712 | tf_op jit(solution)/shard_map/all_to_all | solution.py:346
  46.4 0.1 collective-permute-start.2
  46.5 1.6 %collective-permute-start.1 = (f32[8,256]{1,0:T(8,128)S(1)}, f32[8,256]{1,0:T(8,128)S(1)}, u32[]{:S(2)}, u32[]{:S(2)}) collective-permute-start(f32[8,256]{1,0:T(8,128)S(1)} %convert_reduce_fusion.refs_0_), channel_id=1, source_target_pairs={{0,2},{1,3},{2,0},{3,1},{4,6},{5,7},{6,4},{7,5},{8,10},{9,11},{10,... | collective-permute-start | bytes 24584 | tf_op jit(solution)/shard_map/ppermute | solution.py:353
  48.0 0.2 collective-permute-start
  48.2 1.8 %shard_map.84 = (f32[4,8,256]{2,1,0:T(8,128)S(1)}, bf16[512,256]{1,0:T(8,128)(2,1)S(1)}, bf16[1024,256]{1,0:T(8,128)(2,1)S(1)}, bf16[1536,256]{1,0:T(8,128)(2,1)S(1)}, bf16[2048,256]{1,0:T(8,128)(2,1)S(1)}) custom-call(bf16[8,256,128]{2,1,0:T(8,128)(2,1)S(1)} %get-tuple-element.27.key_ref, bf16[8,128,128]{2,1,0:T(8,128)(2,1)S(1)} %get-tuple-element.28.query_ref), custom_call_target="tpu_custom_call" | custom-call | flops 268435456 | bytes 2621440 | tf_op jit(solution)/shard_map/pallas_call | solution.py:381
  50.0 0.8 %shard_map.80 = bf16[256,512]{1,0:T(8,128)(2,1)} custom-call(bf16[8,80,256]{2,1,0:T(8,128)(2,1)S(1)} %all-to-all-done.1.got_ref), custom_call_target="tpu_custom_call" | custom-call | bytes 524288 | tf_op jit(solution)/shard_map/pallas_call | solution.py:407
  50.9 0.0 collective-permute-done.3.refs_5_
  50.9 0.0 collective-permute-done.2.refs_3_
  50.9 0.0 collective-permute-done.1.refs_2_
  50.9 0.2 collective-permute-done.refs_1_
  51.1 1.4 %shard_map.85 = bf16[1024,128]{1,0:T(8,128)(2,1)} custom-call(f32[8,256]{1,0:T(8,128)S(1)} %convert_reduce_fusion.refs_0_, f32[8,256]{1,0:T(8,128)S(1)} %collective-permute-done.refs_1_, f32[8,256]{1,0:T(8,128)S(1)} %collective-permute-done.1.refs_2_, f32[8,256]{1,0:T(8,128)S(1)} %collective-permute-done.2.refs_3_, ...), custom_call_target="tpu_custom_call" | custom-call | flops 268435456 | bytes 2621440 | tf_op jit(solution)/shard_map/pallas_call | solution.py:394
  (2 shorter events, 0.0 us)
Async XLA Ops:
  0.6 19.3 %copy-start = (f32[512]{0:T(512)S(1)}, f32[512]{0:T(512)}, u32[]{:S(2)}) copy-start(f32[512]{0:T(512)} %param.8) | copy-start | bytes 6148
  0.6 1.0 %copy-start.1 = (bf16[256,512]{1,0:T(8,128)(2,1)S(1)}, bf16[256,512]{1,0:T(8,128)(2,1)}, u32[]{:S(2)}) copy-start(bf16[256,512]{1,0:T(8,128)(2,1)} %query_ref.1) | copy-start | bytes 786436
  1.6 0.9 %copy-start.2 = (bf16[256,512]{1,0:T(8,128)(2,1)S(1)}, bf16[256,512]{1,0:T(8,128)(2,1)}, u32[]{:S(2)}) copy-start(bf16[256,512]{1,0:T(8,128)(2,1)} %key_ref.1) | copy-start | bytes 786436
  2.7 12.6 %collective-permute-start.4 = (bf16[2,256,128]{2,1,0:T(8,128)(2,1)S(1)}, bf16[2,256,128]{2,1,0:T(8,128)(2,1)S(1)}, u32[]{:S(2)}, u32[]{:S(2)}) collective-permute-start(bf16[2,256,128]{2,1,0:T(8,128)(2,1)S(1)} %get-tuple-element.21), channel_id=1, source_target_pairs={{0,8},{4,12},{8,16},{12,20},{16,24},{20,28},{24,0},{28,4},{1,9},{5... | collective-permute-start | bytes 393224 | tf_op jit(solution)/shard_map/ppermute | solution.py:290
  5.8 11.2 %collective-permute-start.5 = (bf16[2,256,128]{2,1,0:T(8,128)(2,1)S(1)}, bf16[2,256,128]{2,1,0:T(8,128)(2,1)S(1)}, u32[]{:S(2)}, u32[]{:S(2)}) collective-permute-start(bf16[2,256,128]{2,1,0:T(8,128)(2,1)S(1)} %get-tuple-element.22), channel_id=1, source_target_pairs={{0,16},{4,20},{8,24},{12,28},{16,0},{20,4},{24,8},{28,12},{1,17},{... | collective-permute-start | bytes 393224 | tf_op jit(solution)/shard_map/ppermute | solution.py:290
  8.4 8.6 %collective-permute-start.6 = (bf16[2,256,128]{2,1,0:T(8,128)(2,1)S(1)}, bf16[2,256,128]{2,1,0:T(8,128)(2,1)S(1)}, u32[]{:S(2)}, u32[]{:S(2)}) collective-permute-start(bf16[2,256,128]{2,1,0:T(8,128)(2,1)S(1)} %get-tuple-element.23), channel_id=1, source_target_pairs={{0,24},{4,28},{8,0},{12,4},{16,8},{20,12},{24,16},{28,20},{1,25},{... | collective-permute-start | bytes 393224 | tf_op jit(solution)/shard_map/ppermute | solution.py:290
  11.8 19.2 %all-to-all-start = ((bf16[8,2,64,256]{3,2,1,0:T(8,128)(2,1)}), bf16[8,2,64,256]{3,2,1,0:T(8,128)(2,1)S(1)}, u32[]{:S(2)}, u32[]{:S(2)}) async-start(bf16[8,2,64,256]{3,2,1,0:T(8,128)(2,1)} %shard_map.77), calls=%async_computation | async-start | bytes 1048576 | tf_op jit(solution)/shard_map/all_to_all | solution.py:301
  17.9 20.3 %collective-permute-start.7 = (bf16[4,256,128]{2,1,0:T(8,128)(2,1)S(1)}, bf16[4,256,128]{2,1,0:T(8,128)(2,1)S(1)}, u32[]{:S(2)}, u32[]{:S(2)}) collective-permute-start(bf16[4,256,128]{2,1,0:T(8,128)(2,1)S(1)} %get-tuple-element.24.refs_0_), channel_id=1, source_target_pairs={{4,0},{0,4},{12,8},{8,12},{20,16},{16,20},{28,24},{24,28},{5,1},{1... | collective-permute-start | bytes 786440 | tf_op jit(solution)/shard_map/ppermute | solution.py:286
  19.4 18.7 %collective-permute-start.8 = (bf16[4,128,128]{2,1,0:T(8,128)(2,1)S(1)}, bf16[4,128,128]{2,1,0:T(8,128)(2,1)S(1)}, u32[]{:S(2)}, u32[]{:S(2)}) collective-permute-start(bf16[4,128,128]{2,1,0:T(8,128)(2,1)S(1)} %get-tuple-element.26), channel_id=1, source_target_pairs={{4,0},{0,4},{12,8},{8,12},{20,16},{16,20},{28,24},{24,28},{5,1},{1... | collective-permute-start | bytes 393224 | tf_op jit(solution)/shard_map/ppermute | solution.py:286
  20.0 0.7 %copy-start.3 = (bf16[2048,4]{0,1:T(4,128)(2,1)S(1)}, bf16[2048,4]{0,1:T(4,128)(2,1)}, u32[]{:S(2)}) copy-start(bf16[2048,4]{0,1:T(4,128)(2,1)} %param.9) | copy-start | bytes 49156
  32.3 14.1 %all-to-all-start.1 = ((bf16[8,80,256]{2,1,0:T(8,128)(2,1)}), bf16[8,80,256]{2,1,0:T(8,128)(2,1)S(1)}, u32[]{:S(2)}, u32[]{:S(2)}) async-start(bf16[8,80,256]{2,1,0:T(8,128)(2,1)} %get-tuple-element.18), calls=%async_computation.1 | async-start | bytes 655360 | tf_op jit(solution)/shard_map/all_to_all | solution.py:346
  36.1 14.8 %collective-permute-start.3 = (bf16[8,64,256]{2,1,0:T(8,128)(2,1)S(1)}, bf16[8,64,256]{2,1,0:T(8,128)(2,1)S(1)}, u32[]{:S(2)}, u32[]{:S(2)}) collective-permute-start(bf16[8,64,256]{2,1,0:T(8,128)(2,1)S(1)} %get-tuple-element.19.refs_4_), channel_id=1, source_target_pairs={{4,0},{0,4},{12,8},{8,12},{20,16},{16,20},{28,24},{24,28},{5,1},{1... | collective-permute-start | bytes 786440 | tf_op jit(solution)/shard_map/ppermute | solution.py:286
  46.4 4.5 %collective-permute-start.2 = (f32[8,256]{1,0:T(8,128)S(1)}, f32[8,256]{1,0:T(8,128)S(1)}, u32[]{:S(2)}, u32[]{:S(2)}) collective-permute-start(f32[8,256]{1,0:T(8,128)S(1)} %convert_reduce_fusion.refs_0_), channel_id=1, source_target_pairs={{0,3},{1,0},{2,1},{3,2},{4,7},{5,4},{6,5},{7,6},{8,11},{9,8},{10,9... | collective-permute-start | bytes 24584 | tf_op jit(solution)/shard_map/ppermute | solution.py:353
  46.5 4.4 %collective-permute-start.1 = (f32[8,256]{1,0:T(8,128)S(1)}, f32[8,256]{1,0:T(8,128)S(1)}, u32[]{:S(2)}, u32[]{:S(2)}) collective-permute-start(f32[8,256]{1,0:T(8,128)S(1)} %convert_reduce_fusion.refs_0_), channel_id=1, source_target_pairs={{0,2},{1,3},{2,0},{3,1},{4,6},{5,7},{6,4},{7,5},{8,10},{9,11},{10,... | collective-permute-start | bytes 24584 | tf_op jit(solution)/shard_map/ppermute | solution.py:353
  48.0 3.1 %collective-permute-start = (f32[8,256]{1,0:T(8,128)S(1)}, f32[8,256]{1,0:T(8,128)S(1)}, u32[]{:S(2)}, u32[]{:S(2)}) collective-permute-start(f32[8,256]{1,0:T(8,128)S(1)} %convert_reduce_fusion.refs_0_), channel_id=1, source_target_pairs={{0,1},{1,2},{2,3},{3,0},{4,5},{5,6},{6,7},{7,4},{8,9},{9,10},{10,1... | collective-permute-start | bytes 24584 | tf_op jit(solution)/shard_map/ppermute | solution.py:353

commit v4 on v3

--- a/solution.py
+++ b/solution.py
@@ -39,78 +39,81 @@
     return lax.fori_loop(0, count, body, carry)
 
 
-def pack_kernel(signal_ref, gate_ref, sent_ref, held_ref, semaphores):
-    count, _, rows, positions = sent_ref.shape
+def pack_kernel(sets, heads, signal_ref, gate_ref, query_ref, key_ref, *refs):
+    sent_ref, key_refs, query_refs = refs[0], refs[1 : 1 + heads], refs[1 + heads : 1 + heads + sets]
+    held_ref, split_ref, turned_ref, loads, stores = refs[1 + heads + sets :]
+    _, count, rows, positions = turned_ref.shape
+    head_dim = split_ref.shape[2]
     copies = [
-        pltpu.make_async_copy(source, held_ref.at[slot], semaphores.at[slot])
-        for slot, source in enumerate((signal_ref, gate_ref))
+        pltpu.make_async_copy(source, held_ref.at[slot], loads.at[slot])
+        for slot, source in enumerate((key_ref, query_ref, signal_ref, gate_ref))
     ]
     for copy in copies:
         copy.start()
-    for slot, copy in enumerate(copies):
-        copy.wait()
-        turned = held_ref[slot].astype(F32).T
-        sent_ref[:, slot] = turned.reshape(count, rows, positions).astype(BF16)
-
-
-def heads_kernel(sets, query_ref, key_ref, *refs):
-    pieces, semaphores = refs[:-1], refs[-1]
+    me = lax.axis_index("seq")
+    results = []
+
+    def store(source, target):
+        results.append(pltpu.make_async_copy(source, target, stores.at[len(results)]))
+        results[-1].start()
+
+    copies[0].wait()
+    for offset, piece in enumerate(key_refs):
+        head = lax.rem(me // sets + offset, heads)
+        lanes = pl.ds(pl.multiple_of(head * head_dim, head_dim), head_dim)
+        split_ref[offset] = held_ref[0, :, lanes]
+        store(split_ref.at[offset], piece)
+    copies[1].wait()
+    for offset, piece in enumerate(query_refs):
+        size = positions // sets
+        first = lax.rem(me + offset, sets) * size
+        store(held_ref.at[1, pl.ds(pl.multiple_of(first, size), size)], piece)
+    for slot in (0, 1):
+        copies[2 + slot].wait()
+        turned = held_ref[2 + slot].astype(F32).T
+        turned_ref[slot] = turned.reshape(count, rows, positions).astype(BF16)
+        store(turned_ref.at[slot], sent_ref.at[:, slot])
+    for result in results:
+        result.wait()
+
+
+def heads_kernel(sets, *refs):
+    parts, pieces = refs[:sets], refs[sets:]
     head_dim = pieces[0].shape[2]
     mine = lax.axis_index("seq") // sets
-    copies = []
     for offset, piece in enumerate(pieces):
         head = lax.rem(mine + offset, len(pieces))
         lanes = pl.ds(pl.multiple_of(head * head_dim, head_dim), head_dim)
-        for slot, source in enumerate((query_ref, key_ref)):
-            copies.append(
-                pltpu.make_async_copy(
-                    source.at[:, lanes], piece.at[slot], semaphores.at[offset, slot]
-                )
-            )
+        for index, part in enumerate(parts):
+            piece[index] = part[:, lanes]
+
+
+def join_kernel(*refs):
+    pieces, (joined_ref, semaphores) = refs[:-2], refs[-2:]
+    copies = [
+        pltpu.make_async_copy(piece, joined_ref.at[index], semaphores.at[index])
+        for index, piece in enumerate(pieces)
+    ]
     for copy in copies:
         copy.start()
     for copy in copies:
         copy.wait()
 
 
-def sets_kernel(sets, *refs):
-    blocks = len(refs) - 2 - sets
-    sources, keys_ref, queries_refs, semaphores = refs[:blocks], refs[blocks], refs[blocks + 1 : -1], refs[-1]
-    rows = queries_refs[0].shape[1]
-    mine = lax.rem(lax.axis_index("seq"), sets)
-    copies = []
-    for block, source in enumerate(sources):
-        copies.append(
-            pltpu.make_async_copy(source.at[1], keys_ref.at[block], semaphores.at[block, sets])
-        )
-        for offset, queries_ref in enumerate(queries_refs):
-            part = lax.rem(mine + offset, sets)
-            span = pl.ds(pl.multiple_of(part * rows, rows), rows)
-            copies.append(
-                pltpu.make_async_copy(
-                    source.at[0, span], queries_ref.at[block], semaphores.at[block, offset]
-                )
-            )
-    for copy in copies:
-        copy.start()
-    for copy in copies:
-        copy.wait()
-
-
 def arrange_kernel(sets, *refs):
-    parts, (keys_ref, queries_ref, semaphores) = refs[: 2 * sets], refs[2 * sets :]
-    heads = parts[0].shape[0]
+    key_parts, query_parts, (keys_ref, queries_ref, semaphores) = refs[:sets], refs[sets:-3], refs[-3:]
+    heads = len(query_parts)
     me = lax.axis_index("seq")
     copies = []
-    for number, part in enumerate(parts):
-        offset, arranged_ref = number % sets, (keys_ref, queries_ref)[number // sets]
-        for index in range(heads):
+    for index in range(heads):
+        for offset in range(sets):
             source = lax.rem(me // sets + heads - index, heads) * sets + lax.rem(me + offset, sets)
-            copies.append(
-                pltpu.make_async_copy(
-                    part.at[index], arranged_ref.at[source], semaphores.at[number, index]
-                )
-            )
+            for slot, (part, target) in enumerate((
+                (key_parts[offset].at[index], keys_ref.at[source]),
+                (query_parts[index].at[offset], queries_ref.at[source]),
+            )):
+                semaphore = semaphores.at[slot, offset, index]
+                copies.append(pltpu.make_async_copy(part, target, semaphore))
     for copy in copies:
         copy.start()
     for copy in copies:
@@ -290,36 +293,44 @@
         return lax.ppermute(array, "seq", pairs)
 
     anywhere = pl.BlockSpec(memory_space=pl.ANY)
-    packed = call(
-        pack_kernel,
-        shape((seq_count, 2, channels, block), BF16),
-        moved=8 * signal.size,
-        in_specs=[anywhere] * 2,
+    packed, *pieces = call(
+        functools.partial(pack_kernel, sets, heads_loc),
+        [shape((seq_count, 2, channels, block), BF16)]
+        + [shape((block, head_dim), BF16)] * heads_loc
+        + [shape((rows, local_width), BF16)] * sets,
+        moved=16 * signal.size,
+        in_specs=[anywhere] * 4,
+        out_specs=[anywhere] * (1 + heads_loc + sets),
         vmem=56,
-        scratch_shapes=[pltpu.VMEM((2,) + signal.shape, BF16), pltpu.SemaphoreType.DMA((2,))],
-    )(signal, gate_rows)
+        scratch_shapes=[
+            pltpu.VMEM((4,) + signal.shape, BF16),
+            pltpu.VMEM((heads_loc, block, head_dim), BF16),
+            pltpu.VMEM((2, seq_count, channels, block), BF16),
+            pltpu.SemaphoreType.DMA((4,)),
+            pltpu.SemaphoreType.DMA((heads_loc + sets + 2,)),
+        ],
+    )(signal, gate_rows, queries, key_rows)
     got = lax.all_to_all(packed, "seq", 0, 0, tiled=True)
-
-    pieces = call(
-        functools.partial(heads_kernel, sets),
-        [shape((2, block, head_dim), BF16)] * heads_loc,
-        moved=8 * signal.size,
-        in_specs=[anywhere] * 2,
-        out_specs=[anywhere] * heads_loc,
-        scratch_shapes=[pltpu.SemaphoreType.DMA((heads_loc, 2))],
-    )(queries, key_rows)
-    pieces = [pieces[0]] + [from_head(pieces[k], k) for k in range(1, heads_loc)]
-    own_keys, *set_queries = call(
-        functools.partial(sets_kernel, sets),
-        [shape((heads_loc, block, head_dim), BF16)] + [shape((heads_loc, rows, head_dim), BF16)] * sets,
-        moved=8 * signal.size,
+    key_pieces, set_queries = pieces[:heads_loc], pieces[heads_loc:]
+    key_pieces = key_pieces[:1] + [from_head(key_pieces[k], k) for k in range(1, heads_loc)]
+    own_keys = call(
+        join_kernel,
+        shape((heads_loc, block, head_dim), BF16),
+        moved=4 * signal.size,
         flops=4 * 10**10,
         in_specs=[anywhere] * heads_loc,
-        out_specs=[anywhere] * (sets + 1),
-        scratch_shapes=[pltpu.SemaphoreType.DMA((heads_loc, sets + 1))],
-    )(*pieces)
+        out_specs=anywhere,
+        scratch_shapes=[pltpu.SemaphoreType.DMA((heads_loc,))],
+    )(*key_pieces)
     key_parts = [own_keys] + [from_set(own_keys, k) for k in range(1, sets)]
-    query_parts = [set_queries[0]] + [from_set(set_queries[-k], k) for k in range(1, sets)]
+    query_sets = set_queries[:1] + [from_set(set_queries[-k], k) for k in range(1, sets)]
+    query_pieces = call(
+        functools.partial(heads_kernel, sets),
+        [shape((sets, rows, head_dim), BF16)] * heads_loc,
+        moved=4 * signal.size,
+        flops=0,
+    )(*query_sets)
+    query_parts = [query_pieces[0]] + [from_head(query_pieces[k], k) for k in range(1, heads_loc)]
 
     matrix = call(
         functools.partial(toeplitz_kernel, sets),
@@ -374,9 +385,9 @@
         [shape((seq_count, block, head_dim), BF16), shape((seq_count, rows, head_dim), BF16)],
         moved=6 * length * head_dim,
         flops=4 * 10**10,
-        in_specs=[anywhere] * (2 * sets),
+        in_specs=[anywhere] * (sets + heads_loc),
         out_specs=[anywhere] * 2,
-        scratch_shapes=[pltpu.SemaphoreType.DMA((2 * sets, heads_loc))],
+        scratch_shapes=[pltpu.SemaphoreType.DMA((2, sets, heads_loc))],
     )(*key_parts, *query_parts)
     totals, *weights = call(
         functools.partial(weights_kernel, gridded),

time: 52.9 us -> 50.7 us (0.958)
  waiting for transfers between devices: 19.1 us -> 14.1 us
  starting transfers between devices: 20.2 us -> 25.2 us
  local copies, waits for them, and re-layouts: 2.7 us -> 0.82 us
    all_to_all x1, waiting for transfers between devices: 10.1 us -> 0.01 us  [shards(): got = lax.all_to_all(packed, 'seq', 0, 0, tiled=True)]
    ppermute x3, waiting for transfers between devices: 0.01 us -> 8.6 us  [from_set(): return lax.ppermute(array, 'seq', pairs)]
    ppermute x3 -> x6, starting transfers between devices: 7.01 us -> 11.7 us  [from_head(): return lax.ppermute(array, 'seq', pairs)]
    unnamed x8 -> x10, local copies, waits for them, and re-layouts: 2.53 us -> 0.64 us
    all_to_all x1, waiting for transfers between devices: 7.06 us -> 5.23 us  [shards(): home = lax.all_to_all(back, 'seq', 0, 0, tiled=True)]
    ppermute x3 -> x6, waiting for transfers between devices: 1.73 us -> 0.02 us  [from_head(): return lax.ppermute(array, 'seq', pairs)]
  transfers between devices with their start and end apart: 11 -> 14, of which waited for: 4 -> 3; matrix products, arithmetic and copies ran while one was open for 0% -> 0% of each run, Pallas kernels for 16% -> 12%
where the time goes in v4:
time: 50.7 us; the launch traced here: 50.3 us
  starting transfers between devices  25.2 us (50%)
  waiting for transfers between devices  14.1 us (28%)
  Pallas kernels  9.39 us (19%)
  local copies, waits for them, and re-layouts  0.82 us (2%)
  between operations  0.76 us (1%)
    ppermute x6, starting transfers between devices, from_head(): return lax.ppermute(array, 'seq', pairs)  11.7 us
    ppermute x3, waiting for transfers between devices, from_set(): return lax.ppermute(array, 'seq', pairs)  8.6 us
    all_to_all x1, waiting for transfers between devices, shards(): home = lax.all_to_all(back, 'seq', 0, 0, tiled=True)  5.23 us
    ppermute x3, starting transfers between devices, from_set(): return lax.ppermute(array, 'seq', pairs)  4.33 us
    all_to_all x1, starting transfers between devices, shards(): home = lax.all_to_all(back, 'seq', 0, 0, tiled=True)  3.73 us
    all_to_all x1, starting transfers between devices, shards(): got = lax.all_to_all(packed, 'seq', 0, 0, tiled=True)  3.62 us
    pallas_call x1, Pallas kernels, shards(): call(functools.partial(pack_kernel, sets, heads_loc), [shape((seq_count,...  2.19 us
    pallas_call x1, Pallas kernels, shards(): call(functools.partial(weights_kernel, gridded), [shape(total_shape, F32)...  1.84 us
  transfers between devices with their start and end apart: 14, of which 3 were waited for; matrix products, arithmetic and copies ran while one was open for 0% of the time, Pallas kernels for 12%

profile of v4, /device:TPU:0, one launch (start us, length us, event | category | flops | bytes accessed | tf_op | source)
XLA Modules:
  0.0 50.3 jit_solution(386624133685594231)
XLA Ops:
  0.6 0.0 copy-start
  0.6 2.2 %shard_map.77 = (bf16[8,2,64,256]{3,2,1,0:T(8,128)(2,1)}, bf16[256,128]{1,0:T(8,128)(2,1)}, bf16[256,128]{1,0:T(8,128)(2,1)}, bf16[256,128]{1,0:T(8,128)(2,1)}, ...) custom-call(bf16[256,512]{1,0:T(8,128)(2,1)} %signal_ref.1, ...), custom_call_target="tpu_custom_call" | custom-call | bytes 2097152 | tf_op jit(solution)/shard_map/pallas_call | solution.py:296
  2.8 3.1 %collective-permute-start.4 = (bf16[256,128]{1,0:T(8,128)(2,1)}, bf16[256,128]{1,0:T(8,128)(2,1)S(1)}, u32[]{:S(2)}, u32[]{:S(2)}) collective-permute-start(bf16[256,128]{1,0:T(8,128)(2,1)} %get-tuple-element.26), channel_id=1, source_target_pairs={{0,8},{4,12},{8,16},{12,20},{16,24},{20,28},{24,0},{28,4},{1,9},{5... | collective-permute-start | bytes 196616 | tf_op jit(solution)/shard_map/ppermute | solution.py:293
  5.9 2.6 %collective-permute-start.5 = (bf16[256,128]{1,0:T(8,128)(2,1)}, bf16[256,128]{1,0:T(8,128)(2,1)S(1)}, u32[]{:S(2)}, u32[]{:S(2)}) collective-permute-start(bf16[256,128]{1,0:T(8,128)(2,1)} %get-tuple-element.27), channel_id=1, source_target_pairs={{0,16},{4,20},{8,24},{12,28},{16,0},{20,4},{24,8},{28,12},{1,17},{... | collective-permute-start | bytes 196616 | tf_op jit(solution)/shard_map/ppermute | solution.py:293
  8.5 1.3 %collective-permute-start.6 = (bf16[256,128]{1,0:T(8,128)(2,1)}, bf16[256,128]{1,0:T(8,128)(2,1)S(1)}, u32[]{:S(2)}, u32[]{:S(2)}) collective-permute-start(bf16[256,128]{1,0:T(8,128)(2,1)} %get-tuple-element.28), channel_id=1, source_target_pairs={{0,24},{4,28},{8,0},{12,4},{16,8},{20,12},{24,16},{28,20},{1,25},{... | collective-permute-start | bytes 196616 | tf_op jit(solution)/shard_map/ppermute | solution.py:293
  9.9 0.0 copy-start.4
  9.9 0.0 copy-start.3
  9.9 3.6 %all-to-all-start = ((bf16[8,2,64,256]{3,2,1,0:T(8,128)(2,1)}), bf16[8,2,64,256]{3,2,1,0:T(8,128)(2,1)S(1)}, u32[]{:S(2)}, u32[]{:S(2)}) async-start(bf16[8,2,64,256]{3,2,1,0:T(8,128)(2,1)} %get-tuple-element.22), calls=%async_computation | async-start | bytes 1048576 | tf_op jit(solution)/shard_map/all_to_all | solution.py:313
  13.5 0.0 copy-done.4
  13.5 1.9 %collective-permute-start.8 = (bf16[128,512]{1,0:T(8,128)(2,1)S(1)}, bf16[128,512]{1,0:T(8,128)(2,1)S(1)}, u32[]{:S(2)}, u32[]{:S(2)}) collective-permute-start(bf16[128,512]{1,0:T(8,128)(2,1)S(1)} %copy-done.4), channel_id=1, source_target_pairs={{4,0},{0,4},{12,8},{8,12},{20,16},{16,20},{28,24},{24,28},{5,1},{1... | collective-permute-start | bytes 393224 | tf_op jit(solution)/shard_map/ppermute | solution.py:289
  15.4 0.0 collective-permute-done.4.refs_1_
  15.4 0.0 collective-permute-done.5.refs_2_
  15.4 0.0 collective-permute-done.6.refs_3_
  15.4 0.0 copy-done.3
  15.4 0.0 copy-start.1
  15.5 0.4 shard_map.81.refs_0_
  15.8 0.2 collective-permute-start.7
  16.1 8.6 %collective-permute-done.8.refs_1_ = bf16[128,512]{1,0:T(8,128)(2,1)S(1)} collective-permute-done((bf16[128,512]{1,0:T(8,128)(2,1)S(1)}, bf16[128,512]{1,0:T(8,128)(2,1)S(1)}, u32[]{:S(2)}, u32[]{:S(2)}) %collective-permute-start.8) | collective-permute-done | bytes 131104 | tf_op jit(solution)/shard_map/ppermute | solution.py:289
  24.7 0.0 copy-done.1
  24.7 1.7 %collective-permute-start.9 = (bf16[2,128,128]{2,1,0:T(8,128)(2,1)S(1)}, bf16[2,128,128]{2,1,0:T(8,128)(2,1)S(1)}, u32[]{:S(2)}, u32[]{:S(2)}) collective-permute-start(bf16[2,128,128]{2,1,0:T(8,128)(2,1)S(1)} %get-tuple-element.32), channel_id=1, source_target_pairs={{0,8},{4,12},{8,16},{12,20},{16,24},{20,28},{24,0},{28,4},{1,9},{5... | collective-permute-start | bytes 196616 | tf_op jit(solution)/shard_map/ppermute | solution.py:293
  26.5 2.7 %collective-permute-start.10 = (bf16[2,128,128]{2,1,0:T(8,128)(2,1)S(1)}, bf16[2,128,128]{2,1,0:T(8,128)(2,1)S(1)}, u32[]{:S(2)}, u32[]{:S(2)}) collective-permute-start(bf16[2,128,128]{2,1,0:T(8,128)(2,1)S(1)} %get-tuple-element.33), channel_id=1, source_target_pairs={{0,16},{4,20},{8,24},{12,28},{16,0},{20,4},{24,8},{28,12},{1,17},{... | collective-permute-start | bytes 196616 | tf_op jit(solution)/shard_map/ppermute | solution.py:293
  29.1 0.3 collective-permute-start.11
  29.5 0.0 copy-done
  29.5 0.1 dynamic-slice_bitcast_fusion
  29.6 0.0 copy-start.2
  29.6 0.1 copy.8.skip_ref
  29.7 0.6 %copy-done.2 = bf16[2048,4]{0,1:T(4,128)(2,1)S(1)} copy-done((bf16[2048,4]{0,1:T(4,128)(2,1)S(1)}, bf16[2048,4]{0,1:T(4,128)(2,1)}, u32[]{:S(2)}) %copy-start.2) | copy-done | bytes 16408
  30.3 0.2 shard_map.78.matrix_ref
  30.5 0.0 all-to-all-done.got_ref
  30.5 1.2 %shard_map.79 = (bf16[8,64,256]{2,1,0:T(8,128)(2,1)S(1)}, bf16[8,80,256]{2,1,0:T(8,128)(2,1)}) custom-call(bf16[8,2,64,256]{3,2,1,0:T(8,128)(2,1)S(1)} %all-to-all-done.got_ref, bf16[256,2048]{1,0:T(8,128)(2,1)S(1)} %shard_map.78.matrix_ref, f32[64,1]{1,0:T(8,128)S(1)} %copy.8.skip_ref), custom_call_target="tpu_custom_call" | custom-call | flops 268435456 | bytes 1310720 | tf_op jit(solution)/shard_map/pallas_call | solution.py:345
  31.7 3.7 %all-to-all-start.1 = ((bf16[8,80,256]{2,1,0:T(8,128)(2,1)}), bf16[8,80,256]{2,1,0:T(8,128)(2,1)S(1)}, u32[]{:S(2)}, u32[]{:S(2)}) async-start(bf16[8,80,256]{2,1,0:T(8,128)(2,1)} %get-tuple-element.23), calls=%async_computation.1 | async-start | bytes 655360 | tf_op jit(solution)/shard_map/all_to_all | solution.py:357
  35.5 2.2 %collective-permute-start.3 = (bf16[8,64,256]{2,1,0:T(8,128)(2,1)S(1)}, bf16[8,64,256]{2,1,0:T(8,128)(2,1)S(1)}, u32[]{:S(2)}, u32[]{:S(2)}) collective-permute-start(bf16[8,64,256]{2,1,0:T(8,128)(2,1)S(1)} %get-tuple-element.24.refs_4_), channel_id=1, source_target_pairs={{4,0},{0,4},{12,8},{8,12},{20,16},{16,20},{28,24},{24,28},{5,1},{1... | collective-permute-start | bytes 786440 | tf_op jit(solution)/shard_map/ppermute | solution.py:289
  37.7 0.0 collective-permute-done.9.refs_3_
  37.7 0.0 collective-permute-done.10.refs_4_
  37.7 0.0 collective-permute-done.11.refs_5_
  37.7 0.0 collective-permute-done.7.refs_1_
  37.7 1.2 %shard_map.83 = (bf16[8,256,128]{2,1,0:T(8,128)(2,1)S(1)}, bf16[8,128,128]{2,1,0:T(8,128)(2,1)S(1)}) custom-call(bf16[4,256,128]{2,1,0:T(8,128)(2,1)S(1)} %shard_map.81.refs_0_, bf16[4,256,128]{2,1,0:T(8,128)(2,1)S(1)} %collective-permute-done.7.refs_1_, bf16[2,128,128]{2,1,0:T(8,128)(2,1)S(1)} %get-tuple-element.31.refs_2_, ...), custom_call_target="tpu_custom_call" | custom-call | flops 40000000000 | bytes 1572864 | tf_op jit(solution)/shard_map/pallas_call | solution.py:383
  38.9 5.2 %all-to-all-done.1.got_ref = bf16[8,80,256]{2,1,0:T(8,128)(2,1)S(1)} async-done(((bf16[8,80,256]{2,1,0:T(8,128)(2,1)}), bf16[8,80,256]{2,1,0:T(8,128)(2,1)S(1)}, u32[]{:S(2)}, u32[]{:S(2)}) %all-to-all-start.1) | async-done | bytes 327712 | tf_op jit(solution)/shard_map/all_to_all | solution.py:357
  44.2 0.1 collective-permute-start.2
  44.2 1.6 %collective-permute-start.1 = (f32[8,256]{1,0:T(8,128)S(1)}, f32[8,256]{1,0:T(8,128)S(1)}, u32[]{:S(2)}, u32[]{:S(2)}) collective-permute-start(f32[8,256]{1,0:T(8,128)S(1)} %convert_reduce_fusion.refs_0_), channel_id=1, source_target_pairs={{0,2},{1,3},{2,0},{3,1},{4,6},{5,7},{6,4},{7,5},{8,10},{9,11},{10,... | collective-permute-start | bytes 24584 | tf_op jit(solution)/shard_map/ppermute | solution.py:364
  45.8 0.2 collective-permute-start
  46.0 1.8 %shard_map.84 = (f32[4,8,256]{2,1,0:T(8,128)S(1)}, bf16[512,256]{1,0:T(8,128)(2,1)S(1)}, bf16[1024,256]{1,0:T(8,128)(2,1)S(1)}, bf16[1536,256]{1,0:T(8,128)(2,1)S(1)}, bf16[2048,256]{1,0:T(8,128)(2,1)S(1)}) custom-call(bf16[8,256,128]{2,1,0:T(8,128)(2,1)S(1)} %get-tuple-element.35.key_ref, bf16[8,128,128]{2,1,0:T(8,128)(2,1)S(1)} %get-tuple-element.36.query_ref), custom_call_target="tpu_custom_call" | custom-call | flops 268435456 | bytes 2621440 | tf_op jit(solution)/shard_map/pallas_call | solution.py:392
  47.8 0.8 %shard_map.80 = bf16[256,512]{1,0:T(8,128)(2,1)} custom-call(bf16[8,80,256]{2,1,0:T(8,128)(2,1)S(1)} %all-to-all-done.1.got_ref), custom_call_target="tpu_custom_call" | custom-call | bytes 524288 | tf_op jit(solution)/shard_map/pallas_call | solution.py:418
  48.6 0.0 collective-permute-done.3.refs_5_
  48.6 0.0 collective-permute-done.2.refs_3_
  48.6 0.0 collective-permute-done.1.refs_2_
  48.6 0.2 collective-permute-done.refs_1_
  48.9 1.4 %shard_map.85 = bf16[1024,128]{1,0:T(8,128)(2,1)} custom-call(f32[8,256]{1,0:T(8,128)S(1)} %convert_reduce_fusion.refs_0_, f32[8,256]{1,0:T(8,128)S(1)} %collective-permute-done.refs_1_, f32[8,256]{1,0:T(8,128)S(1)} %collective-permute-done.1.refs_2_, f32[8,256]{1,0:T(8,128)S(1)} %collective-permute-done.2.refs_3_, ...), custom_call_target="tpu_custom_call" | custom-call | flops 268435456 | bytes 2621440 | tf_op jit(solution)/shard_map/pallas_call | solution.py:405
  (3 shorter events, 0.1 us)
Async XLA Ops:
  0.6 28.8 %copy-start = (f32[512]{0:T(512)S(1)}, f32[512]{0:T(512)}, u32[]{:S(2)}) copy-start(f32[512]{0:T(512)} %param.8) | copy-start | bytes 6148
  2.8 12.6 %collective-permute-start.4 = (bf16[256,128]{1,0:T(8,128)(2,1)}, bf16[256,128]{1,0:T(8,128)(2,1)S(1)}, u32[]{:S(2)}, u32[]{:S(2)}) collective-permute-start(bf16[256,128]{1,0:T(8,128)(2,1)} %get-tuple-element.26), channel_id=1, source_target_pairs={{0,8},{4,12},{8,16},{12,20},{16,24},{20,28},{24,0},{28,4},{1,9},{5... | collective-permute-start | bytes 196616 | tf_op jit(solution)/shard_map/ppermute | solution.py:293
  5.9 9.5 %collective-permute-start.5 = (bf16[256,128]{1,0:T(8,128)(2,1)}, bf16[256,128]{1,0:T(8,128)(2,1)S(1)}, u32[]{:S(2)}, u32[]{:S(2)}) collective-permute-start(bf16[256,128]{1,0:T(8,128)(2,1)} %get-tuple-element.27), channel_id=1, source_target_pairs={{0,16},{4,20},{8,24},{12,28},{16,0},{20,4},{24,8},{28,12},{1,17},{... | collective-permute-start | bytes 196616 | tf_op jit(solution)/shard_map/ppermute | solution.py:293
  8.5 6.9 %collective-permute-start.6 = (bf16[256,128]{1,0:T(8,128)(2,1)}, bf16[256,128]{1,0:T(8,128)(2,1)S(1)}, u32[]{:S(2)}, u32[]{:S(2)}) collective-permute-start(bf16[256,128]{1,0:T(8,128)(2,1)} %get-tuple-element.28), channel_id=1, source_target_pairs={{0,24},{4,28},{8,0},{12,4},{16,8},{20,12},{24,16},{28,20},{1,25},{... | collective-permute-start | bytes 196616 | tf_op jit(solution)/shard_map/ppermute | solution.py:293
  9.9 3.6 %copy-start.4 = (bf16[128,512]{1,0:T(8,128)(2,1)S(1)}, bf16[128,512]{1,0:T(8,128)(2,1)}, u32[]{:S(2)}) copy-start(bf16[128,512]{1,0:T(8,128)(2,1)} %get-tuple-element.30) | copy-start | bytes 393220
  9.9 5.6 %copy-start.3 = (bf16[256,128]{1,0:T(8,128)(2,1)S(1)}, bf16[256,128]{1,0:T(8,128)(2,1)}, u32[]{:S(2)}) copy-start(bf16[256,128]{1,0:T(8,128)(2,1)} %get-tuple-element.25.refs_0_) | copy-start | bytes 196612
  9.9 20.6 %all-to-all-start = ((bf16[8,2,64,256]{3,2,1,0:T(8,128)(2,1)}), bf16[8,2,64,256]{3,2,1,0:T(8,128)(2,1)S(1)}, u32[]{:S(2)}, u32[]{:S(2)}) async-start(bf16[8,2,64,256]{3,2,1,0:T(8,128)(2,1)} %get-tuple-element.22), calls=%async_computation | async-start | bytes 1048576 | tf_op jit(solution)/shard_map/all_to_all | solution.py:313
  13.5 11.2 %collective-permute-start.8 = (bf16[128,512]{1,0:T(8,128)(2,1)S(1)}, bf16[128,512]{1,0:T(8,128)(2,1)S(1)}, u32[]{:S(2)}, u32[]{:S(2)}) collective-permute-start(bf16[128,512]{1,0:T(8,128)(2,1)S(1)} %copy-done.4), channel_id=1, source_target_pairs={{4,0},{0,4},{12,8},{8,12},{20,16},{16,20},{28,24},{24,28},{5,1},{1... | collective-permute-start | bytes 393224 | tf_op jit(solution)/shard_map/ppermute | solution.py:289
  15.4 9.2 %copy-start.1 = (bf16[128,512]{1,0:T(8,128)(2,1)S(1)}, bf16[128,512]{1,0:T(8,128)(2,1)}, u32[]{:S(2)}) copy-start(bf16[128,512]{1,0:T(8,128)(2,1)} %get-tuple-element.29.refs_0_) | copy-start | bytes 393220
  15.8 21.8 %collective-permute-start.7 = (bf16[4,256,128]{2,1,0:T(8,128)(2,1)S(1)}, bf16[4,256,128]{2,1,0:T(8,128)(2,1)S(1)}, u32[]{:S(2)}, u32[]{:S(2)}) collective-permute-start(bf16[4,256,128]{2,1,0:T(8,128)(2,1)S(1)} %shard_map.81.refs_0_), channel_id=1, source_target_pairs={{4,0},{0,4},{12,8},{8,12},{20,16},{16,20},{28,24},{24,28},{5,1},{1... | collective-permute-start | bytes 786440 | tf_op jit(solution)/shard_map/ppermute | solution.py:289
  24.7 12.9 %collective-permute-start.9 = (bf16[2,128,128]{2,1,0:T(8,128)(2,1)S(1)}, bf16[2,128,128]{2,1,0:T(8,128)(2,1)S(1)}, u32[]{:S(2)}, u32[]{:S(2)}) collective-permute-start(bf16[2,128,128]{2,1,0:T(8,128)(2,1)S(1)} %get-tuple-element.32), channel_id=1, source_target_pairs={{0,8},{4,12},{8,16},{12,20},{16,24},{20,28},{24,0},{28,4},{1,9},{5... | collective-permute-start | bytes 196616 | tf_op jit(solution)/shard_map/ppermute | solution.py:293
  26.5 11.2 %collective-permute-start.10 = (bf16[2,128,128]{2,1,0:T(8,128)(2,1)S(1)}, bf16[2,128,128]{2,1,0:T(8,128)(2,1)S(1)}, u32[]{:S(2)}, u32[]{:S(2)}) collective-permute-start(bf16[2,128,128]{2,1,0:T(8,128)(2,1)S(1)} %get-tuple-element.33), channel_id=1, source_target_pairs={{0,16},{4,20},{8,24},{12,28},{16,0},{20,4},{24,8},{28,12},{1,17},{... | collective-permute-start | bytes 196616 | tf_op jit(solution)/shard_map/ppermute | solution.py:293
  29.1 8.5 %collective-permute-start.11 = (bf16[2,128,128]{2,1,0:T(8,128)(2,1)S(1)}, bf16[2,128,128]{2,1,0:T(8,128)(2,1)S(1)}, u32[]{:S(2)}, u32[]{:S(2)}) collective-permute-start(bf16[2,128,128]{2,1,0:T(8,128)(2,1)S(1)} %get-tuple-element.34), channel_id=1, source_target_pairs={{0,24},{4,28},{8,0},{12,4},{16,8},{20,12},{24,16},{28,20},{1,25},{... | collective-permute-start | bytes 196616 | tf_op jit(solution)/shard_map/ppermute | solution.py:293
  29.6 0.7 %copy-start.2 = (bf16[2048,4]{0,1:T(4,128)(2,1)S(1)}, bf16[2048,4]{0,1:T(4,128)(2,1)}, u32[]{:S(2)}) copy-start(bf16[2048,4]{0,1:T(4,128)(2,1)} %param.9) | copy-start | bytes 49156
  31.7 12.4 %all-to-all-start.1 = ((bf16[8,80,256]{2,1,0:T(8,128)(2,1)}), bf16[8,80,256]{2,1,0:T(8,128)(2,1)S(1)}, u32[]{:S(2)}, u32[]{:S(2)}) async-start(bf16[8,80,256]{2,1,0:T(8,128)(2,1)} %get-tuple-element.23), calls=%async_computation.1 | async-start | bytes 655360 | tf_op jit(solution)/shard_map/all_to_all | solution.py:357
  35.5 13.2 %collective-permute-start.3 = (bf16[8,64,256]{2,1,0:T(8,128)(2,1)S(1)}, bf16[8,64,256]{2,1,0:T(8,128)(2,1)S(1)}, u32[]{:S(2)}, u32[]{:S(2)}) collective-permute-start(bf16[8,64,256]{2,1,0:T(8,128)(2,1)S(1)} %get-tuple-element.24.refs_4_), channel_id=1, source_target_pairs={{4,0},{0,4},{12,8},{8,12},{20,16},{16,20},{28,24},{24,28},{5,1},{1... | collective-permute-start | bytes 786440 | tf_op jit(solution)/shard_map/ppermute | solution.py:289
  44.2 4.5 %collective-permute-start.2 = (f32[8,256]{1,0:T(8,128)S(1)}, f32[8,256]{1,0:T(8,128)S(1)}, u32[]{:S(2)}, u32[]{:S(2)}) collective-permute-start(f32[8,256]{1,0:T(8,128)S(1)} %convert_reduce_fusion.refs_0_), channel_id=1, source_target_pairs={{0,3},{1,0},{2,1},{3,2},{4,7},{5,4},{6,5},{7,6},{8,11},{9,8},{10,9... | collective-permute-start | bytes 24584 | tf_op jit(solution)/shard_map/ppermute | solution.py:364
  44.2 4.4 %collective-permute-start.1 = (f32[8,256]{1,0:T(8,128)S(1)}, f32[8,256]{1,0:T(8,128)S(1)}, u32[]{:S(2)}, u32[]{:S(2)}) collective-permute-start(f32[8,256]{1,0:T(8,128)S(1)} %convert_reduce_fusion.refs_0_), channel_id=1, source_target_pairs={{0,2},{1,3},{2,0},{3,1},{4,6},{5,7},{6,4},{7,5},{8,10},{9,11},{10,... | collective-permute-start | bytes 24584 | tf_op jit(solution)/shard_map/ppermute | solution.py:364
  45.8 3.1 %collective-permute-start = (f32[8,256]{1,0:T(8,128)S(1)}, f32[8,256]{1,0:T(8,128)S(1)}, u32[]{:S(2)}, u32[]{:S(2)}) collective-permute-start(f32[8,256]{1,0:T(8,128)S(1)} %convert_reduce_fusion.refs_0_), channel_id=1, source_target_pairs={{0,1},{1,2},{2,3},{3,0},{4,5},{5,6},{6,7},{7,4},{8,9},{9,10},{10,1... | collective-permute-start | bytes 24584 | tf_op jit(solution)/shard_map/ppermute | solution.py:364

commit v5 on v4

--- a/solution.py
+++ b/solution.py
@@ -88,8 +88,8 @@
             piece[index] = part[:, lanes]
 
 
-def join_kernel(*refs):
-    pieces, (joined_ref, semaphores) = refs[:-2], refs[-2:]
+def join_kernel(count, *refs):
+    pieces, (joined_ref, semaphores) = refs[:count], refs[-2:]
     copies = [
         pltpu.make_async_copy(piece, joined_ref.at[index], semaphores.at[index])
         for index, piece in enumerate(pieces)
@@ -143,10 +143,13 @@
 def conv_kernel(got_ref, matrix_ref, skip_ref, mixed_ref, back_ref, total_ref):
     count, _, rows, block = got_ref.shape
     inputs = merge_rows(got_ref[:, 0])
-    for lag in range(count):
+    before = jnp.concatenate([jnp.zeros((rows, block), BF16), inputs[: (count - 1) * rows]], axis=0)
+    pairs = jnp.concatenate([inputs, before], axis=1)
+    for lag in range(0, count, 2):
+        spans = [slice((lag + more) * block, (lag + more + 1) * block) for more in (0, 1)]
         product = jnp.dot(
-            inputs[: (count - lag) * rows],
-            matrix_ref[:, lag * block : (lag + 1) * block],
+            pairs[: (count - lag) * rows],
+            jnp.concatenate([matrix_ref[:, span] for span in spans], axis=0),
             preferred_element_type=F32,
         )
         if lag == 0:
@@ -164,8 +167,7 @@
         widened = mixed.astype(F32)
         sums.append(jnp.sum(widened * widened, axis=0, keepdims=True))
     squares = jnp.concatenate(sums, axis=0)
-    high = squares.astype(BF16).astype(F32)
-    both = jnp.concatenate([high, squares - high], axis=0).astype(BF16)
+    both = squares.astype(BF16)
     for index in range(count):
         back_ref[index, rows:] = both
 
@@ -201,7 +203,7 @@
         return total + jnp.sum(weights, axis=0, keepdims=True)
 
     total = loop(chunks, weigh, jnp.zeros((1, wide), F32))
-    total_ref[...] = jnp.broadcast_to(total, total_ref.shape)
+    total_ref[...] = jnp.broadcast_to(1.0 / total, total_ref.shape)
 
 
 def weights_kernel(gridded, key_ref, query_ref, total_ref, *refs):
@@ -228,9 +230,11 @@
 
 
 def output_kernel(sets, steps, width, gridded, *refs):
-    squares_refs, refs = refs[: -4 - sets - (1 if gridded else steps)], refs[-4 - sets - (1 if gridded else steps) :]
-    parts, total_ref, weights_refs = refs[:sets], refs[sets], refs[sets + 1 : -3]
-    out_ref, wide_ref, values_ref = refs[-3:]
+    own = 4 if gridded else 6
+    first = len(refs) - own - sets - (1 if gridded else steps)
+    squares_refs, parts, refs = refs[:first], refs[first : first + sets], refs[first + sets :]
+    total_ref, weights_refs, refs = refs[0], refs[1 : 1 - own], refs[1 - own :]
+    out_ref, wide_ref, values_ref = refs[:3]
     count, rows, block = parts[0].shape
     mine = lax.rem(lax.axis_index("seq"), sets)
     reach = count * block // steps
@@ -241,28 +245,42 @@
         for offset in range(sets):
             place = lax.rem(mine + offset, sets)
             for index in range(count):
+                span = slice(index * block, (index + 1) * block)
                 part = parts[offset][index].astype(F32) * inv_scale[index : index + 1]
-                wide_ref[place, :, index * block : (index + 1) * block] = part
-        for index in range(count):
-            span = slice(index * block, (index + 1) * block)
-            values_ref[:, span] = merge_rows(wide_ref[:, :, span]).astype(BF16)
-
-    def attend(step, weights, total, out):
+                if rows % 16:
+                    wide_ref[place, :, span] = part
+                else:
+                    lines = pl.ds(pl.multiple_of(place * rows, rows), rows)
+                    values_ref[lines, span] = part.astype(BF16)
+        if rows % 16:
+            for index in range(count):
+                span = slice(index * block, (index + 1) * block)
+                values_ref[:, span] = merge_rows(wide_ref[:, :, span]).astype(BF16)
+
+    def attend(step, weights, total):
         keys = (step + 1) * reach
         summed = jnp.dot(values_ref[:, :keys], weights[:keys], preferred_element_type=F32)
-        out[...] = (summed / total[:1]).T.astype(BF16)
-
-    if not gridded:
-        norm()
+        return (summed * total[:1]).T.astype(BF16)
+
+    if gridded:
+        pl.when(pl.program_id(0) == 0)(norm)
+
+        def block_of(step):
+            out_ref[...] = attend(step, weights_refs[0].at[0], total_ref.at[0])
+
         for step in range(steps):
-            rows_out = out_ref.at[pl.ds(step * QUERY_BLOCK, QUERY_BLOCK)]
-            attend(step, weights_refs[step], total_ref.at[step], rows_out)
+            pl.when(pl.program_id(0) == step)(functools.partial(block_of, step))
         return
-    pl.when(pl.program_id(0) == 0)(norm)
-    for step in range(steps):
-        pl.when(pl.program_id(0) == step)(
-            functools.partial(attend, step, weights_refs[0].at[0], total_ref.at[0], out_ref)
-        )
+    staged_ref, semaphores = refs[3:]
+    norm()
+    copies = []
+    for step in reversed(range(steps)):
+        staged_ref[step] = attend(step, weights_refs[step], total_ref.at[step])
+        lines = out_ref.at[pl.ds(step * QUERY_BLOCK, QUERY_BLOCK)]
+        copies.append(pltpu.make_async_copy(staged_ref.at[step], lines, semaphores.at[step]))
+        copies[-1].start()
+    for copy in copies:
+        copy.wait()
 
 
 def shards(signal, gate_rows, skip_gain, filter_taps, queries, key_rows):
@@ -313,15 +331,25 @@
     got = lax.all_to_all(packed, "seq", 0, 0, tiled=True)
     key_pieces, set_queries = pieces[:heads_loc], pieces[heads_loc:]
     key_pieces = key_pieces[:1] + [from_head(key_pieces[k], k) for k in range(1, heads_loc)]
+    matrix = call(
+        functools.partial(toeplitz_kernel, sets),
+        shape((block, length), BF16),
+        moved=block * length * 2,
+        flops=block * length * 8,
+        vmem=8 if not gridded else 56,
+    )(filter_taps.T)
+    skip = lax.dynamic_slice_in_dim(skip_gain, lax.axis_index("seq") * channels, channels)[:, None]
+
+    whole = pl.BlockSpec(memory_space=pltpu.VMEM)
     own_keys = call(
-        join_kernel,
+        functools.partial(join_kernel, heads_loc),
         shape((heads_loc, block, head_dim), BF16),
         moved=4 * signal.size,
         flops=4 * 10**10,
-        in_specs=[anywhere] * heads_loc,
+        in_specs=[anywhere] * (heads_loc + 1),
         out_specs=anywhere,
         scratch_shapes=[pltpu.SemaphoreType.DMA((heads_loc,))],
-    )(*key_pieces)
+    )(*key_pieces, matrix)
     key_parts = [own_keys] + [from_set(own_keys, k) for k in range(1, sets)]
     query_sets = set_queries[:1] + [from_set(set_queries[-k], k) for k in range(1, sets)]
     query_pieces = call(
@@ -332,31 +360,21 @@
     )(*query_sets)
     query_parts = [query_pieces[0]] + [from_head(query_pieces[k], k) for k in range(1, heads_loc)]
 
-    matrix = call(
-        functools.partial(toeplitz_kernel, sets),
-        shape((block, length), BF16),
-        moved=block * length * 2,
-        flops=block * length * 8,
-        vmem=8 if not gridded else 56,
-    )(filter_taps.T)
-    skip = lax.dynamic_slice_in_dim(skip_gain, lax.axis_index("seq") * channels, channels)
-
-    whole = pl.BlockSpec(memory_space=pltpu.VMEM)
     mixed, back = call(
         conv_kernel,
         [
             shape((seq_count, channels, block), BF16),
-            shape((seq_count, channels + 2 * seq_count, block), BF16),
+            shape((seq_count, channels + seq_count, block), BF16),
         ],
         moved=signal.size * 10,
         flops=length * length * channels,
         vmem=8 if not gridded else 56,
         scratch_shapes=[pltpu.VMEM((seq_count * channels, block), F32)],
-    )(got, matrix, skip[:, None])
+    )(got, matrix, skip)
 
     home = lax.all_to_all(back, "seq", 0, 0, tiled=True)
     mixed_parts = [mixed] + [from_set(mixed, offset) for offset in range(1, sets)]
-    squares = home[:, channels:].astype(F32).reshape(2 * seq_count, seq_count, block)
+    squares = home[:, channels:].astype(F32).reshape(seq_count, seq_count, block)
     squares = jnp.sum(squares, axis=0)
     all_squares = [squares]
     for offset in range(1, chan_count):
@@ -379,7 +397,15 @@
     else:
         weights_shapes = [(length * step // steps, QUERY_BLOCK) for step in range(1, steps + 1)]
         vmem = 12
-        weights_grid = output_grid = {}
+        weights_grid = {}
+        output_grid = dict(
+            in_specs=[whole] * (chan_count + sets + 1 + steps),
+            out_specs=anywhere,
+        )
+        output_scratch = [
+            pltpu.VMEM((steps, QUERY_BLOCK, head_dim), BF16),
+            pltpu.SemaphoreType.DMA((steps,)),
+        ]
     keys, arranged = call(
         functools.partial(arrange_kernel, sets),
         [shape((seq_count, block, head_dim), BF16), shape((seq_count, rows, head_dim), BF16)],
@@ -409,9 +435,10 @@
         flops=query_len * length * head_dim,
         vmem=vmem,
         scratch_shapes=[
-            pltpu.VMEM((sets, channels, length), F32),
+            pltpu.VMEM((sets, channels, length if channels % 16 else block), F32),
             pltpu.VMEM((head_dim, length), BF16),
-        ],
+        ]
+        + ([] if gridded else output_scratch),
         **output_grid,
     )(*all_squares, *mixed_parts, totals, *weights)
 

time: 50.7 us -> 50.3 us (level)
    ppermute x3, waiting for transfers between devices: 8.6 us -> 7.82 us  [from_set(): return lax.ppermute(array, 'seq', pairs)]
    all_to_all x1, waiting for transfers between devices: 0.01 us -> 0.55 us  [shards(): got = lax.all_to_all(packed, 'seq', 0, 0, tiled=True)]
  transfers between devices with their start and end apart: 14 -> 14, of which waited for: 3 -> 4; matrix products, arithmetic and copies ran while one was open for 0% -> 0% of each run, Pallas kernels for 12% -> 12%
where the time goes in v5:
time: 50.3 us; the launch traced here: 50 us
  starting transfers between devices  25.5 us (51%)
  waiting for transfers between devices  13.6 us (27%)
  Pallas kernels  9.29 us (18%)
  local copies, waits for them, and re-layouts  0.77 us (2%)
  between operations  0.76 us (2%)
    ppermute x6, starting transfers between devices, from_head(): return lax.ppermute(array, 'seq', pairs)  11.7 us
    ppermute x3, waiting for transfers between devices, from_set(): return lax.ppermute(array, 'seq', pairs)  7.82 us
    all_to_all x1, waiting for transfers between devices, shards(): home = lax.all_to_all(back, 'seq', 0, 0, tiled=True)  5.02 us
    ppermute x3, starting transfers between devices, from_set(): return lax.ppermute(array, 'seq', pairs)  4.32 us
    all_to_all x1, starting transfers between devices, shards(): home = lax.all_to_all(back, 'seq', 0, 0, tiled=True)  4.03 us
    all_to_all x1, starting transfers between devices, shards(): got = lax.all_to_all(packed, 'seq', 0, 0, tiled=True)  3.62 us
    pallas_call x1, Pallas kernels, shards(): call(functools.partial(pack_kernel, sets, heads_loc), [shape((seq_count,...  2.19 us
    pallas_call x1, Pallas kernels, shards(): call(functools.partial(weights_kernel, gridded), [shape(total_shape, F32)...  1.84 us
  transfers between devices with their start and end apart: 14, of which 4 were waited for; matrix products, arithmetic and copies ran while one was open for 0% of the time, Pallas kernels for 12%

profile of v5, /device:TPU:0, one launch (start us, length us, event | category | flops | bytes accessed | tf_op | source)
XLA Modules:
  0.0 50.0 jit_solution(3970258921903695683)
XLA Ops:
  0.6 0.0 copy-start
  0.6 2.2 %shard_map.77 = (bf16[8,2,64,256]{3,2,1,0:T(8,128)(2,1)}, bf16[256,128]{1,0:T(8,128)(2,1)}, bf16[256,128]{1,0:T(8,128)(2,1)}, bf16[256,128]{1,0:T(8,128)(2,1)}, ...) custom-call(bf16[256,512]{1,0:T(8,128)(2,1)} %signal_ref.1, ...), custom_call_target="tpu_custom_call" | custom-call | bytes 2097152 | tf_op jit(solution)/shard_map/pallas_call | solution.py:314
  2.8 3.1 %collective-permute-start.4 = (bf16[256,128]{1,0:T(8,128)(2,1)}, bf16[256,128]{1,0:T(8,128)(2,1)S(1)}, u32[]{:S(2)}, u32[]{:S(2)}) collective-permute-start(bf16[256,128]{1,0:T(8,128)(2,1)} %get-tuple-element.26), channel_id=1, source_target_pairs={{0,8},{4,12},{8,16},{12,20},{16,24},{20,28},{24,0},{28,4},{1,9},{5... | collective-permute-start | bytes 196616 | tf_op jit(solution)/shard_map/ppermute | solution.py:311
  5.9 2.6 %collective-permute-start.5 = (bf16[256,128]{1,0:T(8,128)(2,1)}, bf16[256,128]{1,0:T(8,128)(2,1)S(1)}, u32[]{:S(2)}, u32[]{:S(2)}) collective-permute-start(bf16[256,128]{1,0:T(8,128)(2,1)} %get-tuple-element.27), channel_id=1, source_target_pairs={{0,16},{4,20},{8,24},{12,28},{16,0},{20,4},{24,8},{28,12},{1,17},{... | collective-permute-start | bytes 196616 | tf_op jit(solution)/shard_map/ppermute | solution.py:311
  8.5 1.3 %collective-permute-start.6 = (bf16[256,128]{1,0:T(8,128)(2,1)}, bf16[256,128]{1,0:T(8,128)(2,1)S(1)}, u32[]{:S(2)}, u32[]{:S(2)}) collective-permute-start(bf16[256,128]{1,0:T(8,128)(2,1)} %get-tuple-element.28), channel_id=1, source_target_pairs={{0,24},{4,28},{8,0},{12,4},{16,8},{20,12},{24,16},{28,20},{1,25},{... | collective-permute-start | bytes 196616 | tf_op jit(solution)/shard_map/ppermute | solution.py:311
  9.9 0.0 copy-start.4
  9.9 0.0 copy-start.2
  9.9 3.6 %all-to-all-start = ((bf16[8,2,64,256]{3,2,1,0:T(8,128)(2,1)}), bf16[8,2,64,256]{3,2,1,0:T(8,128)(2,1)S(1)}, u32[]{:S(2)}, u32[]{:S(2)}) async-start(bf16[8,2,64,256]{3,2,1,0:T(8,128)(2,1)} %get-tuple-element.22), calls=%async_computation | async-start | bytes 1048576 | tf_op jit(solution)/shard_map/all_to_all | solution.py:331
  13.5 0.0 copy-done.4
  13.5 1.9 %collective-permute-start.8 = (bf16[128,512]{1,0:T(8,128)(2,1)S(1)}, bf16[128,512]{1,0:T(8,128)(2,1)S(1)}, u32[]{:S(2)}, u32[]{:S(2)}) collective-permute-start(bf16[128,512]{1,0:T(8,128)(2,1)S(1)} %copy-done.4), channel_id=1, source_target_pairs={{4,0},{0,4},{12,8},{8,12},{20,16},{16,20},{28,24},{24,28},{5,1},{1... | collective-permute-start | bytes 393224 | tf_op jit(solution)/shard_map/ppermute | solution.py:307
  15.4 0.0 copy-done.2
  15.4 0.0 copy-start.3
  15.4 0.2 shard_map.78.matrix_ref.refs_4_
  15.7 0.0 collective-permute-done.4.refs_1_
  15.7 0.0 collective-permute-done.5.refs_2_
  15.7 0.0 collective-permute-done.6.refs_3_
  15.7 0.6 %copy-done.3 = bf16[256,128]{1,0:T(8,128)(2,1)S(1)} copy-done((bf16[256,128]{1,0:T(8,128)(2,1)S(1)}, bf16[256,128]{1,0:T(8,128)(2,1)}, u32[]{:S(2)}) %copy-start.3) | copy-done | bytes 65560
  16.3 0.0 copy-start.1
  16.3 0.4 shard_map.81.refs_0_
  16.6 0.2 collective-permute-start.7
  16.9 7.8 %collective-permute-done.8.refs_1_ = bf16[128,512]{1,0:T(8,128)(2,1)S(1)} collective-permute-done((bf16[128,512]{1,0:T(8,128)(2,1)S(1)}, bf16[128,512]{1,0:T(8,128)(2,1)S(1)}, u32[]{:S(2)}, u32[]{:S(2)}) %collective-permute-start.8) | collective-permute-done | bytes 131104 | tf_op jit(solution)/shard_map/ppermute | solution.py:307
  24.7 0.0 copy-done.1
  24.7 1.7 %collective-permute-start.9 = (bf16[2,128,128]{2,1,0:T(8,128)(2,1)S(1)}, bf16[2,128,128]{2,1,0:T(8,128)(2,1)S(1)}, u32[]{:S(2)}, u32[]{:S(2)}) collective-permute-start(bf16[2,128,128]{2,1,0:T(8,128)(2,1)S(1)} %get-tuple-element.32), channel_id=1, source_target_pairs={{0,8},{4,12},{8,16},{12,20},{16,24},{20,28},{24,0},{28,4},{1,9},{5... | collective-permute-start | bytes 196616 | tf_op jit(solution)/shard_map/ppermute | solution.py:311
  26.5 2.7 %collective-permute-start.10 = (bf16[2,128,128]{2,1,0:T(8,128)(2,1)S(1)}, bf16[2,128,128]{2,1,0:T(8,128)(2,1)S(1)}, u32[]{:S(2)}, u32[]{:S(2)}) collective-permute-start(bf16[2,128,128]{2,1,0:T(8,128)(2,1)S(1)} %get-tuple-element.33), channel_id=1, source_target_pairs={{0,16},{4,20},{8,24},{12,28},{16,0},{20,4},{24,8},{28,12},{1,17},{... | collective-permute-start | bytes 196616 | tf_op jit(solution)/shard_map/ppermute | solution.py:311
  29.1 0.3 collective-permute-start.11
  29.5 0.0 copy-done
  29.5 0.1 dynamic-slice_bitcast_fusion
  29.6 0.1 copy.8.skip_ref
  29.7 0.6 %all-to-all-done.got_ref = bf16[8,2,64,256]{3,2,1,0:T(8,128)(2,1)S(1)} async-done(((bf16[8,2,64,256]{3,2,1,0:T(8,128)(2,1)}), bf16[8,2,64,256]{3,2,1,0:T(8,128)(2,1)S(1)}, u32[]{:S(2)}, u32[]{:S(2)}) %all-to-all-start) | async-done | bytes 524320 | tf_op jit(solution)/shard_map/all_to_all | solution.py:331
  30.2 1.3 %shard_map.79 = (bf16[8,64,256]{2,1,0:T(8,128)(2,1)S(1)}, bf16[8,72,256]{2,1,0:T(8,128)(2,1)}) custom-call(bf16[8,2,64,256]{3,2,1,0:T(8,128)(2,1)S(1)} %all-to-all-done.got_ref, bf16[256,2048]{1,0:T(8,128)(2,1)S(1)} %shard_map.78.matrix_ref.refs_4_, f32[64,1]{1,0:T(8,128)S(1)} %copy.8.skip_ref), custom_call_target="tpu_custom_call" | custom-call | flops 268435456 | bytes 1310720 | tf_op jit(solution)/shard_map/pallas_call | solution.py:363
  31.5 4.0 %all-to-all-start.1 = ((bf16[8,72,256]{2,1,0:T(8,128)(2,1)}), bf16[8,72,256]{2,1,0:T(8,128)(2,1)S(1)}, u32[]{:S(2)}, u32[]{:S(2)}) async-start(bf16[8,72,256]{2,1,0:T(8,128)(2,1)} %get-tuple-element.23), calls=%async_computation.1 | async-start | bytes 589824 | tf_op jit(solution)/shard_map/all_to_all | solution.py:375
  35.5 2.2 %collective-permute-start.3 = (bf16[8,64,256]{2,1,0:T(8,128)(2,1)S(1)}, bf16[8,64,256]{2,1,0:T(8,128)(2,1)S(1)}, u32[]{:S(2)}, u32[]{:S(2)}) collective-permute-start(bf16[8,64,256]{2,1,0:T(8,128)(2,1)S(1)} %get-tuple-element.24.refs_4_), channel_id=1, source_target_pairs={{4,0},{0,4},{12,8},{8,12},{20,16},{16,20},{28,24},{24,28},{5,1},{1... | collective-permute-start | bytes 786440 | tf_op jit(solution)/shard_map/ppermute | solution.py:307
  37.7 0.0 collective-permute-done.9.refs_3_
  37.7 0.0 collective-permute-done.10.refs_4_
  37.7 0.0 collective-permute-done.11.refs_5_
  37.7 0.0 collective-permute-done.7.refs_1_
  37.7 1.2 %shard_map.83 = (bf16[8,256,128]{2,1,0:T(8,128)(2,1)S(1)}, bf16[8,128,128]{2,1,0:T(8,128)(2,1)S(1)}) custom-call(bf16[4,256,128]{2,1,0:T(8,128)(2,1)S(1)} %shard_map.81.refs_0_, bf16[4,256,128]{2,1,0:T(8,128)(2,1)S(1)} %collective-permute-done.7.refs_1_, bf16[2,128,128]{2,1,0:T(8,128)(2,1)S(1)} %get-tuple-element.31.refs_2_, ...), custom_call_target="tpu_custom_call" | custom-call | flops 40000000000 | bytes 1572864 | tf_op jit(solution)/shard_map/pallas_call | solution.py:409
  38.9 5.0 %all-to-all-done.1.got_ref = bf16[8,72,256]{2,1,0:T(8,128)(2,1)S(1)} async-done(((bf16[8,72,256]{2,1,0:T(8,128)(2,1)}), bf16[8,72,256]{2,1,0:T(8,128)(2,1)S(1)}, u32[]{:S(2)}, u32[]{:S(2)}) %all-to-all-start.1) | async-done | bytes 294944 | tf_op jit(solution)/shard_map/all_to_all | solution.py:375
  44.0 0.1 collective-permute-start.2
  44.0 1.6 %collective-permute-start.1 = (f32[8,256]{1,0:T(8,128)S(1)}, f32[8,256]{1,0:T(8,128)S(1)}, u32[]{:S(2)}, u32[]{:S(2)}) collective-permute-start(f32[8,256]{1,0:T(8,128)S(1)} %convert_reduce_fusion.refs_0_), channel_id=1, source_target_pairs={{0,2},{1,3},{2,0},{3,1},{4,6},{5,7},{6,4},{7,5},{8,10},{9,11},{10,... | collective-permute-start | bytes 24584 | tf_op jit(solution)/shard_map/ppermute | solution.py:382
  45.6 0.2 collective-permute-start
  45.8 1.8 %shard_map.84 = (f32[4,8,256]{2,1,0:T(8,128)S(1)}, bf16[512,256]{1,0:T(8,128)(2,1)S(1)}, bf16[1024,256]{1,0:T(8,128)(2,1)S(1)}, bf16[1536,256]{1,0:T(8,128)(2,1)S(1)}, bf16[2048,256]{1,0:T(8,128)(2,1)S(1)}) custom-call(bf16[8,256,128]{2,1,0:T(8,128)(2,1)S(1)} %get-tuple-element.35.key_ref, bf16[8,128,128]{2,1,0:T(8,128)(2,1)S(1)} %get-tuple-element.36.query_ref), custom_call_target="tpu_custom_call" | custom-call | flops 268435456 | bytes 2621440 | tf_op jit(solution)/shard_map/pallas_call | solution.py:418
  47.6 0.8 %shard_map.80 = bf16[256,512]{1,0:T(8,128)(2,1)} custom-call(bf16[8,72,256]{2,1,0:T(8,128)(2,1)S(1)} %all-to-all-done.1.got_ref), custom_call_target="tpu_custom_call" | custom-call | bytes 524288 | tf_op jit(solution)/shard_map/pallas_call | solution.py:445
  48.4 0.0 collective-permute-done.3.refs_5_
  48.4 0.0 collective-permute-done.2.refs_3_
  48.5 0.0 collective-permute-done.1.refs_2_
  48.5 0.2 collective-permute-done.refs_1_
  48.7 1.3 %shard_map.85 = bf16[1024,128]{1,0:T(8,128)(2,1)} custom-call(f32[8,256]{1,0:T(8,128)S(1)} %convert_reduce_fusion.refs_0_, f32[8,256]{1,0:T(8,128)S(1)} %collective-permute-done.refs_1_, f32[8,256]{1,0:T(8,128)S(1)} %collective-permute-done.1.refs_2_, f32[8,256]{1,0:T(8,128)S(1)} %collective-permute-done.2.refs_3_, ...), custom_call_target="tpu_custom_call" | custom-call | flops 268435456 | bytes 2621440 | tf_op jit(solution)/shard_map/pallas_call | solution.py:431
  (2 shorter events, 0.1 us)
Async XLA Ops:
  0.6 28.8 %copy-start = (f32[512]{0:T(512)S(1)}, f32[512]{0:T(512)}, u32[]{:S(2)}) copy-start(f32[512]{0:T(512)} %param.8) | copy-start | bytes 6148
  2.8 12.8 %collective-permute-start.4 = (bf16[256,128]{1,0:T(8,128)(2,1)}, bf16[256,128]{1,0:T(8,128)(2,1)S(1)}, u32[]{:S(2)}, u32[]{:S(2)}) collective-permute-start(bf16[256,128]{1,0:T(8,128)(2,1)} %get-tuple-element.26), channel_id=1, source_target_pairs={{0,8},{4,12},{8,16},{12,20},{16,24},{20,28},{24,0},{28,4},{1,9},{5... | collective-permute-start | bytes 196616 | tf_op jit(solution)/shard_map/ppermute | solution.py:311
  5.9 9.7 %collective-permute-start.5 = (bf16[256,128]{1,0:T(8,128)(2,1)}, bf16[256,128]{1,0:T(8,128)(2,1)S(1)}, u32[]{:S(2)}, u32[]{:S(2)}) collective-permute-start(bf16[256,128]{1,0:T(8,128)(2,1)} %get-tuple-element.27), channel_id=1, source_target_pairs={{0,16},{4,20},{8,24},{12,28},{16,0},{20,4},{24,8},{28,12},{1,17},{... | collective-permute-start | bytes 196616 | tf_op jit(solution)/shard_map/ppermute | solution.py:311
  8.5 7.2 %collective-permute-start.6 = (bf16[256,128]{1,0:T(8,128)(2,1)}, bf16[256,128]{1,0:T(8,128)(2,1)S(1)}, u32[]{:S(2)}, u32[]{:S(2)}) collective-permute-start(bf16[256,128]{1,0:T(8,128)(2,1)} %get-tuple-element.28), channel_id=1, source_target_pairs={{0,24},{4,28},{8,0},{12,4},{16,8},{20,12},{24,16},{28,20},{1,25},{... | collective-permute-start | bytes 196616 | tf_op jit(solution)/shard_map/ppermute | solution.py:311
  9.9 3.6 %copy-start.4 = (bf16[128,512]{1,0:T(8,128)(2,1)S(1)}, bf16[128,512]{1,0:T(8,128)(2,1)}, u32[]{:S(2)}) copy-start(bf16[128,512]{1,0:T(8,128)(2,1)} %get-tuple-element.30) | copy-start | bytes 393220
  9.9 5.6 %copy-start.2 = (bf16[2048,4]{0,1:T(4,128)(2,1)S(1)}, bf16[2048,4]{0,1:T(4,128)(2,1)}, u32[]{:S(2)}) copy-start(bf16[2048,4]{0,1:T(4,128)(2,1)} %param.9) | copy-start | bytes 49156
  9.9 20.3 %all-to-all-start = ((bf16[8,2,64,256]{3,2,1,0:T(8,128)(2,1)}), bf16[8,2,64,256]{3,2,1,0:T(8,128)(2,1)S(1)}, u32[]{:S(2)}, u32[]{:S(2)}) async-start(bf16[8,2,64,256]{3,2,1,0:T(8,128)(2,1)} %get-tuple-element.22), calls=%async_computation | async-start | bytes 1048576 | tf_op jit(solution)/shard_map/all_to_all | solution.py:331
  13.5 11.2 %collective-permute-start.8 = (bf16[128,512]{1,0:T(8,128)(2,1)S(1)}, bf16[128,512]{1,0:T(8,128)(2,1)S(1)}, u32[]{:S(2)}, u32[]{:S(2)}) collective-permute-start(bf16[128,512]{1,0:T(8,128)(2,1)S(1)} %copy-done.4), channel_id=1, source_target_pairs={{4,0},{0,4},{12,8},{8,12},{20,16},{16,20},{28,24},{24,28},{5,1},{1... | collective-permute-start | bytes 393224 | tf_op jit(solution)/shard_map/ppermute | solution.py:307
  15.4 0.8 %copy-start.3 = (bf16[256,128]{1,0:T(8,128)(2,1)S(1)}, bf16[256,128]{1,0:T(8,128)(2,1)}, u32[]{:S(2)}) copy-start(bf16[256,128]{1,0:T(8,128)(2,1)} %get-tuple-element.25.refs_0_) | copy-start | bytes 196612
  16.3 8.4 %copy-start.1 = (bf16[128,512]{1,0:T(8,128)(2,1)S(1)}, bf16[128,512]{1,0:T(8,128)(2,1)}, u32[]{:S(2)}) copy-start(bf16[128,512]{1,0:T(8,128)(2,1)} %get-tuple-element.29.refs_0_) | copy-start | bytes 393220
  16.6 21.1 %collective-permute-start.7 = (bf16[4,256,128]{2,1,0:T(8,128)(2,1)S(1)}, bf16[4,256,128]{2,1,0:T(8,128)(2,1)S(1)}, u32[]{:S(2)}, u32[]{:S(2)}) collective-permute-start(bf16[4,256,128]{2,1,0:T(8,128)(2,1)S(1)} %shard_map.81.refs_0_), channel_id=1, source_target_pairs={{4,0},{0,4},{12,8},{8,12},{20,16},{16,20},{28,24},{24,28},{5,1},{1... | collective-permute-start | bytes 786440 | tf_op jit(solution)/shard_map/ppermute | solution.py:307
  24.7 12.9 %collective-permute-start.9 = (bf16[2,128,128]{2,1,0:T(8,128)(2,1)S(1)}, bf16[2,128,128]{2,1,0:T(8,128)(2,1)S(1)}, u32[]{:S(2)}, u32[]{:S(2)}) collective-permute-start(bf16[2,128,128]{2,1,0:T(8,128)(2,1)S(1)} %get-tuple-element.32), channel_id=1, source_target_pairs={{0,8},{4,12},{8,16},{12,20},{16,24},{20,28},{24,0},{28,4},{1,9},{5... | collective-permute-start | bytes 196616 | tf_op jit(solution)/shard_map/ppermute | solution.py:311
  26.5 11.2 %collective-permute-start.10 = (bf16[2,128,128]{2,1,0:T(8,128)(2,1)S(1)}, bf16[2,128,128]{2,1,0:T(8,128)(2,1)S(1)}, u32[]{:S(2)}, u32[]{:S(2)}) collective-permute-start(bf16[2,128,128]{2,1,0:T(8,128)(2,1)S(1)} %get-tuple-element.33), channel_id=1, source_target_pairs={{0,16},{4,20},{8,24},{12,28},{16,0},{20,4},{24,8},{28,12},{1,17},{... | collective-permute-start | bytes 196616 | tf_op jit(solution)/shard_map/ppermute | solution.py:311
  29.1 8.5 %collective-permute-start.11 = (bf16[2,128,128]{2,1,0:T(8,128)(2,1)S(1)}, bf16[2,128,128]{2,1,0:T(8,128)(2,1)S(1)}, u32[]{:S(2)}, u32[]{:S(2)}) collective-permute-start(bf16[2,128,128]{2,1,0:T(8,128)(2,1)S(1)} %get-tuple-element.34), channel_id=1, source_target_pairs={{0,24},{4,28},{8,0},{12,4},{16,8},{20,12},{24,16},{28,20},{1,25},{... | collective-permute-start | bytes 196616 | tf_op jit(solution)/shard_map/ppermute | solution.py:311
  31.5 12.5 %all-to-all-start.1 = ((bf16[8,72,256]{2,1,0:T(8,128)(2,1)}), bf16[8,72,256]{2,1,0:T(8,128)(2,1)S(1)}, u32[]{:S(2)}, u32[]{:S(2)}) async-start(bf16[8,72,256]{2,1,0:T(8,128)(2,1)} %get-tuple-element.23), calls=%async_computation.1 | async-start | bytes 589824 | tf_op jit(solution)/shard_map/all_to_all | solution.py:375
  35.5 12.9 %collective-permute-start.3 = (bf16[8,64,256]{2,1,0:T(8,128)(2,1)S(1)}, bf16[8,64,256]{2,1,0:T(8,128)(2,1)S(1)}, u32[]{:S(2)}, u32[]{:S(2)}) collective-permute-start(bf16[8,64,256]{2,1,0:T(8,128)(2,1)S(1)} %get-tuple-element.24.refs_4_), channel_id=1, source_target_pairs={{4,0},{0,4},{12,8},{8,12},{20,16},{16,20},{28,24},{24,28},{5,1},{1... | collective-permute-start | bytes 786440 | tf_op jit(solution)/shard_map/ppermute | solution.py:307
  44.0 4.5 %collective-permute-start.2 = (f32[8,256]{1,0:T(8,128)S(1)}, f32[8,256]{1,0:T(8,128)S(1)}, u32[]{:S(2)}, u32[]{:S(2)}) collective-permute-start(f32[8,256]{1,0:T(8,128)S(1)} %convert_reduce_fusion.refs_0_), channel_id=1, source_target_pairs={{0,3},{1,0},{2,1},{3,2},{4,7},{5,4},{6,5},{7,6},{8,11},{9,8},{10,9... | collective-permute-start | bytes 24584 | tf_op jit(solution)/shard_map/ppermute | solution.py:382
  44.0 4.4 %collective-permute-start.1 = (f32[8,256]{1,0:T(8,128)S(1)}, f32[8,256]{1,0:T(8,128)S(1)}, u32[]{:S(2)}, u32[]{:S(2)}) collective-permute-start(f32[8,256]{1,0:T(8,128)S(1)} %convert_reduce_fusion.refs_0_), channel_id=1, source_target_pairs={{0,2},{1,3},{2,0},{3,1},{4,6},{5,7},{6,4},{7,5},{8,10},{9,11},{10,... | collective-permute-start | bytes 24584 | tf_op jit(solution)/shard_map/ppermute | solution.py:382
  45.6 3.1 %collective-permute-start = (f32[8,256]{1,0:T(8,128)S(1)}, f32[8,256]{1,0:T(8,128)S(1)}, u32[]{:S(2)}, u32[]{:S(2)}) collective-permute-start(f32[8,256]{1,0:T(8,128)S(1)} %convert_reduce_fusion.refs_0_), channel_id=1, source_target_pairs={{0,1},{1,2},{2,3},{3,0},{4,5},{5,6},{6,7},{7,4},{8,9},{9,10},{10,1... | collective-permute-start | bytes 24584 | tf_op jit(solution)/shard_map/ppermute | solution.py:382

commit v6 on v5

--- a/solution.py
+++ b/solution.py
@@ -98,6 +98,10 @@
         copy.start()
     for copy in copies:
         copy.wait()
+
+
+def squares_kernel(rows, home_ref, after_ref, squares_ref):
+    squares_ref[...] = jnp.sum(home_ref[:, rows:].astype(F32), axis=0)
 
 
 def arrange_kernel(sets, *refs):
@@ -374,13 +378,6 @@
 
     home = lax.all_to_all(back, "seq", 0, 0, tiled=True)
     mixed_parts = [mixed] + [from_set(mixed, offset) for offset in range(1, sets)]
-    squares = home[:, channels:].astype(F32).reshape(seq_count, seq_count, block)
-    squares = jnp.sum(squares, axis=0)
-    all_squares = [squares]
-    for offset in range(1, chan_count):
-        pairs = [(source, (source + offset) % chan_count) for source in range(chan_count)]
-        all_squares.append(lax.ppermute(squares, "chan", pairs))
-
     total_shape = (steps, 8, QUERY_BLOCK)
     one = lambda dims: pl.BlockSpec((1,) + dims[1:], lambda step: (step, 0, 0))
     whole = pl.BlockSpec(memory_space=pltpu.VMEM)
@@ -428,6 +425,18 @@
         **weights_grid,
     )(keys, arranged)
 
+    squares = call(
+        functools.partial(squares_kernel, channels),
+        shape((seq_count, block), F32),
+        moved=4 * length,
+        in_specs=[whole, anywhere],
+        vmem=8 if not gridded else 56,
+    )(home, totals)
+    all_squares = [squares]
+    for offset in range(1, chan_count):
+        pairs = [(source, (source + offset) % chan_count) for source in range(chan_count)]
+        all_squares.append(lax.ppermute(squares, "chan", pairs))
+
     attended = call(
         functools.partial(output_kernel, sets, steps, local_width * chan_count, gridded),
         shape((query_len, head_dim), BF16),

time: 50.3 us -> 50.2 us (level)
  waiting for transfers between devices: 13.6 us -> 12.1 us
  starting transfers between devices: 25.5 us -> 26.7 us
    all_to_all x1, waiting for transfers between devices: 5.02 us -> 3.18 us  [shards(): home = lax.all_to_all(back, 'seq', 0, 0, tiled=True)]
    ppermute x3, starting transfers between devices: 1.78 us -> 3 us  [shards(): all_squares.append(lax.ppermute(squares, 'chan', pairs))]
where the time goes in v6:
time: 50.2 us; the launch traced here: 49.6 us
  starting transfers between devices  26.7 us (53%)
  waiting for transfers between devices  12.1 us (24%)
  Pallas kernels  9.3 us (19%)
  local copies, waits for them, and re-layouts  0.77 us (2%)
  between operations  0.76 us (2%)
    ppermute x6, starting transfers between devices, from_head(): return lax.ppermute(array, 'seq', pairs)  11.7 us
    ppermute x3, waiting for transfers between devices, from_set(): return lax.ppermute(array, 'seq', pairs)  7.82 us
    ppermute x3, starting transfers between devices, from_set(): return lax.ppermute(array, 'seq', pairs)  4.32 us
    all_to_all x1, starting transfers between devices, shards(): home = lax.all_to_all(back, 'seq', 0, 0, tiled=True)  4.03 us
    all_to_all x1, starting transfers between devices, shards(): got = lax.all_to_all(packed, 'seq', 0, 0, tiled=True)  3.62 us
    all_to_all x1, waiting for transfers between devices, shards(): home = lax.all_to_all(back, 'seq', 0, 0, tiled=True)  3.18 us
    ppermute x3, starting transfers between devices, shards(): all_squares.append(lax.ppermute(squares, 'chan', pairs))  3 us
    pallas_call x1, Pallas kernels, shards(): call(functools.partial(pack_kernel, sets, heads_loc), [shape((seq_count,...  2.2 us
  transfers between devices with their start and end apart: 14, of which 4 were waited for; matrix products, arithmetic and copies ran while one was open for 0% of the time, Pallas kernels for 12%

profile of v6, /device:TPU:0, one launch (start us, length us, event | category | flops | bytes accessed | tf_op | source)
XLA Modules:
  0.0 49.6 jit_solution(1916299083242238864)
XLA Ops:
  0.6 0.0 copy-start
  0.6 2.2 %shard_map.77 = (bf16[8,2,64,256]{3,2,1,0:T(8,128)(2,1)}, bf16[256,128]{1,0:T(8,128)(2,1)}, bf16[256,128]{1,0:T(8,128)(2,1)}, bf16[256,128]{1,0:T(8,128)(2,1)}, ...) custom-call(bf16[256,512]{1,0:T(8,128)(2,1)} %signal_ref.1, ...), custom_call_target="tpu_custom_call" | custom-call | bytes 2097152 | tf_op jit(solution)/shard_map/pallas_call | solution.py:318
  2.9 3.1 %collective-permute-start = (bf16[256,128]{1,0:T(8,128)(2,1)}, bf16[256,128]{1,0:T(8,128)(2,1)S(1)}, u32[]{:S(2)}, u32[]{:S(2)}) collective-permute-start(bf16[256,128]{1,0:T(8,128)(2,1)} %get-tuple-element.25), channel_id=1, source_target_pairs={{0,8},{4,12},{8,16},{12,20},{16,24},{20,28},{24,0},{28,4},{1,9},{5... | collective-permute-start | bytes 196616 | tf_op jit(solution)/shard_map/ppermute | solution.py:315
  5.9 2.6 %collective-permute-start.1 = (bf16[256,128]{1,0:T(8,128)(2,1)}, bf16[256,128]{1,0:T(8,128)(2,1)S(1)}, u32[]{:S(2)}, u32[]{:S(2)}) collective-permute-start(bf16[256,128]{1,0:T(8,128)(2,1)} %get-tuple-element.26), channel_id=1, source_target_pairs={{0,16},{4,20},{8,24},{12,28},{16,0},{20,4},{24,8},{28,12},{1,17},{... | collective-permute-start | bytes 196616 | tf_op jit(solution)/shard_map/ppermute | solution.py:315
  8.5 1.3 %collective-permute-start.2 = (bf16[256,128]{1,0:T(8,128)(2,1)}, bf16[256,128]{1,0:T(8,128)(2,1)S(1)}, u32[]{:S(2)}, u32[]{:S(2)}) collective-permute-start(bf16[256,128]{1,0:T(8,128)(2,1)} %get-tuple-element.27), channel_id=1, source_target_pairs={{0,24},{4,28},{8,0},{12,4},{16,8},{20,12},{24,16},{28,20},{1,25},{... | collective-permute-start | bytes 196616 | tf_op jit(solution)/shard_map/ppermute | solution.py:315
  9.9 0.0 copy-start.4
  9.9 0.0 copy-start.2
  9.9 3.6 %all-to-all-start = ((bf16[8,2,64,256]{3,2,1,0:T(8,128)(2,1)}), bf16[8,2,64,256]{3,2,1,0:T(8,128)(2,1)S(1)}, u32[]{:S(2)}, u32[]{:S(2)}) async-start(bf16[8,2,64,256]{3,2,1,0:T(8,128)(2,1)} %get-tuple-element.22), calls=%async_computation | async-start | bytes 1048576 | tf_op jit(solution)/shard_map/all_to_all | solution.py:335
  13.5 0.0 copy-done.4
  13.5 1.9 %collective-permute-start.4 = (bf16[128,512]{1,0:T(8,128)(2,1)S(1)}, bf16[128,512]{1,0:T(8,128)(2,1)S(1)}, u32[]{:S(2)}, u32[]{:S(2)}) collective-permute-start(bf16[128,512]{1,0:T(8,128)(2,1)S(1)} %copy-done.4), channel_id=1, source_target_pairs={{4,0},{0,4},{12,8},{8,12},{20,16},{16,20},{28,24},{24,28},{5,1},{1... | collective-permute-start | bytes 393224 | tf_op jit(solution)/shard_map/ppermute | solution.py:311
  15.4 0.0 copy-done.2
  15.4 0.0 copy-start.3
  15.4 0.2 shard_map.78.matrix_ref.refs_4_
  15.7 0.0 collective-permute-done.refs_1_
  15.7 0.0 collective-permute-done.1.refs_2_
  15.7 0.0 collective-permute-done.2.refs_3_
  15.7 0.6 %copy-done.3 = bf16[256,128]{1,0:T(8,128)(2,1)S(1)} copy-done((bf16[256,128]{1,0:T(8,128)(2,1)S(1)}, bf16[256,128]{1,0:T(8,128)(2,1)}, u32[]{:S(2)}) %copy-start.3) | copy-done | bytes 65560
  16.3 0.0 copy-start.1
  16.3 0.4 shard_map.81.refs_0_
  16.6 0.2 collective-permute-start.3
  16.9 7.8 %collective-permute-done.4.refs_1_ = bf16[128,512]{1,0:T(8,128)(2,1)S(1)} collective-permute-done((bf16[128,512]{1,0:T(8,128)(2,1)S(1)}, bf16[128,512]{1,0:T(8,128)(2,1)S(1)}, u32[]{:S(2)}, u32[]{:S(2)}) %collective-permute-start.4) | collective-permute-done | bytes 131104 | tf_op jit(solution)/shard_map/ppermute | solution.py:311
  24.7 0.0 copy-done.1
  24.8 1.7 %collective-permute-start.5 = (bf16[2,128,128]{2,1,0:T(8,128)(2,1)S(1)}, bf16[2,128,128]{2,1,0:T(8,128)(2,1)S(1)}, u32[]{:S(2)}, u32[]{:S(2)}) collective-permute-start(bf16[2,128,128]{2,1,0:T(8,128)(2,1)S(1)} %get-tuple-element.31), channel_id=1, source_target_pairs={{0,8},{4,12},{8,16},{12,20},{16,24},{20,28},{24,0},{28,4},{1,9},{5... | collective-permute-start | bytes 196616 | tf_op jit(solution)/shard_map/ppermute | solution.py:315
  26.5 2.7 %collective-permute-start.6 = (bf16[2,128,128]{2,1,0:T(8,128)(2,1)S(1)}, bf16[2,128,128]{2,1,0:T(8,128)(2,1)S(1)}, u32[]{:S(2)}, u32[]{:S(2)}) collective-permute-start(bf16[2,128,128]{2,1,0:T(8,128)(2,1)S(1)} %get-tuple-element.32), channel_id=1, source_target_pairs={{0,16},{4,20},{8,24},{12,28},{16,0},{20,4},{24,8},{28,12},{1,17},{... | collective-permute-start | bytes 196616 | tf_op jit(solution)/shard_map/ppermute | solution.py:315
  29.2 0.3 collective-permute-start.7
  29.5 0.0 copy-done
  29.5 0.1 dynamic-slice_bitcast_fusion
  29.6 0.1 copy.8.skip_ref
  29.7 0.6 %all-to-all-done.got_ref = bf16[8,2,64,256]{3,2,1,0:T(8,128)(2,1)S(1)} async-done(((bf16[8,2,64,256]{3,2,1,0:T(8,128)(2,1)}), bf16[8,2,64,256]{3,2,1,0:T(8,128)(2,1)S(1)}, u32[]{:S(2)}, u32[]{:S(2)}) %all-to-all-start) | async-done | bytes 524320 | tf_op jit(solution)/shard_map/all_to_all | solution.py:335
  30.2 1.3 %shard_map.79 = (bf16[8,64,256]{2,1,0:T(8,128)(2,1)S(1)}, bf16[8,72,256]{2,1,0:T(8,128)(2,1)}) custom-call(bf16[8,2,64,256]{3,2,1,0:T(8,128)(2,1)S(1)} %all-to-all-done.got_ref, bf16[256,2048]{1,0:T(8,128)(2,1)S(1)} %shard_map.78.matrix_ref.refs_4_, f32[64,1]{1,0:T(8,128)S(1)} %copy.8.skip_ref), custom_call_target="tpu_custom_call" | custom-call | flops 268435456 | bytes 1310720 | tf_op jit(solution)/shard_map/pallas_call | solution.py:367
  31.5 4.0 %all-to-all-start.1 = ((bf16[8,72,256]{2,1,0:T(8,128)(2,1)}), bf16[8,72,256]{2,1,0:T(8,128)(2,1)S(1)}, u32[]{:S(2)}, u32[]{:S(2)}) async-start(bf16[8,72,256]{2,1,0:T(8,128)(2,1)} %get-tuple-element.23), calls=%async_computation.1 | async-start | bytes 589824 | tf_op jit(solution)/shard_map/all_to_all | solution.py:379
  35.5 2.2 %collective-permute-start.11 = (bf16[8,64,256]{2,1,0:T(8,128)(2,1)S(1)}, bf16[8,64,256]{2,1,0:T(8,128)(2,1)S(1)}, u32[]{:S(2)}, u32[]{:S(2)}) collective-permute-start(bf16[8,64,256]{2,1,0:T(8,128)(2,1)S(1)} %get-tuple-element.37.refs_4_), channel_id=1, source_target_pairs={{4,0},{0,4},{12,8},{8,12},{20,16},{16,20},{28,24},{24,28},{5,1},{1... | collective-permute-start | bytes 786440 | tf_op jit(solution)/shard_map/ppermute | solution.py:311
  37.7 0.0 collective-permute-done.5.refs_3_
  37.7 0.0 collective-permute-done.6.refs_4_
  37.7 0.0 collective-permute-done.7.refs_5_
  37.7 0.0 collective-permute-done.3.refs_1_
  37.7 1.2 %shard_map.83 = (bf16[8,256,128]{2,1,0:T(8,128)(2,1)S(1)}, bf16[8,128,128]{2,1,0:T(8,128)(2,1)S(1)}) custom-call(bf16[4,256,128]{2,1,0:T(8,128)(2,1)S(1)} %shard_map.81.refs_0_, bf16[4,256,128]{2,1,0:T(8,128)(2,1)S(1)} %collective-permute-done.3.refs_1_, bf16[2,128,128]{2,1,0:T(8,128)(2,1)S(1)} %get-tuple-element.30.refs_2_, ...), custom_call_target="tpu_custom_call" | custom-call | flops 40000000000 | bytes 1572864 | tf_op jit(solution)/shard_map/pallas_call | solution.py:406
  38.9 1.8 %shard_map.84 = (f32[4,8,256]{2,1,0:T(8,128)S(1)}, bf16[512,256]{1,0:T(8,128)(2,1)S(1)}, bf16[1024,256]{1,0:T(8,128)(2,1)S(1)}, bf16[1536,256]{1,0:T(8,128)(2,1)S(1)}, bf16[2048,256]{1,0:T(8,128)(2,1)S(1)}) custom-call(bf16[8,256,128]{2,1,0:T(8,128)(2,1)S(1)} %get-tuple-element.34.key_ref, bf16[8,128,128]{2,1,0:T(8,128)(2,1)S(1)} %get-tuple-element.35.query_ref), custom_call_target="tpu_custom_call" | custom-call | flops 268435456 | bytes 2621440 | tf_op jit(solution)/shard_map/pallas_call | solution.py:415
  40.8 3.2 %all-to-all-done.1.got_ref.home_ref = bf16[8,72,256]{2,1,0:T(8,128)(2,1)S(1)} async-done(((bf16[8,72,256]{2,1,0:T(8,128)(2,1)}), bf16[8,72,256]{2,1,0:T(8,128)(2,1)S(1)}, u32[]{:S(2)}, u32[]{:S(2)}) %all-to-all-start.1) | async-done | bytes 294944 | tf_op jit(solution)/shard_map/all_to_all | solution.py:379
  44.0 0.1 collective-permute-start.8
  44.0 1.6 %collective-permute-start.9 = (f32[8,256]{1,0:T(8,128)S(1)}, f32[8,256]{1,0:T(8,128)S(1)}, u32[]{:S(2)}, u32[]{:S(2)}) collective-permute-start(f32[8,256]{1,0:T(8,128)S(1)} %shard_map.85.refs_0_), channel_id=1, source_target_pairs={{0,2},{1,3},{2,0},{3,1},{4,6},{5,7},{6,4},{7,5},{8,10},{9,11},{10,... | collective-permute-start | bytes 24584 | tf_op jit(solution)/shard_map/ppermute | solution.py:438
  45.6 1.4 %collective-permute-start.10 = (f32[8,256]{1,0:T(8,128)S(1)}, f32[8,256]{1,0:T(8,128)S(1)}, u32[]{:S(2)}, u32[]{:S(2)}) collective-permute-start(f32[8,256]{1,0:T(8,128)S(1)} %shard_map.85.refs_0_), channel_id=1, source_target_pairs={{0,3},{1,0},{2,1},{3,2},{4,7},{5,4},{6,5},{7,6},{8,11},{9,8},{10,9... | collective-permute-start | bytes 24584 | tf_op jit(solution)/shard_map/ppermute | solution.py:438
  47.0 0.8 %shard_map.80 = bf16[256,512]{1,0:T(8,128)(2,1)} custom-call(bf16[8,72,256]{2,1,0:T(8,128)(2,1)S(1)} %all-to-all-done.1.got_ref.home_ref), custom_call_target="tpu_custom_call" | custom-call | bytes 524288 | tf_op jit(solution)/shard_map/pallas_call | solution.py:454
  47.8 0.0 collective-permute-done.11.refs_5_
  47.8 0.0 collective-permute-done.8.refs_1_
  47.8 0.0 collective-permute-done.9.refs_2_
  47.8 0.5 %collective-permute-done.10.refs_3_ = f32[8,256]{1,0:T(8,128)S(1)} collective-permute-done((f32[8,256]{1,0:T(8,128)S(1)}, f32[8,256]{1,0:T(8,128)S(1)}, u32[]{:S(2)}, u32[]{:S(2)}) %collective-permute-start.10) | collective-permute-done | bytes 8224 | tf_op jit(solution)/shard_map/ppermute | solution.py:438
  48.3 1.3 %shard_map.86 = bf16[1024,128]{1,0:T(8,128)(2,1)} custom-call(f32[8,256]{1,0:T(8,128)S(1)} %shard_map.85.refs_0_, f32[8,256]{1,0:T(8,128)S(1)} %collective-permute-done.8.refs_1_, f32[8,256]{1,0:T(8,128)S(1)} %collective-permute-done.9.refs_2_, f32[8,256]{1,0:T(8,128)S(1)} %collective-permute-done.10.refs_3_, ...), custom_call_target="tpu_custom_call" | custom-call | flops 268435456 | bytes 2621440 | tf_op jit(solution)/shard_map/pallas_call | solution.py:440
  (2 shorter events, 0.1 us)
Async XLA Ops:
  0.6 28.9 %copy-start = (f32[512]{0:T(512)S(1)}, f32[512]{0:T(512)}, u32[]{:S(2)}) copy-start(f32[512]{0:T(512)} %param.8) | copy-start | bytes 6148
  2.9 12.8 %collective-permute-start = (bf16[256,128]{1,0:T(8,128)(2,1)}, bf16[256,128]{1,0:T(8,128)(2,1)S(1)}, u32[]{:S(2)}, u32[]{:S(2)}) collective-permute-start(bf16[256,128]{1,0:T(8,128)(2,1)} %get-tuple-element.25), channel_id=1, source_target_pairs={{0,8},{4,12},{8,16},{12,20},{16,24},{20,28},{24,0},{28,4},{1,9},{5... | collective-permute-start | bytes 196616 | tf_op jit(solution)/shard_map/ppermute | solution.py:315
  5.9 9.7 %collective-permute-start.1 = (bf16[256,128]{1,0:T(8,128)(2,1)}, bf16[256,128]{1,0:T(8,128)(2,1)S(1)}, u32[]{:S(2)}, u32[]{:S(2)}) collective-permute-start(bf16[256,128]{1,0:T(8,128)(2,1)} %get-tuple-element.26), channel_id=1, source_target_pairs={{0,16},{4,20},{8,24},{12,28},{16,0},{20,4},{24,8},{28,12},{1,17},{... | collective-permute-start | bytes 196616 | tf_op jit(solution)/shard_map/ppermute | solution.py:315
  8.5 7.2 %collective-permute-start.2 = (bf16[256,128]{1,0:T(8,128)(2,1)}, bf16[256,128]{1,0:T(8,128)(2,1)S(1)}, u32[]{:S(2)}, u32[]{:S(2)}) collective-permute-start(bf16[256,128]{1,0:T(8,128)(2,1)} %get-tuple-element.27), channel_id=1, source_target_pairs={{0,24},{4,28},{8,0},{12,4},{16,8},{20,12},{24,16},{28,20},{1,25},{... | collective-permute-start | bytes 196616 | tf_op jit(solution)/shard_map/ppermute | solution.py:315
  9.9 3.6 %copy-start.4 = (bf16[128,512]{1,0:T(8,128)(2,1)S(1)}, bf16[128,512]{1,0:T(8,128)(2,1)}, u32[]{:S(2)}) copy-start(bf16[128,512]{1,0:T(8,128)(2,1)} %get-tuple-element.29) | copy-start | bytes 393220
  9.9 5.6 %copy-start.2 = (bf16[2048,4]{0,1:T(4,128)(2,1)S(1)}, bf16[2048,4]{0,1:T(4,128)(2,1)}, u32[]{:S(2)}) copy-start(bf16[2048,4]{0,1:T(4,128)(2,1)} %param.9) | copy-start | bytes 49156
  9.9 20.3 %all-to-all-start = ((bf16[8,2,64,256]{3,2,1,0:T(8,128)(2,1)}), bf16[8,2,64,256]{3,2,1,0:T(8,128)(2,1)S(1)}, u32[]{:S(2)}, u32[]{:S(2)}) async-start(bf16[8,2,64,256]{3,2,1,0:T(8,128)(2,1)} %get-tuple-element.22), calls=%async_computation | async-start | bytes 1048576 | tf_op jit(solution)/shard_map/all_to_all | solution.py:335
  13.5 11.2 %collective-permute-start.4 = (bf16[128,512]{1,0:T(8,128)(2,1)S(1)}, bf16[128,512]{1,0:T(8,128)(2,1)S(1)}, u32[]{:S(2)}, u32[]{:S(2)}) collective-permute-start(bf16[128,512]{1,0:T(8,128)(2,1)S(1)} %copy-done.4), channel_id=1, source_target_pairs={{4,0},{0,4},{12,8},{8,12},{20,16},{16,20},{28,24},{24,28},{5,1},{1... | collective-permute-start | bytes 393224 | tf_op jit(solution)/shard_map/ppermute | solution.py:311
  15.4 0.8 %copy-start.3 = (bf16[256,128]{1,0:T(8,128)(2,1)S(1)}, bf16[256,128]{1,0:T(8,128)(2,1)}, u32[]{:S(2)}) copy-start(bf16[256,128]{1,0:T(8,128)(2,1)} %get-tuple-element.24.refs_0_) | copy-start | bytes 196612
  16.3 8.4 %copy-start.1 = (bf16[128,512]{1,0:T(8,128)(2,1)S(1)}, bf16[128,512]{1,0:T(8,128)(2,1)}, u32[]{:S(2)}) copy-start(bf16[128,512]{1,0:T(8,128)(2,1)} %get-tuple-element.28.refs_0_) | copy-start | bytes 393220
  16.6 21.1 %collective-permute-start.3 = (bf16[4,256,128]{2,1,0:T(8,128)(2,1)S(1)}, bf16[4,256,128]{2,1,0:T(8,128)(2,1)S(1)}, u32[]{:S(2)}, u32[]{:S(2)}) collective-permute-start(bf16[4,256,128]{2,1,0:T(8,128)(2,1)S(1)} %shard_map.81.refs_0_), channel_id=1, source_target_pairs={{4,0},{0,4},{12,8},{8,12},{20,16},{16,20},{28,24},{24,28},{5,1},{1... | collective-permute-start | bytes 786440 | tf_op jit(solution)/shard_map/ppermute | solution.py:311
  24.8 12.9 %collective-permute-start.5 = (bf16[2,128,128]{2,1,0:T(8,128)(2,1)S(1)}, bf16[2,128,128]{2,1,0:T(8,128)(2,1)S(1)}, u32[]{:S(2)}, u32[]{:S(2)}) collective-permute-start(bf16[2,128,128]{2,1,0:T(8,128)(2,1)S(1)} %get-tuple-element.31), channel_id=1, source_target_pairs={{0,8},{4,12},{8,16},{12,20},{16,24},{20,28},{24,0},{28,4},{1,9},{5... | collective-permute-start | bytes 196616 | tf_op jit(solution)/shard_map/ppermute | solution.py:315
  26.5 11.2 %collective-permute-start.6 = (bf16[2,128,128]{2,1,0:T(8,128)(2,1)S(1)}, bf16[2,128,128]{2,1,0:T(8,128)(2,1)S(1)}, u32[]{:S(2)}, u32[]{:S(2)}) collective-permute-start(bf16[2,128,128]{2,1,0:T(8,128)(2,1)S(1)} %get-tuple-element.32), channel_id=1, source_target_pairs={{0,16},{4,20},{8,24},{12,28},{16,0},{20,4},{24,8},{28,12},{1,17},{... | collective-permute-start | bytes 196616 | tf_op jit(solution)/shard_map/ppermute | solution.py:315
  29.2 8.5 %collective-permute-start.7 = (bf16[2,128,128]{2,1,0:T(8,128)(2,1)S(1)}, bf16[2,128,128]{2,1,0:T(8,128)(2,1)S(1)}, u32[]{:S(2)}, u32[]{:S(2)}) collective-permute-start(bf16[2,128,128]{2,1,0:T(8,128)(2,1)S(1)} %get-tuple-element.33), channel_id=1, source_target_pairs={{0,24},{4,28},{8,0},{12,4},{16,8},{20,12},{24,16},{28,20},{1,25},{... | collective-permute-start | bytes 196616 | tf_op jit(solution)/shard_map/ppermute | solution.py:315
  31.5 12.5 %all-to-all-start.1 = ((bf16[8,72,256]{2,1,0:T(8,128)(2,1)}), bf16[8,72,256]{2,1,0:T(8,128)(2,1)S(1)}, u32[]{:S(2)}, u32[]{:S(2)}) async-start(bf16[8,72,256]{2,1,0:T(8,128)(2,1)} %get-tuple-element.23), calls=%async_computation.1 | async-start | bytes 589824 | tf_op jit(solution)/shard_map/all_to_all | solution.py:379
  35.5 12.3 %collective-permute-start.11 = (bf16[8,64,256]{2,1,0:T(8,128)(2,1)S(1)}, bf16[8,64,256]{2,1,0:T(8,128)(2,1)S(1)}, u32[]{:S(2)}, u32[]{:S(2)}) collective-permute-start(bf16[8,64,256]{2,1,0:T(8,128)(2,1)S(1)} %get-tuple-element.37.refs_4_), channel_id=1, source_target_pairs={{4,0},{0,4},{12,8},{8,12},{20,16},{16,20},{28,24},{24,28},{5,1},{1... | collective-permute-start | bytes 786440 | tf_op jit(solution)/shard_map/ppermute | solution.py:311
  44.0 3.9 %collective-permute-start.8 = (f32[8,256]{1,0:T(8,128)S(1)}, f32[8,256]{1,0:T(8,128)S(1)}, u32[]{:S(2)}, u32[]{:S(2)}) collective-permute-start(f32[8,256]{1,0:T(8,128)S(1)} %shard_map.85.refs_0_), channel_id=1, source_target_pairs={{0,1},{1,2},{2,3},{3,0},{4,5},{5,6},{6,7},{7,4},{8,9},{9,10},{10,1... | collective-permute-start | bytes 24584 | tf_op jit(solution)/shard_map/ppermute | solution.py:438
  44.0 3.8 %collective-permute-start.9 = (f32[8,256]{1,0:T(8,128)S(1)}, f32[8,256]{1,0:T(8,128)S(1)}, u32[]{:S(2)}, u32[]{:S(2)}) collective-permute-start(f32[8,256]{1,0:T(8,128)S(1)} %shard_map.85.refs_0_), channel_id=1, source_target_pairs={{0,2},{1,3},{2,0},{3,1},{4,6},{5,7},{6,4},{7,5},{8,10},{9,11},{10,... | collective-permute-start | bytes 24584 | tf_op jit(solution)/shard_map/ppermute | solution.py:438
  45.6 2.8 %collective-permute-start.10 = (f32[8,256]{1,0:T(8,128)S(1)}, f32[8,256]{1,0:T(8,128)S(1)}, u32[]{:S(2)}, u32[]{:S(2)}) collective-permute-start(f32[8,256]{1,0:T(8,128)S(1)} %shard_map.85.refs_0_), channel_id=1, source_target_pairs={{0,3},{1,0},{2,1},{3,2},{4,7},{5,4},{6,5},{7,6},{8,11},{9,8},{10,9... | collective-permute-start | bytes 24584 | tf_op jit(solution)/shard_map/ppermute | solution.py:438

commit v7 on v6

--- a/solution.py
+++ b/solution.py
@@ -434,7 +434,7 @@
     )(home, totals)
     all_squares = [squares]
     for offset in range(1, chan_count):
-        pairs = [(source, (source + offset) % chan_count) for source in range(chan_count)]
+        pairs = [(source, source ^ offset) for source in range(chan_count)]
         all_squares.append(lax.ppermute(squares, "chan", pairs))
 
     attended = call(

time: 50.2 us -> 50.3 us (level)
  waiting for transfers between devices: 12.1 us -> 13.5 us
  starting transfers between devices: 26.7 us -> 25.7 us
    ppermute x3, waiting for transfers between devices: 0.52 us -> 1.93 us  [shards(): all_squares.append(lax.ppermute(squares, 'chan', pairs))]
    ppermute x3, starting transfers between devices: 3 us -> 1.93 us  [shards(): all_squares.append(lax.ppermute(squares, 'chan', pairs))]
  transfers between devices with their start and end apart: 14 -> 14, of which waited for: 4 -> 5; matrix products, arithmetic and copies ran while one was open for 0% -> 0% of each run, Pallas kernels for 12% -> 12%
where the time goes in v7:
time: 50.3 us; the launch traced here: 50 us
  starting transfers between devices  25.7 us (51%)
  waiting for transfers between devices  13.5 us (27%)
  Pallas kernels  9.3 us (18%)
  local copies, waits for them, and re-layouts  0.77 us (2%)
  between operations  0.76 us (2%)
    ppermute x6, starting transfers between devices, from_head(): return lax.ppermute(array, 'seq', pairs)  11.7 us
    ppermute x3, waiting for transfers between devices, from_set(): return lax.ppermute(array, 'seq', pairs)  7.82 us
    ppermute x3, starting transfers between devices, from_set(): return lax.ppermute(array, 'seq', pairs)  4.32 us
    all_to_all x1, starting transfers between devices, shards(): home = lax.all_to_all(back, 'seq', 0, 0, tiled=True)  4.03 us
    all_to_all x1, starting transfers between devices, shards(): got = lax.all_to_all(packed, 'seq', 0, 0, tiled=True)  3.62 us
    all_to_all x1, waiting for transfers between devices, shards(): home = lax.all_to_all(back, 'seq', 0, 0, tiled=True)  3.18 us
    pallas_call x1, Pallas kernels, shards(): call(functools.partial(pack_kernel, sets, heads_loc), [shape((seq_count,...  2.2 us
    ppermute x3, starting transfers between devices, shards(): all_squares.append(lax.ppermute(squares, 'chan', pairs))  1.93 us
  transfers between devices with their start and end apart: 14, of which 5 were waited for; matrix products, arithmetic and copies ran while one was open for 0% of the time, Pallas kernels for 12%

profile of v7, /device:TPU:0, one launch (start us, length us, event | category | flops | bytes accessed | tf_op | source)
XLA Modules:
  0.0 50.0 jit_solution(2157443578567526304)
XLA Ops:
  0.6 0.0 copy-start
  0.6 2.2 %shard_map.77 = (bf16[8,2,64,256]{3,2,1,0:T(8,128)(2,1)}, bf16[256,128]{1,0:T(8,128)(2,1)}, bf16[256,128]{1,0:T(8,128)(2,1)}, bf16[256,128]{1,0:T(8,128)(2,1)}, ...) custom-call(bf16[256,512]{1,0:T(8,128)(2,1)} %signal_ref.1, ...), custom_call_target="tpu_custom_call" | custom-call | bytes 2097152 | tf_op jit(solution)/shard_map/pallas_call | solution.py:318
  2.9 3.1 %collective-permute-start = (bf16[256,128]{1,0:T(8,128)(2,1)}, bf16[256,128]{1,0:T(8,128)(2,1)S(1)}, u32[]{:S(2)}, u32[]{:S(2)}) collective-permute-start(bf16[256,128]{1,0:T(8,128)(2,1)} %get-tuple-element.25), channel_id=1, source_target_pairs={{0,8},{4,12},{8,16},{12,20},{16,24},{20,28},{24,0},{28,4},{1,9},{5... | collective-permute-start | bytes 196616 | tf_op jit(solution)/shard_map/ppermute | solution.py:315
  5.9 2.6 %collective-permute-start.1 = (bf16[256,128]{1,0:T(8,128)(2,1)}, bf16[256,128]{1,0:T(8,128)(2,1)S(1)}, u32[]{:S(2)}, u32[]{:S(2)}) collective-permute-start(bf16[256,128]{1,0:T(8,128)(2,1)} %get-tuple-element.26), channel_id=1, source_target_pairs={{0,16},{4,20},{8,24},{12,28},{16,0},{20,4},{24,8},{28,12},{1,17},{... | collective-permute-start | bytes 196616 | tf_op jit(solution)/shard_map/ppermute | solution.py:315
  8.5 1.3 %collective-permute-start.2 = (bf16[256,128]{1,0:T(8,128)(2,1)}, bf16[256,128]{1,0:T(8,128)(2,1)S(1)}, u32[]{:S(2)}, u32[]{:S(2)}) collective-permute-start(bf16[256,128]{1,0:T(8,128)(2,1)} %get-tuple-element.27), channel_id=1, source_target_pairs={{0,24},{4,28},{8,0},{12,4},{16,8},{20,12},{24,16},{28,20},{1,25},{... | collective-permute-start | bytes 196616 | tf_op jit(solution)/shard_map/ppermute | solution.py:315
  9.9 0.0 copy-start.4
  9.9 0.0 copy-start.2
  9.9 3.6 %all-to-all-start = ((bf16[8,2,64,256]{3,2,1,0:T(8,128)(2,1)}), bf16[8,2,64,256]{3,2,1,0:T(8,128)(2,1)S(1)}, u32[]{:S(2)}, u32[]{:S(2)}) async-start(bf16[8,2,64,256]{3,2,1,0:T(8,128)(2,1)} %get-tuple-element.22), calls=%async_computation | async-start | bytes 1048576 | tf_op jit(solution)/shard_map/all_to_all | solution.py:335
  13.5 0.0 copy-done.4
  13.5 1.9 %collective-permute-start.4 = (bf16[128,512]{1,0:T(8,128)(2,1)S(1)}, bf16[128,512]{1,0:T(8,128)(2,1)S(1)}, u32[]{:S(2)}, u32[]{:S(2)}) collective-permute-start(bf16[128,512]{1,0:T(8,128)(2,1)S(1)} %copy-done.4), channel_id=1, source_target_pairs={{4,0},{0,4},{12,8},{8,12},{20,16},{16,20},{28,24},{24,28},{5,1},{1... | collective-permute-start | bytes 393224 | tf_op jit(solution)/shard_map/ppermute | solution.py:311
  15.4 0.0 copy-done.2
  15.4 0.0 copy-start.3
  15.4 0.2 shard_map.78.matrix_ref.refs_4_
  15.7 0.0 collective-permute-done.refs_1_
  15.7 0.0 collective-permute-done.1.refs_2_
  15.7 0.0 collective-permute-done.2.refs_3_
  15.7 0.6 %copy-done.3 = bf16[256,128]{1,0:T(8,128)(2,1)S(1)} copy-done((bf16[256,128]{1,0:T(8,128)(2,1)S(1)}, bf16[256,128]{1,0:T(8,128)(2,1)}, u32[]{:S(2)}) %copy-start.3) | copy-done | bytes 65560
  16.3 0.0 copy-start.1
  16.3 0.4 shard_map.81.refs_0_
  16.6 0.2 collective-permute-start.3
  16.9 7.8 %collective-permute-done.4.refs_1_ = bf16[128,512]{1,0:T(8,128)(2,1)S(1)} collective-permute-done((bf16[128,512]{1,0:T(8,128)(2,1)S(1)}, bf16[128,512]{1,0:T(8,128)(2,1)S(1)}, u32[]{:S(2)}, u32[]{:S(2)}) %collective-permute-start.4) | collective-permute-done | bytes 131104 | tf_op jit(solution)/shard_map/ppermute | solution.py:311
  24.7 0.0 copy-done.1
  24.8 1.7 %collective-permute-start.5 = (bf16[2,128,128]{2,1,0:T(8,128)(2,1)S(1)}, bf16[2,128,128]{2,1,0:T(8,128)(2,1)S(1)}, u32[]{:S(2)}, u32[]{:S(2)}) collective-permute-start(bf16[2,128,128]{2,1,0:T(8,128)(2,1)S(1)} %get-tuple-element.31), channel_id=1, source_target_pairs={{0,8},{4,12},{8,16},{12,20},{16,24},{20,28},{24,0},{28,4},{1,9},{5... | collective-permute-start | bytes 196616 | tf_op jit(solution)/shard_map/ppermute | solution.py:315
  26.5 2.7 %collective-permute-start.6 = (bf16[2,128,128]{2,1,0:T(8,128)(2,1)S(1)}, bf16[2,128,128]{2,1,0:T(8,128)(2,1)S(1)}, u32[]{:S(2)}, u32[]{:S(2)}) collective-permute-start(bf16[2,128,128]{2,1,0:T(8,128)(2,1)S(1)} %get-tuple-element.32), channel_id=1, source_target_pairs={{0,16},{4,20},{8,24},{12,28},{16,0},{20,4},{24,8},{28,12},{1,17},{... | collective-permute-start | bytes 196616 | tf_op jit(solution)/shard_map/ppermute | solution.py:315
  29.2 0.3 collective-permute-start.7
  29.5 0.0 copy-done
  29.5 0.1 dynamic-slice_bitcast_fusion
  29.6 0.1 copy.8.skip_ref
  29.7 0.6 %all-to-all-done.got_ref = bf16[8,2,64,256]{3,2,1,0:T(8,128)(2,1)S(1)} async-done(((bf16[8,2,64,256]{3,2,1,0:T(8,128)(2,1)}), bf16[8,2,64,256]{3,2,1,0:T(8,128)(2,1)S(1)}, u32[]{:S(2)}, u32[]{:S(2)}) %all-to-all-start) | async-done | bytes 524320 | tf_op jit(solution)/shard_map/all_to_all | solution.py:335
  30.2 1.3 %shard_map.79 = (bf16[8,64,256]{2,1,0:T(8,128)(2,1)S(1)}, bf16[8,72,256]{2,1,0:T(8,128)(2,1)}) custom-call(bf16[8,2,64,256]{3,2,1,0:T(8,128)(2,1)S(1)} %all-to-all-done.got_ref, bf16[256,2048]{1,0:T(8,128)(2,1)S(1)} %shard_map.78.matrix_ref.refs_4_, f32[64,1]{1,0:T(8,128)S(1)} %copy.8.skip_ref), custom_call_target="tpu_custom_call" | custom-call | flops 268435456 | bytes 1310720 | tf_op jit(solution)/shard_map/pallas_call | solution.py:367
  31.5 4.0 %all-to-all-start.1 = ((bf16[8,72,256]{2,1,0:T(8,128)(2,1)}), bf16[8,72,256]{2,1,0:T(8,128)(2,1)S(1)}, u32[]{:S(2)}, u32[]{:S(2)}) async-start(bf16[8,72,256]{2,1,0:T(8,128)(2,1)} %get-tuple-element.23), calls=%async_computation.1 | async-start | bytes 589824 | tf_op jit(solution)/shard_map/all_to_all | solution.py:379
  35.5 2.2 %collective-permute-start.11 = (bf16[8,64,256]{2,1,0:T(8,128)(2,1)S(1)}, bf16[8,64,256]{2,1,0:T(8,128)(2,1)S(1)}, u32[]{:S(2)}, u32[]{:S(2)}) collective-permute-start(bf16[8,64,256]{2,1,0:T(8,128)(2,1)S(1)} %get-tuple-element.37.refs_4_), channel_id=1, source_target_pairs={{4,0},{0,4},{12,8},{8,12},{20,16},{16,20},{28,24},{24,28},{5,1},{1... | collective-permute-start | bytes 786440 | tf_op jit(solution)/shard_map/ppermute | solution.py:311
  37.7 0.0 collective-permute-done.5.refs_3_
  37.7 0.0 collective-permute-done.6.refs_4_
  37.7 0.0 collective-permute-done.7.refs_5_
  37.7 0.0 collective-permute-done.3.refs_1_
  37.7 1.2 %shard_map.83 = (bf16[8,256,128]{2,1,0:T(8,128)(2,1)S(1)}, bf16[8,128,128]{2,1,0:T(8,128)(2,1)S(1)}) custom-call(bf16[4,256,128]{2,1,0:T(8,128)(2,1)S(1)} %shard_map.81.refs_0_, bf16[4,256,128]{2,1,0:T(8,128)(2,1)S(1)} %collective-permute-done.3.refs_1_, bf16[2,128,128]{2,1,0:T(8,128)(2,1)S(1)} %get-tuple-element.30.refs_2_, ...), custom_call_target="tpu_custom_call" | custom-call | flops 40000000000 | bytes 1572864 | tf_op jit(solution)/shard_map/pallas_call | solution.py:406
  38.9 1.8 %shard_map.84 = (f32[4,8,256]{2,1,0:T(8,128)S(1)}, bf16[512,256]{1,0:T(8,128)(2,1)S(1)}, bf16[1024,256]{1,0:T(8,128)(2,1)S(1)}, bf16[1536,256]{1,0:T(8,128)(2,1)S(1)}, bf16[2048,256]{1,0:T(8,128)(2,1)S(1)}) custom-call(bf16[8,256,128]{2,1,0:T(8,128)(2,1)S(1)} %get-tuple-element.34.key_ref, bf16[8,128,128]{2,1,0:T(8,128)(2,1)S(1)} %get-tuple-element.35.query_ref), custom_call_target="tpu_custom_call" | custom-call | flops 268435456 | bytes 2621440 | tf_op jit(solution)/shard_map/pallas_call | solution.py:415
  40.8 3.2 %all-to-all-done.1.got_ref.home_ref = bf16[8,72,256]{2,1,0:T(8,128)(2,1)S(1)} async-done(((bf16[8,72,256]{2,1,0:T(8,128)(2,1)}), bf16[8,72,256]{2,1,0:T(8,128)(2,1)S(1)}, u32[]{:S(2)}, u32[]{:S(2)}) %all-to-all-start.1) | async-done | bytes 294944 | tf_op jit(solution)/shard_map/all_to_all | solution.py:379
  44.0 0.1 collective-permute-start.8
  44.0 1.6 %collective-permute-start.9 = (f32[8,256]{1,0:T(8,128)S(1)}, f32[8,256]{1,0:T(8,128)S(1)}, u32[]{:S(2)}, u32[]{:S(2)}) collective-permute-start(f32[8,256]{1,0:T(8,128)S(1)} %shard_map.85.refs_0_), channel_id=1, source_target_pairs={{0,2},{1,3},{2,0},{3,1},{4,6},{5,7},{6,4},{7,5},{8,10},{9,11},{10,... | collective-permute-start | bytes 24584 | tf_op jit(solution)/shard_map/ppermute | solution.py:438
  45.6 0.3 collective-permute-start.10
  45.9 0.8 %shard_map.80 = bf16[256,512]{1,0:T(8,128)(2,1)} custom-call(bf16[8,72,256]{2,1,0:T(8,128)(2,1)S(1)} %all-to-all-done.1.got_ref.home_ref), custom_call_target="tpu_custom_call" | custom-call | bytes 524288 | tf_op jit(solution)/shard_map/pallas_call | solution.py:454
  46.7 0.0 collective-permute-done.11.refs_5_
  46.7 0.0 collective-permute-done.8.refs_1_
  46.8 1.0 %collective-permute-done.9.refs_2_ = f32[8,256]{1,0:T(8,128)S(1)} collective-permute-done((f32[8,256]{1,0:T(8,128)S(1)}, f32[8,256]{1,0:T(8,128)S(1)}, u32[]{:S(2)}, u32[]{:S(2)}) %collective-permute-start.9) | collective-permute-done | bytes 8224 | tf_op jit(solution)/shard_map/ppermute | solution.py:438
  47.8 0.9 %collective-permute-done.10.refs_3_ = f32[8,256]{1,0:T(8,128)S(1)} collective-permute-done((f32[8,256]{1,0:T(8,128)S(1)}, f32[8,256]{1,0:T(8,128)S(1)}, u32[]{:S(2)}, u32[]{:S(2)}) %collective-permute-start.10) | collective-permute-done | bytes 8224 | tf_op jit(solution)/shard_map/ppermute | solution.py:438
  48.7 1.3 %shard_map.86 = bf16[1024,128]{1,0:T(8,128)(2,1)} custom-call(f32[8,256]{1,0:T(8,128)S(1)} %shard_map.85.refs_0_, f32[8,256]{1,0:T(8,128)S(1)} %collective-permute-done.8.refs_1_, f32[8,256]{1,0:T(8,128)S(1)} %collective-permute-done.9.refs_2_, f32[8,256]{1,0:T(8,128)S(1)} %collective-permute-done.10.refs_3_, ...), custom_call_target="tpu_custom_call" | custom-call | flops 268435456 | bytes 2621440 | tf_op jit(solution)/shard_map/pallas_call | solution.py:440
  (2 shorter events, 0.1 us)
Async XLA Ops:
  0.6 28.9 %copy-start = (f32[512]{0:T(512)S(1)}, f32[512]{0:T(512)}, u32[]{:S(2)}) copy-start(f32[512]{0:T(512)} %param.8) | copy-start | bytes 6148
  2.9 12.8 %collective-permute-start = (bf16[256,128]{1,0:T(8,128)(2,1)}, bf16[256,128]{1,0:T(8,128)(2,1)S(1)}, u32[]{:S(2)}, u32[]{:S(2)}) collective-permute-start(bf16[256,128]{1,0:T(8,128)(2,1)} %get-tuple-element.25), channel_id=1, source_target_pairs={{0,8},{4,12},{8,16},{12,20},{16,24},{20,28},{24,0},{28,4},{1,9},{5... | collective-permute-start | bytes 196616 | tf_op jit(solution)/shard_map/ppermute | solution.py:315
  5.9 9.7 %collective-permute-start.1 = (bf16[256,128]{1,0:T(8,128)(2,1)}, bf16[256,128]{1,0:T(8,128)(2,1)S(1)}, u32[]{:S(2)}, u32[]{:S(2)}) collective-permute-start(bf16[256,128]{1,0:T(8,128)(2,1)} %get-tuple-element.26), channel_id=1, source_target_pairs={{0,16},{4,20},{8,24},{12,28},{16,0},{20,4},{24,8},{28,12},{1,17},{... | collective-permute-start | bytes 196616 | tf_op jit(solution)/shard_map/ppermute | solution.py:315
  8.5 7.2 %collective-permute-start.2 = (bf16[256,128]{1,0:T(8,128)(2,1)}, bf16[256,128]{1,0:T(8,128)(2,1)S(1)}, u32[]{:S(2)}, u32[]{:S(2)}) collective-permute-start(bf16[256,128]{1,0:T(8,128)(2,1)} %get-tuple-element.27), channel_id=1, source_target_pairs={{0,24},{4,28},{8,0},{12,4},{16,8},{20,12},{24,16},{28,20},{1,25},{... | collective-permute-start | bytes 196616 | tf_op jit(solution)/shard_map/ppermute | solution.py:315
  9.9 3.6 %copy-start.4 = (bf16[128,512]{1,0:T(8,128)(2,1)S(1)}, bf16[128,512]{1,0:T(8,128)(2,1)}, u32[]{:S(2)}) copy-start(bf16[128,512]{1,0:T(8,128)(2,1)} %get-tuple-element.29) | copy-start | bytes 393220
  9.9 5.6 %copy-start.2 = (bf16[2048,4]{0,1:T(4,128)(2,1)S(1)}, bf16[2048,4]{0,1:T(4,128)(2,1)}, u32[]{:S(2)}) copy-start(bf16[2048,4]{0,1:T(4,128)(2,1)} %param.9) | copy-start | bytes 49156
  9.9 20.3 %all-to-all-start = ((bf16[8,2,64,256]{3,2,1,0:T(8,128)(2,1)}), bf16[8,2,64,256]{3,2,1,0:T(8,128)(2,1)S(1)}, u32[]{:S(2)}, u32[]{:S(2)}) async-start(bf16[8,2,64,256]{3,2,1,0:T(8,128)(2,1)} %get-tuple-element.22), calls=%async_computation | async-start | bytes 1048576 | tf_op jit(solution)/shard_map/all_to_all | solution.py:335
  13.5 11.2 %collective-permute-start.4 = (bf16[128,512]{1,0:T(8,128)(2,1)S(1)}, bf16[128,512]{1,0:T(8,128)(2,1)S(1)}, u32[]{:S(2)}, u32[]{:S(2)}) collective-permute-start(bf16[128,512]{1,0:T(8,128)(2,1)S(1)} %copy-done.4), channel_id=1, source_target_pairs={{4,0},{0,4},{12,8},{8,12},{20,16},{16,20},{28,24},{24,28},{5,1},{1... | collective-permute-start | bytes 393224 | tf_op jit(solution)/shard_map/ppermute | solution.py:311
  15.4 0.8 %copy-start.3 = (bf16[256,128]{1,0:T(8,128)(2,1)S(1)}, bf16[256,128]{1,0:T(8,128)(2,1)}, u32[]{:S(2)}) copy-start(bf16[256,128]{1,0:T(8,128)(2,1)} %get-tuple-element.24.refs_0_) | copy-start | bytes 196612
  16.3 8.4 %copy-start.1 = (bf16[128,512]{1,0:T(8,128)(2,1)S(1)}, bf16[128,512]{1,0:T(8,128)(2,1)}, u32[]{:S(2)}) copy-start(bf16[128,512]{1,0:T(8,128)(2,1)} %get-tuple-element.28.refs_0_) | copy-start | bytes 393220
  16.6 21.1 %collective-permute-start.3 = (bf16[4,256,128]{2,1,0:T(8,128)(2,1)S(1)}, bf16[4,256,128]{2,1,0:T(8,128)(2,1)S(1)}, u32[]{:S(2)}, u32[]{:S(2)}) collective-permute-start(bf16[4,256,128]{2,1,0:T(8,128)(2,1)S(1)} %shard_map.81.refs_0_), channel_id=1, source_target_pairs={{4,0},{0,4},{12,8},{8,12},{20,16},{16,20},{28,24},{24,28},{5,1},{1... | collective-permute-start | bytes 786440 | tf_op jit(solution)/shard_map/ppermute | solution.py:311
  24.8 12.9 %collective-permute-start.5 = (bf16[2,128,128]{2,1,0:T(8,128)(2,1)S(1)}, bf16[2,128,128]{2,1,0:T(8,128)(2,1)S(1)}, u32[]{:S(2)}, u32[]{:S(2)}) collective-permute-start(bf16[2,128,128]{2,1,0:T(8,128)(2,1)S(1)} %get-tuple-element.31), channel_id=1, source_target_pairs={{0,8},{4,12},{8,16},{12,20},{16,24},{20,28},{24,0},{28,4},{1,9},{5... | collective-permute-start | bytes 196616 | tf_op jit(solution)/shard_map/ppermute | solution.py:315
  26.5 11.2 %collective-permute-start.6 = (bf16[2,128,128]{2,1,0:T(8,128)(2,1)S(1)}, bf16[2,128,128]{2,1,0:T(8,128)(2,1)S(1)}, u32[]{:S(2)}, u32[]{:S(2)}) collective-permute-start(bf16[2,128,128]{2,1,0:T(8,128)(2,1)S(1)} %get-tuple-element.32), channel_id=1, source_target_pairs={{0,16},{4,20},{8,24},{12,28},{16,0},{20,4},{24,8},{28,12},{1,17},{... | collective-permute-start | bytes 196616 | tf_op jit(solution)/shard_map/ppermute | solution.py:315
  29.2 8.5 %collective-permute-start.7 = (bf16[2,128,128]{2,1,0:T(8,128)(2,1)S(1)}, bf16[2,128,128]{2,1,0:T(8,128)(2,1)S(1)}, u32[]{:S(2)}, u32[]{:S(2)}) collective-permute-start(bf16[2,128,128]{2,1,0:T(8,128)(2,1)S(1)} %get-tuple-element.33), channel_id=1, source_target_pairs={{0,24},{4,28},{8,0},{12,4},{16,8},{20,12},{24,16},{28,20},{1,25},{... | collective-permute-start | bytes 196616 | tf_op jit(solution)/shard_map/ppermute | solution.py:315
  31.5 12.5 %all-to-all-start.1 = ((bf16[8,72,256]{2,1,0:T(8,128)(2,1)}), bf16[8,72,256]{2,1,0:T(8,128)(2,1)S(1)}, u32[]{:S(2)}, u32[]{:S(2)}) async-start(bf16[8,72,256]{2,1,0:T(8,128)(2,1)} %get-tuple-element.23), calls=%async_computation.1 | async-start | bytes 589824 | tf_op jit(solution)/shard_map/all_to_all | solution.py:379
  35.5 11.2 %collective-permute-start.11 = (bf16[8,64,256]{2,1,0:T(8,128)(2,1)S(1)}, bf16[8,64,256]{2,1,0:T(8,128)(2,1)S(1)}, u32[]{:S(2)}, u32[]{:S(2)}) collective-permute-start(bf16[8,64,256]{2,1,0:T(8,128)(2,1)S(1)} %get-tuple-element.37.refs_4_), channel_id=1, source_target_pairs={{4,0},{0,4},{12,8},{8,12},{20,16},{16,20},{28,24},{24,28},{5,1},{1... | collective-permute-start | bytes 786440 | tf_op jit(solution)/shard_map/ppermute | solution.py:311
  44.0 2.8 %collective-permute-start.8 = (f32[8,256]{1,0:T(8,128)S(1)}, f32[8,256]{1,0:T(8,128)S(1)}, u32[]{:S(2)}, u32[]{:S(2)}) collective-permute-start(f32[8,256]{1,0:T(8,128)S(1)} %shard_map.85.refs_0_), channel_id=1, source_target_pairs={{0,1},{1,0},{2,3},{3,2},{4,5},{5,4},{6,7},{7,6},{8,9},{9,8},{10,11... | collective-permute-start | bytes 24584 | tf_op jit(solution)/shard_map/ppermute | solution.py:438
  44.0 3.7 %collective-permute-start.9 = (f32[8,256]{1,0:T(8,128)S(1)}, f32[8,256]{1,0:T(8,128)S(1)}, u32[]{:S(2)}, u32[]{:S(2)}) collective-permute-start(f32[8,256]{1,0:T(8,128)S(1)} %shard_map.85.refs_0_), channel_id=1, source_target_pairs={{0,2},{1,3},{2,0},{3,1},{4,6},{5,7},{6,4},{7,5},{8,10},{9,11},{10,... | collective-permute-start | bytes 24584 | tf_op jit(solution)/shard_map/ppermute | solution.py:438
  45.6 3.1 %collective-permute-start.10 = (f32[8,256]{1,0:T(8,128)S(1)}, f32[8,256]{1,0:T(8,128)S(1)}, u32[]{:S(2)}, u32[]{:S(2)}) collective-permute-start(f32[8,256]{1,0:T(8,128)S(1)} %shard_map.85.refs_0_), channel_id=1, source_target_pairs={{0,3},{1,2},{2,1},{3,0},{4,7},{5,6},{6,5},{7,4},{8,11},{9,10},{10,... | collective-permute-start | bytes 24584 | tf_op jit(solution)/shard_map/ppermute | solution.py:438

commit v8 on v7

--- a/solution.py
+++ b/solution.py
@@ -433,7 +433,7 @@
         vmem=8 if not gridded else 56,
     )(home, totals)
     all_squares = [squares]
-    for offset in range(1, chan_count):
+    for offset in reversed(range(1, chan_count)):
         pairs = [(source, source ^ offset) for source in range(chan_count)]
         all_squares.append(lax.ppermute(squares, "chan", pairs))
 

time: 50.3 us -> 49.4 us (0.982)
  waiting for transfers between devices: 13.5 us -> 12.6 us
    ppermute x3, waiting for transfers between devices: 1.93 us -> 1.03 us  [shards(): all_squares.append(lax.ppermute(squares, 'chan', pairs))]
where the time goes in v8:
time: 49.4 us; the launch traced here: 49.1 us
  starting transfers between devices  25.6 us (52%)
  waiting for transfers between devices  12.6 us (26%)
  Pallas kernels  9.3 us (19%)
  local copies, waits for them, and re-layouts  0.77 us (2%)
  between operations  0.76 us (2%)
    ppermute x6, starting transfers between devices, from_head(): return lax.ppermute(array, 'seq', pairs)  11.7 us
    ppermute x3, waiting for transfers between devices, from_set(): return lax.ppermute(array, 'seq', pairs)  7.82 us
    ppermute x3, starting transfers between devices, from_set(): return lax.ppermute(array, 'seq', pairs)  4.32 us
    all_to_all x1, starting transfers between devices, shards(): home = lax.all_to_all(back, 'seq', 0, 0, tiled=True)  4.03 us
    all_to_all x1, starting transfers between devices, shards(): got = lax.all_to_all(packed, 'seq', 0, 0, tiled=True)  3.62 us
    all_to_all x1, waiting for transfers between devices, shards(): home = lax.all_to_all(back, 'seq', 0, 0, tiled=True)  3.18 us
    pallas_call x1, Pallas kernels, shards(): call(functools.partial(pack_kernel, sets, heads_loc), [shape((seq_count,...  2.2 us
    ppermute x3, starting transfers between devices, shards(): all_squares.append(lax.ppermute(squares, 'chan', pairs))  1.92 us
  transfers between devices with their start and end apart: 14, of which 5 were waited for; matrix products, arithmetic and copies ran while one was open for 0% of the time, Pallas kernels for 12%

profile of v8, /device:TPU:0, one launch (start us, length us, event | category | flops | bytes accessed | tf_op | source)
XLA Modules:
  0.0 49.1 jit_solution(1454269529254896027)
XLA Ops:
  0.6 0.0 copy-start
  0.6 2.2 %shard_map.77 = (bf16[8,2,64,256]{3,2,1,0:T(8,128)(2,1)}, bf16[256,128]{1,0:T(8,128)(2,1)}, bf16[256,128]{1,0:T(8,128)(2,1)}, bf16[256,128]{1,0:T(8,128)(2,1)}, ...) custom-call(bf16[256,512]{1,0:T(8,128)(2,1)} %signal_ref.1, ...), custom_call_target="tpu_custom_call" | custom-call | bytes 2097152 | tf_op jit(solution)/shard_map/pallas_call | solution.py:318
  2.9 3.1 %collective-permute-start = (bf16[256,128]{1,0:T(8,128)(2,1)}, bf16[256,128]{1,0:T(8,128)(2,1)S(1)}, u32[]{:S(2)}, u32[]{:S(2)}) collective-permute-start(bf16[256,128]{1,0:T(8,128)(2,1)} %get-tuple-element.25), channel_id=1, source_target_pairs={{0,8},{4,12},{8,16},{12,20},{16,24},{20,28},{24,0},{28,4},{1,9},{5... | collective-permute-start | bytes 196616 | tf_op jit(solution)/shard_map/ppermute | solution.py:315
  5.9 2.6 %collective-permute-start.1 = (bf16[256,128]{1,0:T(8,128)(2,1)}, bf16[256,128]{1,0:T(8,128)(2,1)S(1)}, u32[]{:S(2)}, u32[]{:S(2)}) collective-permute-start(bf16[256,128]{1,0:T(8,128)(2,1)} %get-tuple-element.26), channel_id=1, source_target_pairs={{0,16},{4,20},{8,24},{12,28},{16,0},{20,4},{24,8},{28,12},{1,17},{... | collective-permute-start | bytes 196616 | tf_op jit(solution)/shard_map/ppermute | solution.py:315
  8.5 1.3 %collective-permute-start.2 = (bf16[256,128]{1,0:T(8,128)(2,1)}, bf16[256,128]{1,0:T(8,128)(2,1)S(1)}, u32[]{:S(2)}, u32[]{:S(2)}) collective-permute-start(bf16[256,128]{1,0:T(8,128)(2,1)} %get-tuple-element.27), channel_id=1, source_target_pairs={{0,24},{4,28},{8,0},{12,4},{16,8},{20,12},{24,16},{28,20},{1,25},{... | collective-permute-start | bytes 196616 | tf_op jit(solution)/shard_map/ppermute | solution.py:315
  9.9 0.0 copy-start.4
  9.9 0.0 copy-start.2
  9.9 3.6 %all-to-all-start = ((bf16[8,2,64,256]{3,2,1,0:T(8,128)(2,1)}), bf16[8,2,64,256]{3,2,1,0:T(8,128)(2,1)S(1)}, u32[]{:S(2)}, u32[]{:S(2)}) async-start(bf16[8,2,64,256]{3,2,1,0:T(8,128)(2,1)} %get-tuple-element.22), calls=%async_computation | async-start | bytes 1048576 | tf_op jit(solution)/shard_map/all_to_all | solution.py:335
  13.5 0.0 copy-done.4
  13.5 1.9 %collective-permute-start.4 = (bf16[128,512]{1,0:T(8,128)(2,1)S(1)}, bf16[128,512]{1,0:T(8,128)(2,1)S(1)}, u32[]{:S(2)}, u32[]{:S(2)}) collective-permute-start(bf16[128,512]{1,0:T(8,128)(2,1)S(1)} %copy-done.4), channel_id=1, source_target_pairs={{4,0},{0,4},{12,8},{8,12},{20,16},{16,20},{28,24},{24,28},{5,1},{1... | collective-permute-start | bytes 393224 | tf_op jit(solution)/shard_map/ppermute | solution.py:311
  15.4 0.0 copy-done.2
  15.4 0.0 copy-start.3
  15.4 0.2 shard_map.78.matrix_ref.refs_4_
  15.7 0.0 collective-permute-done.refs_1_
  15.7 0.0 collective-permute-done.1.refs_2_
  15.7 0.0 collective-permute-done.2.refs_3_
  15.7 0.6 %copy-done.3 = bf16[256,128]{1,0:T(8,128)(2,1)S(1)} copy-done((bf16[256,128]{1,0:T(8,128)(2,1)S(1)}, bf16[256,128]{1,0:T(8,128)(2,1)}, u32[]{:S(2)}) %copy-start.3) | copy-done | bytes 65560
  16.3 0.0 copy-start.1
  16.3 0.4 shard_map.81.refs_0_
  16.6 0.2 collective-permute-start.3
  16.9 7.8 %collective-permute-done.4.refs_1_ = bf16[128,512]{1,0:T(8,128)(2,1)S(1)} collective-permute-done((bf16[128,512]{1,0:T(8,128)(2,1)S(1)}, bf16[128,512]{1,0:T(8,128)(2,1)S(1)}, u32[]{:S(2)}, u32[]{:S(2)}) %collective-permute-start.4) | collective-permute-done | bytes 131104 | tf_op jit(solution)/shard_map/ppermute | solution.py:311
  24.7 0.0 copy-done.1
  24.8 1.7 %collective-permute-start.5 = (bf16[2,128,128]{2,1,0:T(8,128)(2,1)S(1)}, bf16[2,128,128]{2,1,0:T(8,128)(2,1)S(1)}, u32[]{:S(2)}, u32[]{:S(2)}) collective-permute-start(bf16[2,128,128]{2,1,0:T(8,128)(2,1)S(1)} %get-tuple-element.31), channel_id=1, source_target_pairs={{0,8},{4,12},{8,16},{12,20},{16,24},{20,28},{24,0},{28,4},{1,9},{5... | collective-permute-start | bytes 196616 | tf_op jit(solution)/shard_map/ppermute | solution.py:315
  26.5 2.7 %collective-permute-start.6 = (bf16[2,128,128]{2,1,0:T(8,128)(2,1)S(1)}, bf16[2,128,128]{2,1,0:T(8,128)(2,1)S(1)}, u32[]{:S(2)}, u32[]{:S(2)}) collective-permute-start(bf16[2,128,128]{2,1,0:T(8,128)(2,1)S(1)} %get-tuple-element.32), channel_id=1, source_target_pairs={{0,16},{4,20},{8,24},{12,28},{16,0},{20,4},{24,8},{28,12},{1,17},{... | collective-permute-start | bytes 196616 | tf_op jit(solution)/shard_map/ppermute | solution.py:315
  29.2 0.3 collective-permute-start.7
  29.5 0.0 copy-done
  29.5 0.1 dynamic-slice_bitcast_fusion
  29.6 0.1 copy.8.skip_ref
  29.7 0.6 %all-to-all-done.got_ref = bf16[8,2,64,256]{3,2,1,0:T(8,128)(2,1)S(1)} async-done(((bf16[8,2,64,256]{3,2,1,0:T(8,128)(2,1)}), bf16[8,2,64,256]{3,2,1,0:T(8,128)(2,1)S(1)}, u32[]{:S(2)}, u32[]{:S(2)}) %all-to-all-start) | async-done | bytes 524320 | tf_op jit(solution)/shard_map/all_to_all | solution.py:335
  30.2 1.3 %shard_map.79 = (bf16[8,64,256]{2,1,0:T(8,128)(2,1)S(1)}, bf16[8,72,256]{2,1,0:T(8,128)(2,1)}) custom-call(bf16[8,2,64,256]{3,2,1,0:T(8,128)(2,1)S(1)} %all-to-all-done.got_ref, bf16[256,2048]{1,0:T(8,128)(2,1)S(1)} %shard_map.78.matrix_ref.refs_4_, f32[64,1]{1,0:T(8,128)S(1)} %copy.8.skip_ref), custom_call_target="tpu_custom_call" | custom-call | flops 268435456 | bytes 1310720 | tf_op jit(solution)/shard_map/pallas_call | solution.py:367
  31.5 4.0 %all-to-all-start.1 = ((bf16[8,72,256]{2,1,0:T(8,128)(2,1)}), bf16[8,72,256]{2,1,0:T(8,128)(2,1)S(1)}, u32[]{:S(2)}, u32[]{:S(2)}) async-start(bf16[8,72,256]{2,1,0:T(8,128)(2,1)} %get-tuple-element.23), calls=%async_computation.1 | async-start | bytes 589824 | tf_op jit(solution)/shard_map/all_to_all | solution.py:379
  35.5 2.2 %collective-permute-start.11 = (bf16[8,64,256]{2,1,0:T(8,128)(2,1)S(1)}, bf16[8,64,256]{2,1,0:T(8,128)(2,1)S(1)}, u32[]{:S(2)}, u32[]{:S(2)}) collective-permute-start(bf16[8,64,256]{2,1,0:T(8,128)(2,1)S(1)} %get-tuple-element.37.refs_4_), channel_id=1, source_target_pairs={{4,0},{0,4},{12,8},{8,12},{20,16},{16,20},{28,24},{24,28},{5,1},{1... | collective-permute-start | bytes 786440 | tf_op jit(solution)/shard_map/ppermute | solution.py:311
  37.7 0.0 collective-permute-done.5.refs_3_
  37.7 0.0 collective-permute-done.6.refs_4_
  37.7 0.0 collective-permute-done.7.refs_5_
  37.7 0.0 collective-permute-done.3.refs_1_
  37.7 1.2 %shard_map.83 = (bf16[8,256,128]{2,1,0:T(8,128)(2,1)S(1)}, bf16[8,128,128]{2,1,0:T(8,128)(2,1)S(1)}) custom-call(bf16[4,256,128]{2,1,0:T(8,128)(2,1)S(1)} %shard_map.81.refs_0_, bf16[4,256,128]{2,1,0:T(8,128)(2,1)S(1)} %collective-permute-done.3.refs_1_, bf16[2,128,128]{2,1,0:T(8,128)(2,1)S(1)} %get-tuple-element.30.refs_2_, ...), custom_call_target="tpu_custom_call" | custom-call | flops 40000000000 | bytes 1572864 | tf_op jit(solution)/shard_map/pallas_call | solution.py:406
  38.9 1.8 %shard_map.84 = (f32[4,8,256]{2,1,0:T(8,128)S(1)}, bf16[512,256]{1,0:T(8,128)(2,1)S(1)}, bf16[1024,256]{1,0:T(8,128)(2,1)S(1)}, bf16[1536,256]{1,0:T(8,128)(2,1)S(1)}, bf16[2048,256]{1,0:T(8,128)(2,1)S(1)}) custom-call(bf16[8,256,128]{2,1,0:T(8,128)(2,1)S(1)} %get-tuple-element.34.key_ref, bf16[8,128,128]{2,1,0:T(8,128)(2,1)S(1)} %get-tuple-element.35.query_ref), custom_call_target="tpu_custom_call" | custom-call | flops 268435456 | bytes 2621440 | tf_op jit(solution)/shard_map/pallas_call | solution.py:415
  40.8 3.2 %all-to-all-done.1.got_ref.home_ref = bf16[8,72,256]{2,1,0:T(8,128)(2,1)S(1)} async-done(((bf16[8,72,256]{2,1,0:T(8,128)(2,1)}), bf16[8,72,256]{2,1,0:T(8,128)(2,1)S(1)}, u32[]{:S(2)}, u32[]{:S(2)}) %all-to-all-start.1) | async-done | bytes 294944 | tf_op jit(solution)/shard_map/all_to_all | solution.py:379
  44.0 0.1 collective-permute-start.8
  44.0 1.6 %collective-permute-start.9 = (f32[8,256]{1,0:T(8,128)S(1)}, f32[8,256]{1,0:T(8,128)S(1)}, u32[]{:S(2)}, u32[]{:S(2)}) collective-permute-start(f32[8,256]{1,0:T(8,128)S(1)} %shard_map.85.refs_0_), channel_id=1, source_target_pairs={{0,2},{1,3},{2,0},{3,1},{4,6},{5,7},{6,4},{7,5},{8,10},{9,11},{10,... | collective-permute-start | bytes 24584 | tf_op jit(solution)/shard_map/ppermute | solution.py:438
  45.6 0.3 collective-permute-start.10
  45.9 0.8 %shard_map.80 = bf16[256,512]{1,0:T(8,128)(2,1)} custom-call(bf16[8,72,256]{2,1,0:T(8,128)(2,1)S(1)} %all-to-all-done.1.got_ref.home_ref), custom_call_target="tpu_custom_call" | custom-call | bytes 524288 | tf_op jit(solution)/shard_map/pallas_call | solution.py:454
  46.7 0.0 collective-permute-done.11.refs_5_
  46.7 0.4 collective-permute-done.8.refs_1_
  47.1 0.6 %collective-permute-done.9.refs_2_ = f32[8,256]{1,0:T(8,128)S(1)} collective-permute-done((f32[8,256]{1,0:T(8,128)S(1)}, f32[8,256]{1,0:T(8,128)S(1)}, u32[]{:S(2)}, u32[]{:S(2)}) %collective-permute-start.9) | collective-permute-done | bytes 8224 | tf_op jit(solution)/shard_map/ppermute | solution.py:438
  47.8 0.0 collective-permute-done.10.refs_3_
  47.8 1.3 %shard_map.86 = bf16[1024,128]{1,0:T(8,128)(2,1)} custom-call(f32[8,256]{1,0:T(8,128)S(1)} %shard_map.85.refs_0_, f32[8,256]{1,0:T(8,128)S(1)} %collective-permute-done.8.refs_1_, f32[8,256]{1,0:T(8,128)S(1)} %collective-permute-done.9.refs_2_, f32[8,256]{1,0:T(8,128)S(1)} %collective-permute-done.10.refs_3_, ...), custom_call_target="tpu_custom_call" | custom-call | flops 268435456 | bytes 2621440 | tf_op jit(solution)/shard_map/pallas_call | solution.py:440
  (2 shorter events, 0.1 us)
Async XLA Ops:
  0.6 28.9 %copy-start = (f32[512]{0:T(512)S(1)}, f32[512]{0:T(512)}, u32[]{:S(2)}) copy-start(f32[512]{0:T(512)} %param.8) | copy-start | bytes 6148
  2.9 12.8 %collective-permute-start = (bf16[256,128]{1,0:T(8,128)(2,1)}, bf16[256,128]{1,0:T(8,128)(2,1)S(1)}, u32[]{:S(2)}, u32[]{:S(2)}) collective-permute-start(bf16[256,128]{1,0:T(8,128)(2,1)} %get-tuple-element.25), channel_id=1, source_target_pairs={{0,8},{4,12},{8,16},{12,20},{16,24},{20,28},{24,0},{28,4},{1,9},{5... | collective-permute-start | bytes 196616 | tf_op jit(solution)/shard_map/ppermute | solution.py:315
  5.9 9.7 %collective-permute-start.1 = (bf16[256,128]{1,0:T(8,128)(2,1)}, bf16[256,128]{1,0:T(8,128)(2,1)S(1)}, u32[]{:S(2)}, u32[]{:S(2)}) collective-permute-start(bf16[256,128]{1,0:T(8,128)(2,1)} %get-tuple-element.26), channel_id=1, source_target_pairs={{0,16},{4,20},{8,24},{12,28},{16,0},{20,4},{24,8},{28,12},{1,17},{... | collective-permute-start | bytes 196616 | tf_op jit(solution)/shard_map/ppermute | solution.py:315
  8.5 7.2 %collective-permute-start.2 = (bf16[256,128]{1,0:T(8,128)(2,1)}, bf16[256,128]{1,0:T(8,128)(2,1)S(1)}, u32[]{:S(2)}, u32[]{:S(2)}) collective-permute-start(bf16[256,128]{1,0:T(8,128)(2,1)} %get-tuple-element.27), channel_id=1, source_target_pairs={{0,24},{4,28},{8,0},{12,4},{16,8},{20,12},{24,16},{28,20},{1,25},{... | collective-permute-start | bytes 196616 | tf_op jit(solution)/shard_map/ppermute | solution.py:315
  9.9 3.6 %copy-start.4 = (bf16[128,512]{1,0:T(8,128)(2,1)S(1)}, bf16[128,512]{1,0:T(8,128)(2,1)}, u32[]{:S(2)}) copy-start(bf16[128,512]{1,0:T(8,128)(2,1)} %get-tuple-element.29) | copy-start | bytes 393220
  9.9 5.6 %copy-start.2 = (bf16[2048,4]{0,1:T(4,128)(2,1)S(1)}, bf16[2048,4]{0,1:T(4,128)(2,1)}, u32[]{:S(2)}) copy-start(bf16[2048,4]{0,1:T(4,128)(2,1)} %param.9) | copy-start | bytes 49156
  9.9 20.3 %all-to-all-start = ((bf16[8,2,64,256]{3,2,1,0:T(8,128)(2,1)}), bf16[8,2,64,256]{3,2,1,0:T(8,128)(2,1)S(1)}, u32[]{:S(2)}, u32[]{:S(2)}) async-start(bf16[8,2,64,256]{3,2,1,0:T(8,128)(2,1)} %get-tuple-element.22), calls=%async_computation | async-start | bytes 1048576 | tf_op jit(solution)/shard_map/all_to_all | solution.py:335
  13.5 11.2 %collective-permute-start.4 = (bf16[128,512]{1,0:T(8,128)(2,1)S(1)}, bf16[128,512]{1,0:T(8,128)(2,1)S(1)}, u32[]{:S(2)}, u32[]{:S(2)}) collective-permute-start(bf16[128,512]{1,0:T(8,128)(2,1)S(1)} %copy-done.4), channel_id=1, source_target_pairs={{4,0},{0,4},{12,8},{8,12},{20,16},{16,20},{28,24},{24,28},{5,1},{1... | collective-permute-start | bytes 393224 | tf_op jit(solution)/shard_map/ppermute | solution.py:311
  15.4 0.8 %copy-start.3 = (bf16[256,128]{1,0:T(8,128)(2,1)S(1)}, bf16[256,128]{1,0:T(8,128)(2,1)}, u32[]{:S(2)}) copy-start(bf16[256,128]{1,0:T(8,128)(2,1)} %get-tuple-element.24.refs_0_) | copy-start | bytes 196612
  16.3 8.4 %copy-start.1 = (bf16[128,512]{1,0:T(8,128)(2,1)S(1)}, bf16[128,512]{1,0:T(8,128)(2,1)}, u32[]{:S(2)}) copy-start(bf16[128,512]{1,0:T(8,128)(2,1)} %get-tuple-element.28.refs_0_) | copy-start | bytes 393220
  16.6 21.1 %collective-permute-start.3 = (bf16[4,256,128]{2,1,0:T(8,128)(2,1)S(1)}, bf16[4,256,128]{2,1,0:T(8,128)(2,1)S(1)}, u32[]{:S(2)}, u32[]{:S(2)}) collective-permute-start(bf16[4,256,128]{2,1,0:T(8,128)(2,1)S(1)} %shard_map.81.refs_0_), channel_id=1, source_target_pairs={{4,0},{0,4},{12,8},{8,12},{20,16},{16,20},{28,24},{24,28},{5,1},{1... | collective-permute-start | bytes 786440 | tf_op jit(solution)/shard_map/ppermute | solution.py:311
  24.8 12.9 %collective-permute-start.5 = (bf16[2,128,128]{2,1,0:T(8,128)(2,1)S(1)}, bf16[2,128,128]{2,1,0:T(8,128)(2,1)S(1)}, u32[]{:S(2)}, u32[]{:S(2)}) collective-permute-start(bf16[2,128,128]{2,1,0:T(8,128)(2,1)S(1)} %get-tuple-element.31), channel_id=1, source_target_pairs={{0,8},{4,12},{8,16},{12,20},{16,24},{20,28},{24,0},{28,4},{1,9},{5... | collective-permute-start | bytes 196616 | tf_op jit(solution)/shard_map/ppermute | solution.py:315
  26.5 11.2 %collective-permute-start.6 = (bf16[2,128,128]{2,1,0:T(8,128)(2,1)S(1)}, bf16[2,128,128]{2,1,0:T(8,128)(2,1)S(1)}, u32[]{:S(2)}, u32[]{:S(2)}) collective-permute-start(bf16[2,128,128]{2,1,0:T(8,128)(2,1)S(1)} %get-tuple-element.32), channel_id=1, source_target_pairs={{0,16},{4,20},{8,24},{12,28},{16,0},{20,4},{24,8},{28,12},{1,17},{... | collective-permute-start | bytes 196616 | tf_op jit(solution)/shard_map/ppermute | solution.py:315
  29.2 8.5 %collective-permute-start.7 = (bf16[2,128,128]{2,1,0:T(8,128)(2,1)S(1)}, bf16[2,128,128]{2,1,0:T(8,128)(2,1)S(1)}, u32[]{:S(2)}, u32[]{:S(2)}) collective-permute-start(bf16[2,128,128]{2,1,0:T(8,128)(2,1)S(1)} %get-tuple-element.33), channel_id=1, source_target_pairs={{0,24},{4,28},{8,0},{12,4},{16,8},{20,12},{24,16},{28,20},{1,25},{... | collective-permute-start | bytes 196616 | tf_op jit(solution)/shard_map/ppermute | solution.py:315
  31.5 12.5 %all-to-all-start.1 = ((bf16[8,72,256]{2,1,0:T(8,128)(2,1)}), bf16[8,72,256]{2,1,0:T(8,128)(2,1)S(1)}, u32[]{:S(2)}, u32[]{:S(2)}) async-start(bf16[8,72,256]{2,1,0:T(8,128)(2,1)} %get-tuple-element.23), calls=%async_computation.1 | async-start | bytes 589824 | tf_op jit(solution)/shard_map/all_to_all | solution.py:379
  35.5 11.2 %collective-permute-start.11 = (bf16[8,64,256]{2,1,0:T(8,128)(2,1)S(1)}, bf16[8,64,256]{2,1,0:T(8,128)(2,1)S(1)}, u32[]{:S(2)}, u32[]{:S(2)}) collective-permute-start(bf16[8,64,256]{2,1,0:T(8,128)(2,1)S(1)} %get-tuple-element.37.refs_4_), channel_id=1, source_target_pairs={{4,0},{0,4},{12,8},{8,12},{20,16},{16,20},{28,24},{24,28},{5,1},{1... | collective-permute-start | bytes 786440 | tf_op jit(solution)/shard_map/ppermute | solution.py:311
  44.0 3.2 %collective-permute-start.8 = (f32[8,256]{1,0:T(8,128)S(1)}, f32[8,256]{1,0:T(8,128)S(1)}, u32[]{:S(2)}, u32[]{:S(2)}) collective-permute-start(f32[8,256]{1,0:T(8,128)S(1)} %shard_map.85.refs_0_), channel_id=1, source_target_pairs={{0,3},{1,2},{2,1},{3,0},{4,7},{5,6},{6,5},{7,4},{8,11},{9,10},{10,... | collective-permute-start | bytes 24584 | tf_op jit(solution)/shard_map/ppermute | solution.py:438
  44.0 3.7 %collective-permute-start.9 = (f32[8,256]{1,0:T(8,128)S(1)}, f32[8,256]{1,0:T(8,128)S(1)}, u32[]{:S(2)}, u32[]{:S(2)}) collective-permute-start(f32[8,256]{1,0:T(8,128)S(1)} %shard_map.85.refs_0_), channel_id=1, source_target_pairs={{0,2},{1,3},{2,0},{3,1},{4,6},{5,7},{6,4},{7,5},{8,10},{9,11},{10,... | collective-permute-start | bytes 24584 | tf_op jit(solution)/shard_map/ppermute | solution.py:438
  45.6 2.2 %collective-permute-start.10 = (f32[8,256]{1,0:T(8,128)S(1)}, f32[8,256]{1,0:T(8,128)S(1)}, u32[]{:S(2)}, u32[]{:S(2)}) collective-permute-start(f32[8,256]{1,0:T(8,128)S(1)} %shard_map.85.refs_0_), channel_id=1, source_target_pairs={{0,1},{1,0},{2,3},{3,2},{4,5},{5,4},{6,7},{7,6},{8,9},{9,8},{10,11... | collective-permute-start | bytes 24584 | tf_op jit(solution)/shard_map/ppermute | solution.py:438
